TPU v7x, 256 devices: a whole 4x4x8 slice. The times are simulated.
256 devices in a mesh: row: 64 (over x, z, y_hi), rep: 4 (over y_lo, core).
Axes of the slice: x: 4, y: 4 (y_hi: 2, y_lo: 2; y = y_hi * 2 + y_lo), z: 8, core: 2. Of those that a mesh axis runs over, the one named last changes fastest.
Arguments:
- features: bfloat16 [4, 16384, 128], P('rep', 'row'), may hold values from -6 to 6
- weight: bfloat16 [128, 256], replicated, may hold values from -0.5 to 0.5
- bias_vector: float32 [256], replicated, may hold values from -3 to 3
- edge_tiles: bfloat16 [512, 4, 24, 128, 128], P('row', 'rep'), may hold values from -0.109375 to 0.109375
- tile_columns: int32 [512, 4, 24], P('row', 'rep'), may hold values from 0 to 127, as said below
- live_counts: int32 [512, 4], P('row', 'rep'), may hold values from 1 to 24, as said below
- cotangent: bfloat16 [65536, 256], P(('row', 'rep')), may hold values from -6 to 6
Outputs:
- hidden_out: bfloat16 [65536, 256], P(('row', 'rep'))
- feature_grad: bfloat16 [4, 16384, 128], P('rep', 'row')
- weight_grad: float32 [128, 256], replicated
- bias_grad: float32 [256], replicated
Inputs may be any that keep to these rules, and one draw needn't show every extreme that they name: `tile_columns`: the slots of one block row and section name distinct column tiles. The first live_counts slots of a block row and section are live. On some row indices, row index 0 among them, every block row fills all 24 slots of every section; on the others no count passes 24 // 4.
All inputs are finite; a program needn't handle non-finite values.
Results may differ from a plain program's by a relative error of at most 0.0075.
Values may be sent and summed in bfloat16 or wider, within the bound.
No kernel may reach another device: no remote copies, remote signals or barrier semaphores. Data moves between devices by JAX's collectives and lax.ppermute only.
A program may use at most 128 MiB of HBM per device.

v0:
```python
import functools

import jax
import jax.numpy as jnp
from jax import lax
from jax.experimental import pallas as pl
from jax.experimental.pallas import tpu as pltpu
from jax.sharding import Mesh
from jax.sharding import PartitionSpec as P

NX, NZ, NY = 4, 8, 2
TILE = 128
GROUP = 6
BF = jnp.bfloat16
F32 = jnp.float32
VMEM = pltpu.VMEM
SMEM = pltpu.SMEM


def shift_x(value, k):
    return lax.ppermute(value, "x", [(i, (i + k) % NX) for i in range(NX)])


def shift_z(value, k):
    return lax.ppermute(value, "z", [(i, (i + k) % NZ) for i in range(NZ)])


def swap(value, *axes):
    pairs = [(i, (1 << len(axes)) - 1 - i) for i in range(1 << len(axes))]
    return lax.ppermute(value, axes, pairs)


def add32(*values):
    total = values[0].astype(F32)
    for value in values[1:]:
        total = total + value.astype(F32)
    return total


def add(*values):
    return add32(*values).astype(BF)


def forward_kernel(places, rep_ref, count_ref, pos_ref, edge_ref, *rest):
    pieces = rest[: len(places)]
    outs = rest[len(places):-2]
    table, sems = rest[-2:]
    step = pl.program_id(0)

    @pl.when(step == 0)
    def _():
        copies = []
        for i, (start, size) in enumerate(places):
            copies.append(pltpu.make_async_copy(pieces[i], table.at[pl.ds(start, size)], sems.at[i]))
        for copy in copies:
            copy.start()
        for copy in copies:
            copy.wait()

    count = count_ref[step]
    slots = edge_ref.shape[2]

    def body(g, acc):
        left, right = [], []
        for i in range(GROUP):
            s = g * GROUP + i
            tile = edge_ref[0, 0, s]
            left.append(jnp.where(s < count, tile, jnp.zeros_like(tile)))
            right.append(table[pos_ref[step * slots + s]])
        return acc + jnp.dot(
            jnp.concatenate(left, axis=1), jnp.concatenate(right, axis=0), preferred_element_type=F32
        )

    groups = (count + (GROUP - 1)) // GROUP
    acc = lax.fori_loop(0, groups, body, jnp.zeros((TILE, TILE), F32))
    for q in range(len(outs)):

        @pl.when((step // 2) ^ rep_ref[0] == q)
        def _(q=q):
            outs[q][step % 2] = acc.astype(BF)


def forward(rep, counts, positions, edge_tiles, pieces):
    places = tuple((start, piece.shape[0]) for start, piece in pieces)
    arrays = [piece for _, piece in pieces]
    rows, _, slots = edge_tiles.shape[:3]
    return pl.pallas_call(
        functools.partial(forward_kernel, places),
        grid=(rows,),
        out_shape=(jax.ShapeDtypeStruct((2, TILE, TILE), BF),) * 4,
        in_specs=[pl.BlockSpec(memory_space=SMEM)] * 3
        + [pl.BlockSpec((1, 1, slots, TILE, TILE), lambda t: (t, 0, 0, 0, 0))]
        + [pl.BlockSpec(memory_space=pl.ANY)] * len(arrays),
        out_specs=(pl.BlockSpec((2, TILE, TILE), lambda t: (0, 0, 0)),) * 4,
        scratch_shapes=[VMEM((2 * NX * NZ * NY, TILE, TILE), BF), pltpu.SemaphoreType.DMA((len(arrays),))],
        compiler_params=pltpu.CompilerParams(vmem_limit_bytes=56 * 2**20),
        name="forward",
    )(rep, counts, positions, edge_tiles, *arrays)


def middle_kernel(rep_ref, p0, p1, p2, p3, weight_ref, bias_ref, cot_ref, hidden_ref, slope_ref, near_ref, pair_ref, far_ref):
    agg = add32(*[jnp.concatenate([p[0], p[1]], axis=0) for p in (p0, p1, p2, p3)])
    weight = weight_ref[...]
    preact = (
        jnp.dot(agg, weight.astype(F32), preferred_element_type=F32, precision=lax.Precision.HIGHEST)
        + bias_ref[...]
    )
    gate = jax.nn.sigmoid(preact)
    hidden_ref[...] = (preact * gate).astype(BF)
    outgrad = (cot_ref[...].astype(F32) * gate * (1.0 + preact * (1.0 - gate))).astype(BF)
    slope = lax.dot_general(weight, outgrad, (((1,), (1,)), ((), ())), preferred_element_type=F32).astype(BF)
    for i in range(slope_ref.shape[0]):
        slope_ref[i] = slope[:, i * TILE:(i + 1) * TILE]
    wide = outgrad.astype(F32)
    grad = lax.dot_general(
        agg, wide, (((0,), (0,)), ((), ())), preferred_element_type=F32, precision=lax.Precision.HIGHEST
    )
    bias = jnp.sum(wide, axis=0, keepdims=True)
    places = (near_ref, (pair_ref, 0), far_ref, (pair_ref, 1))
    for q in range(4):
        if q % 2:
            ref = places[q][0].at[places[q][1]]
        else:
            ref = places[q]
        for p in range(4):

            @pl.when(rep_ref[0] ^ q == p)
            def _(ref=ref, p=p):
                ref[0:32, :] = grad[p * 32:(p + 1) * 32, 0:TILE]
                ref[32:64, :] = grad[p * 32:(p + 1) * 32, TILE:]

        ref[64:72, :] = jnp.broadcast_to(bias[:, 0:TILE], (8, TILE))
        ref[72:80, :] = jnp.broadcast_to(bias[:, TILE:], (8, TILE))


def middle(rep, parts, weight, bias, cotangent):
    nodes, width = cotangent.shape
    vmem = pl.BlockSpec(memory_space=VMEM)
    quarter = jax.ShapeDtypeStruct((80, TILE), F32)
    return pl.pallas_call(
        middle_kernel,
        out_shape=(
            jax.ShapeDtypeStruct((nodes, width), BF),
            jax.ShapeDtypeStruct((nodes // TILE, TILE, TILE), BF),
            quarter,
            jax.ShapeDtypeStruct((2, 80, TILE), F32),
            quarter,
        ),
        in_specs=[pl.BlockSpec(memory_space=SMEM)] + [vmem] * 7,
        out_specs=(vmem,) * 5,
        compiler_params=pltpu.CompilerParams(vmem_limit_bytes=32 * 2**20),
        name="middle",
    )(rep, *parts, weight, bias.reshape(1, -1), cotangent)


def backward_kernel(places, count_ref, pos_ref, edge_ref, slope_ref, *rest):
    outs, totals = rest[:-1], rest[-1]
    step = pl.program_id(0)

    @pl.when(step == 0)
    def _():
        def clear(i, carry):
            totals[pl.ds(i * 8, 8)] = jnp.zeros((8, TILE, TILE), F32)
            return carry

        lax.fori_loop(0, totals.shape[0] // 8, clear, 0)

    count = count_ref[step]
    slots = edge_ref.shape[2]
    slope = slope_ref[step]

    def body(g, carry):
        tiles, where = [], []
        for i in range(GROUP):
            s = g * GROUP + i
            tile = edge_ref[0, 0, s]
            tiles.append(jnp.where(s < count, tile, jnp.zeros_like(tile)))
            where.append(pos_ref[step * slots + s])
        terms = jnp.dot(slope, jnp.concatenate(tiles, axis=1), preferred_element_type=F32)
        old = [totals[w] for w in where]
        for i in range(GROUP):
            totals[where[i]] = old[i] + terms[:, i * TILE:(i + 1) * TILE]
        return carry

    lax.fori_loop(0, (count + (GROUP - 1)) // GROUP, body, 0)

    @pl.when(step == pl.num_programs(0) - 1)
    def _():
        for out, (start, size) in zip(outs, places):
            def store(i, carry, out=out, start=start):
                out[i] = totals[start + i].astype(out.dtype)
                return carry

            lax.fori_loop(0, size, store, 0)


def backward(counts, positions, edge_tiles, slope, places):
    rows, _, slots = edge_tiles.shape[:3]
    whole = lambda t: (0, 0, 0)
    return pl.pallas_call(
        functools.partial(backward_kernel, places),
        grid=(rows,),
        out_shape=tuple(jax.ShapeDtypeStruct((size, TILE, TILE), BF) for _, size in places),
        in_specs=[
            pl.BlockSpec(memory_space=SMEM),
            pl.BlockSpec(memory_space=SMEM),
            pl.BlockSpec((1, 1, slots, TILE, TILE), lambda t: (t, 0, 0, 0, 0)),
            pl.BlockSpec(slope.shape, whole),
        ],
        out_specs=tuple(pl.BlockSpec((size, TILE, TILE), whole) for _, size in places),
        scratch_shapes=[VMEM((2 * NX * NZ * NY, TILE, TILE), F32)],
        compiler_params=pltpu.CompilerParams(vmem_limit_bytes=56 * 2**20),
        name="backward",
    )(counts, positions, edge_tiles, slope)


def last_kernel(own_ref, got_ref, quarter_ref, feature_ref, weight_ref, bias_ref):
    for i in range(2):
        total = own_ref[i] + got_ref[i].astype(F32)
        feature_ref[0, i * TILE:(i + 1) * TILE, :] = total.T.astype(BF)
    for q in range(4):
        weight_ref[q * 32:(q + 1) * 32, 0:TILE] = quarter_ref[q, 0:32, :]
        weight_ref[q * 32:(q + 1) * 32, TILE:] = quarter_ref[q, 32:64, :]
    bias_ref[:, 0:TILE] = quarter_ref[0, 64:65, :]
    bias_ref[:, TILE:] = quarter_ref[0, 72:73, :]


def last(own, got, quarters):
    vmem = pl.BlockSpec(memory_space=VMEM)
    return pl.pallas_call(
        last_kernel,
        out_shape=(
            jax.ShapeDtypeStruct((1, 2 * TILE, TILE), BF),
            jax.ShapeDtypeStruct((TILE, 2 * TILE), F32),
            jax.ShapeDtypeStruct((1, 2 * TILE), F32),
        ),
        in_specs=[vmem] * 3,
        out_specs=(vmem, vmem, vmem),
        name="last",
    )(own, got, quarters)


def gather_features(own):
    other = swap(own, "y")
    base = jnp.concatenate([own, other[:1]])
    spread = jnp.broadcast_to(other[None, 1], (NZ, TILE, TILE))
    line = lax.all_to_all(spread, "z", 0, 0, tiled=True)
    plane = jnp.concatenate([base, shift_x(base, 1), shift_x(base, 2), shift_x(base, -1)])
    pieces = [(0, plane), (96, line)]
    for k, hop in ((1, 1), (2, 2), (3, -1)):
        pieces.append((96 + 8 * k, shift_x(line, hop)))
    up = down = plane
    for k in (1, 2, 3):
        up, down = shift_z(up, 1), shift_z(down, -1)
        pieces += [(12 * k, up), (12 * (8 - k), down)]
    pieces += [(48, shift_z(up[:6], 1)), (54, shift_z(down[6:], -1))]
    return pieces


A_PLACES = ((48, 6), (54, 6)) + tuple((12 * k, 12) for k in (3, 5, 2, 6, 1, 7, 0))
B_PLACES = tuple((96 + 8 * k, 8) for k in range(4))


def split(value):
    high = lax.reduce_precision(value, 8, 7)
    return jnp.concatenate([high.astype(BF), (value - high).astype(BF)])


def join(value):
    half = value.shape[0] // 2
    return value[:half].astype(F32) + value[half:].astype(F32)


def scatter_totals(parts, grad):
    rows = [p.reshape(-1, TILE) for p in parts]
    up, down = rows[0], rows[1]
    ups, downs = [None, rows[2], rows[4], rows[6]], [None, rows[3], rows[5], rows[7]]
    b = rows[9:]
    got_b = [shift_x(b[1], 1), shift_x(b[2], 2), shift_x(b[3], -1)]
    half, full = 6 * TILE, 12 * TILE
    wide = split(grad)
    grads = [grad]
    ride_up = ride_down = wide
    for step in range(4):
        up = shift_z(jnp.concatenate([up, ride_up]), 1)
        if step < 3:
            down = shift_z(jnp.concatenate([down, ride_down]), -1)
            size = half if step == 0 else full
            ride_up, ride_down = up[size:], down[size:]
            grads += [join(ride_up), join(ride_down)]
            up, down = up[:size], down[:size]
            if step == 0:
                up = jnp.concatenate([add(up, ups[1][:half]), ups[1][half:]])
                down = jnp.concatenate([downs[1][:half], add(down, downs[1][half:])])
            else:
                up, down = add(up, ups[step + 1]), add(down, downs[step + 1])
        else:
            down = shift_z(down, -1)
            grads.append(join(up[full:]))
            up = up[:full]
    line = add(b[0], *got_b)
    line = lax.all_to_all(line.reshape(NZ, TILE, TILE), "z", 0, 0, tiled=True)
    grad = add32(*grads)
    wide = split(grad)
    part = 3 * TILE
    total = add32(rows[8], up, down)
    sent = [total[k * part:(k + 1) * part].astype(BF) for k in (1, 2, 3)]
    got = [shift_x(jnp.concatenate([v, wide]), hop) for v, hop in zip(sent, (1, 2, -1))]
    total = add32(total[:part], *[g[:part] for g in got])
    grad = add32(grad, *[join(g[part:]) for g in got])
    last_b = add(*[line[k] for k in range(NZ)])
    theirs = swap(jnp.concatenate([total[2 * TILE:].astype(BF), last_b]), "y")
    return total[:2 * TILE].reshape(2, TILE, TILE), theirs.reshape(2, TILE, TILE), grad


def shards(features, weight, bias_vector, edge_tiles, tile_columns, live_counts, cotangent):
    x, z, y = lax.axis_index("x"), lax.axis_index("z"), lax.axis_index("y")
    rep = (lax.axis_index("near") * 2 + lax.axis_index("core")).reshape(1)
    columns = tile_columns.reshape(-1)
    owner, which = columns // 2, columns % 2
    ox, oz, oy = owner // (NZ * NY), (owner // NY) % NZ, owner % NY
    kind = (oy ^ y) * 2 + which

    def places(dx, dz):
        return jnp.where(kind < 3, (dz * NX + dx) * 3 + kind, 96 + dx * NZ + oz).astype(jnp.int32)

    behind = places((x - ox) % NX, (z - oz) % NZ)
    ahead = places((ox - x) % NX, (oz - z) % NZ)
    counts = live_counts.reshape(-1)

    with jax.named_scope("gather"):
        pieces = gather_features(features.reshape(2, TILE, TILE))
    partial = forward(rep, counts, behind, edge_tiles, pieces)
    with jax.named_scope("sections"):
        parts = [
            partial[0],
            swap(partial[1], "core"),
            swap(partial[2], "near"),
            swap(partial[3], "near", "core"),
        ]
    hidden_out, slope, near, pair, far = middle(rep, parts, weight, bias_vector, cotangent)
    with jax.named_scope("slopes"):
        slopes = lax.all_gather(slope, ("near", "core"), axis=0, tiled=True)
    with jax.named_scope("weights"):
        pair = swap(pair, "core")
        near, far = near + pair[0], far + pair[1]
        grad = near + swap(far, "near") + swap(near, "y") + swap(far, "y", "near")
    totals = backward(counts, ahead, edge_tiles, slopes, A_PLACES + B_PLACES)
    with jax.named_scope("scatter"):
        mine, theirs, grad = scatter_totals(totals, grad)
        quarters = lax.all_gather(grad, ("near", "core"), axis=0)
    feature_grad, weight_grad, bias_grad = last(mine, theirs, quarters)
    return hidden_out, feature_grad, weight_grad, bias_grad.reshape(-1)


def solution(mesh):
    grid = Mesh(mesh.devices.reshape(NX, NZ, NY, 2, 2), ("x", "z", "y", "near", "core"))
    row, rep = ("x", "z", "y"), ("near", "core")
    in_specs = (
        P(rep, row, None),
        P(),
        P(),
        P(row, rep, None, None, None),
        P(row, rep, None),
        P(row, rep),
        P(row + rep, None),
    )
    out_specs = (P(row + rep, None), P(rep, row, None), P(), P())
    return jax.shard_map(shards, mesh=grid, in_specs=in_specs, out_specs=out_specs, check_vma=False)
```

profile of v0, /device:TPU:1, one launch (start us, length us, event | category | flops | bytes accessed | tf_op | source)
XLA Modules:
  0.0 184.6 jit_solution(14077445762161302766)
XLA Ops:
  0.6 3.8 %collective-permute-start = (bf16[2,128,128]{2,1,0:T(8,128)(2,1)}, bf16[2,128,128]{2,1,0:T(8,128)(2,1)S(1)}, u32[]{:S(2)}, u32[]{:S(2)}) collective-permute-start(bf16[2,128,128]{2,1,0:T(8,128)(2,1)} %bitcast.58), channel_id=1, source_target_pairs={{0,4},{4,0},{1,5},{5,1},{2,6},{6,2},{3,7},{7,3},{8,12},{12,8},{9,1... | collective-permute-start | bytes 196616 | tf_op jit(solution)/shard_map/gather/ppermute | solution.py:30
  5.3 1.0 collective-permute-done
  7.2 1.3 collective-permute-start.1
  8.5 1.4 collective-permute-start.3
  10.0 1.6 collective-permute-start.2
  12.0 3.7 %collective-permute-done.2 = bf16[3,128,128]{2,1,0:T(8,128)(2,1)S(1)} collective-permute-done((bf16[3,128,128]{2,1,0:T(8,128)(2,1)S(1)}, bf16[3,128,128]{2,1,0:T(8,128)(2,1)S(1)}, u32[]{:S(2)}, u32[]{:S(2)}) %collective-permute-start.2) | collective-permute-done | bytes 98336 | tf_op jit(solution)/shard_map/gather/ppermute | solution.py:21
  15.8 5.7 %collective-permute-start.8 = (bf16[12,128,128]{2,1,0:T(8,128)(2,1)S(1)}, bf16[12,128,128]{2,1,0:T(8,128)(2,1)S(1)}, u32[]{:S(2)}, u32[]{:S(2)}) collective-permute-start(bf16[12,128,128]{2,1,0:T(8,128)(2,1)S(1)} %constant_dynamic-update-slice_fusion.rest_0_), channel_id=1, source_target_pairs={{0,56},{8,0},{16,8},{24,16},{32,24},{40,32},{48,40},{56,48},{1,57}... | collective-permute-start | bytes 1179656 | tf_op jit(solution)/shard_map/gather/ppermute | solution.py:25
  21.4 5.6 %collective-permute-done.8.rest_6_ = bf16[12,128,128]{2,1,0:T(8,128)(2,1)S(1)} collective-permute-done((bf16[12,128,128]{2,1,0:T(8,128)(2,1)S(1)}, bf16[12,128,128]{2,1,0:T(8,128)(2,1)S(1)}, u32[]{:S(2)}, u32[]{:S(2)}) %collective-permute-start.8) | collective-permute-done | bytes 393248 | tf_op jit(solution)/shard_map/gather/ppermute | solution.py:25
  27.1 3.4 %collective-permute-start.10 = (bf16[12,128,128]{2,1,0:T(8,128)(2,1)S(1)}, bf16[12,128,128]{2,1,0:T(8,128)(2,1)S(1)}, u32[]{:S(2)}, u32[]{:S(2)}) collective-permute-start(bf16[12,128,128]{2,1,0:T(8,128)(2,1)S(1)} %collective-permute-done.8.rest_6_), channel_id=1, source_target_pairs={{0,56},{8,0},{16,8},{24,16},{32,24},{40,32},{48,40},{56,48},{1,57}... | collective-permute-start | bytes 1179656 | tf_op jit(solution)/shard_map/gather/ppermute | solution.py:25
  31.3 3.9 %all-to-all-start = ((bf16[8,128,128]{2,1,0:T(8,128)(2,1)}), bf16[8,128,128]{2,1,0:T(8,128)(2,1)S(1)}, u32[]{:S(2)}, u32[]{:S(2)}) async-start(bf16[8,128,128]{2,1,0:T(8,128)(2,1)} %broadcast_in_dim.8), calls=%async_computation | async-start | bytes 524288 | tf_op jit(solution)/shard_map/gather/all_to_all | solution.py:247
  35.2 3.1 %collective-permute-start.12 = (bf16[12,128,128]{2,1,0:T(8,128)(2,1)S(1)}, bf16[12,128,128]{2,1,0:T(8,128)(2,1)S(1)}, u32[]{:S(2)}, u32[]{:S(2)}) collective-permute-start(bf16[12,128,128]{2,1,0:T(8,128)(2,1)S(1)} %collective-permute-done.10.rest_8_), channel_id=1, source_target_pairs={{0,56},{8,0},{16,8},{24,16},{32,24},{40,32},{48,40},{56,48},{1,57}... | collective-permute-start | bytes 1179656 | tf_op jit(solution)/shard_map/gather/ppermute | solution.py:25
  38.9 1.3 reduce.3
  40.3 4.4 %all-to-all-done.rest_1_ = bf16[8,128,128]{2,1,0:T(8,128)(2,1)S(1)} async-done(((bf16[8,128,128]{2,1,0:T(8,128)(2,1)}), bf16[8,128,128]{2,1,0:T(8,128)(2,1)S(1)}, u32[]{:S(2)}, u32[]{:S(2)}) %all-to-all-start) | async-done | bytes 262176 | tf_op jit(solution)/shard_map/gather/all_to_all | solution.py:247
  44.7 1.7 collective-permute-start.6
  48.1 1.1 collective-permute-done.12.rest_10_
  49.3 3.2 %collective-permute-start.14 = (bf16[6,128,128]{2,1,0:T(8,128)(2,1)S(1)}, bf16[6,128,128]{2,1,0:T(8,128)(2,1)S(1)}, u32[]{:S(2)}, u32[]{:S(2)}) collective-permute-start(bf16[6,128,128]{2,1,0:T(8,128)(2,1)S(1)} %slice.278), channel_id=1, source_target_pairs={{0,56},{8,0},{16,8},{24,16},{32,24},{40,32},{48,40},{56,48},{1,57}... | collective-permute-start | bytes 589832 | tf_op jit(solution)/shard_map/gather/ppermute | solution.py:25
  53.4 2.8 %collective-permute-done.4.rest_2_ = bf16[8,128,128]{2,1,0:T(8,128)(2,1)} collective-permute-done((bf16[8,128,128]{2,1,0:T(8,128)(2,1)S(1)}, bf16[8,128,128]{2,1,0:T(8,128)(2,1)}, u32[]{:S(2)}, u32[]{:S(2)}) %collective-permute-start.4) | collective-permute-done | bytes 262176 | tf_op jit(solution)/shard_map/gather/ppermute | solution.py:21
  56.2 1.0 collective-permute-done.14.rest_12_
  57.2 3.8 %collective-permute-done.13.rest_11_ = bf16[6,128,128]{2,1,0:T(8,128)(2,1)S(1)} collective-permute-done((bf16[6,128,128]{2,1,0:T(8,128)(2,1)S(1)}, bf16[6,128,128]{2,1,0:T(8,128)(2,1)S(1)}, u32[]{:S(2)}, u32[]{:S(2)}) %collective-permute-start.13) | collective-permute-done | bytes 196640 | tf_op jit(solution)/shard_map/gather/ppermute | solution.py:25
  61.7 12.3 %forward.1 = (bf16[2,128,128]{2,1,0:T(8,128)(2,1)}, bf16[2,128,128]{2,1,0:T(8,128)(2,1)}, bf16[2,128,128]{2,1,0:T(8,128)(2,1)}, bf16[2,128,128]{2,1,0:T(8,128)(2,1)}) custom-call(s32[1]{0:T(128)} %bitcast.rep_ref, s32[8]{0:T(128)} %bitcast.64, s32[192]{0:T(256)} %add_select_fusion.1.pos_ref, bf16[8,1,24,128,128]{4,3,2,1,0:T(8,128)(2,1)} %edge_ref.3, ...), custom_call_target="tpu_custom_call" | custom-call | tf_op jit(solution)/shard_map/forward/pallas_call | solution.py:87
  74.0 7.8 %collective-permute-start.15 = (bf16[2,128,128]{2,1,0:T(8,128)(2,1)}, bf16[2,128,128]{2,1,0:T(8,128)(2,1)S(1)}, u32[]{:S(2)}, u32[]{:S(2)}) collective-permute-start(bf16[2,128,128]{2,1,0:T(8,128)(2,1)} %get-tuple-element.30), channel_id=1, source_target_pairs={{0,1},{1,0},{2,3},{3,2},{4,5},{5,4},{6,7},{7,6},{8,9},{9,8},{10,11... | collective-permute-start | bytes 196616 | tf_op jit(solution)/shard_map/sections/ppermute | solution.py:30
  81.8 1.3 collective-permute-start.16
  83.5 2.1 %collective-permute-done.16.p2 = bf16[2,128,128]{2,1,0:T(8,128)(2,1)S(1)} collective-permute-done((bf16[2,128,128]{2,1,0:T(8,128)(2,1)}, bf16[2,128,128]{2,1,0:T(8,128)(2,1)S(1)}, u32[]{:S(2)}, u32[]{:S(2)}) %collective-permute-start.16) | collective-permute-done | bytes 65568 | tf_op jit(solution)/shard_map/sections/ppermute | solution.py:30
  85.6 1.7 collective-permute-done.17.p3
  88.2 1.6 middle.1
  90.2 6.3 %all_gather.9.slope_ref = bf16[8,128,128]{2,1,0:T(8,128)(2,1)} all-gather(bf16[2,128,128]{2,1,0:T(8,128)(2,1)S(1)} %get-tuple-element.34), channel_id=1, replica_groups=mesh['x'=4,'z'=8,'y'=2,'near'=2,'core'=2] {'near','core'}, dimensions={0}, use_global_device_ids=true | all-gather | bytes 327680 | tf_op jit(solution)/shard_map/slopes/all_gather | solution.py:343
  96.5 12.9 %backward.1 = (bf16[6,128,128]{2,1,0:T(8,128)(2,1)}, bf16[6,128,128]{2,1,0:T(8,128)(2,1)}, bf16[12,128,128]{2,1,0:T(8,128)(2,1)}, bf16[12,128,128]{2,1,0:T(8,128...) custom-call(s32[8]{0:T(128)} %bitcast.65, ...), custom_call_target="tpu_custom_call" | custom-call | tf_op jit(solution)/shard_map/backward/pallas_call | solution.py:200
  109.6 5.0 %collective-permute-start.21 = (f32[80,128]{1,0:T(8,128)S(1)}, f32[80,128]{1,0:T(8,128)S(1)}, u32[]{:S(2)}, u32[]{:S(2)}) collective-permute-start(f32[80,128]{1,0:T(8,128)S(1)} %get-tuple-element.72), channel_id=1, source_target_pairs={{0,6},{2,4},{4,2},{6,0},{1,7},{3,5},{5,3},{7,1},{8,14},{10,12},{12... | collective-permute-start | bytes 122888 | tf_op jit(solution)/shard_map/weights/ppermute | solution.py:30
  114.7 1.2 collective-permute-start.20
  115.9 1.0 fusion.32
  116.9 2.4 %collective-permute-done.20 = f32[80,128]{1,0:T(8,128)S(1)} collective-permute-done((f32[80,128]{1,0:T(8,128)S(1)}, f32[80,128]{1,0:T(8,128)S(1)}, u32[]{:S(2)}, u32[]{:S(2)}) %collective-permute-start.20) | collective-permute-done | bytes 40992 | tf_op jit(solution)/shard_map/weights/ppermute | solution.py:30
  119.5 1.1 pad_maximum_fusion.6
  120.6 1.0 fusion.33
  121.7 2.7 %collective-permute-start.26 = (bf16[928,128]{1,0:T(8,128)(2,1)S(1)}, bf16[928,128]{1,0:T(8,128)(2,1)S(1)}, u32[]{:S(2)}, u32[]{:S(2)}) collective-permute-start(bf16[928,128]{1,0:T(8,128)(2,1)S(1)} %get-tuple-element.80), channel_id=1, source_target_pairs={{0,56},{8,0},{16,8},{24,16},{32,24},{40,32},{48,40},{56,48},{1,57}... | collective-permute-start | bytes 712712 | tf_op jit(solution)/shard_map/scatter/ppermute | solution.py:25
  124.4 2.4 %collective-permute-done.22 = bf16[928,128]{1,0:T(8,128)(2,1)S(1)} collective-permute-done((bf16[928,128]{1,0:T(8,128)(2,1)S(1)}, bf16[928,128]{1,0:T(8,128)(2,1)S(1)}, u32[]{:S(2)}, u32[]{:S(2)}) %collective-permute-start.22) | collective-permute-done | bytes 237600 | tf_op jit(solution)/shard_map/scatter/ppermute | solution.py:25
  128.2 3.2 %collective-permute-start.27 = (bf16[1696,128]{1,0:T(8,128)(2,1)S(1)}, bf16[1696,128]{1,0:T(8,128)(2,1)S(1)}, u32[]{:S(2)}, u32[]{:S(2)}) collective-permute-start(bf16[1696,128]{1,0:T(8,128)(2,1)S(1)} %pad_maximum_fusion.3), channel_id=1, source_target_pairs={{0,56},{8,0},{16,8},{24,16},{32,24},{40,32},{48,40},{56,48},{1,57}... | collective-permute-start | bytes 1302536 | tf_op jit(solution)/shard_map/scatter/ppermute | solution.py:25
  131.4 5.1 %collective-permute-done.23 = bf16[1696,128]{1,0:T(8,128)(2,1)S(1)} collective-permute-done((bf16[1696,128]{1,0:T(8,128)(2,1)S(1)}, bf16[1696,128]{1,0:T(8,128)(2,1)S(1)}, u32[]{:S(2)}, u32[]{:S(2)}) %collective-permute-start.23) | collective-permute-done | bytes 434208 | tf_op jit(solution)/shard_map/scatter/ppermute | solution.py:25
  137.3 3.7 %collective-permute-start.28 = (bf16[1696,128]{1,0:T(8,128)(2,1)S(1)}, bf16[1696,128]{1,0:T(8,128)(2,1)S(1)}, u32[]{:S(2)}, u32[]{:S(2)}) collective-permute-start(bf16[1696,128]{1,0:T(8,128)(2,1)S(1)} %pad_maximum_fusion.4), channel_id=1, source_target_pairs={{0,56},{8,0},{16,8},{24,16},{32,24},{40,32},{48,40},{56,48},{1,57}... | collective-permute-start | bytes 1302536 | tf_op jit(solution)/shard_map/scatter/ppermute | solution.py:25
  141.0 3.9 %collective-permute-done.24 = bf16[1696,128]{1,0:T(8,128)(2,1)S(1)} collective-permute-done((bf16[1696,128]{1,0:T(8,128)(2,1)S(1)}, bf16[1696,128]{1,0:T(8,128)(2,1)S(1)}, u32[]{:S(2)}, u32[]{:S(2)}) %collective-permute-start.24) | collective-permute-done | bytes 434208 | tf_op jit(solution)/shard_map/scatter/ppermute | solution.py:25
  147.1 3.1 %collective-permute-start.29 = (bf16[1536,128]{1,0:T(8,128)(2,1)}, bf16[1536,128]{1,0:T(8,128)(2,1)}, u32[]{:S(2)}, u32[]{:S(2)}) collective-permute-start(bf16[1536,128]{1,0:T(8,128)(2,1)} %fusion), channel_id=1, source_target_pairs={{0,56},{8,0},{16,8},{24,16},{32,24},{40,32},{48,40},{56,48},{1,57}... | collective-permute-start | bytes 1179656 | tf_op jit(solution)/shard_map/scatter/ppermute | solution.py:25
  151.1 3.4 %all-to-all-start.1 = ((bf16[8,128,128]{2,1,0:T(8,128)(2,1)}), bf16[8,128,128]{2,1,0:T(8,128)(2,1)S(1)}, u32[]{:S(2)}, u32[]{:S(2)}) async-start(bf16[8,128,128]{2,1,0:T(8,128)(2,1)} %bitcast.23), calls=%async_computation.1 | async-start | bytes 524288 | tf_op jit(solution)/shard_map/scatter/all_to_all | solution.py:302
  155.4 1.2 fusion.28
  156.7 1.5 collective-permute-start.30
  158.3 2.3 %collective-permute-start.32 = (bf16[544,128]{1,0:T(8,128)(2,1)S(1)}, bf16[544,128]{1,0:T(8,128)(2,1)S(1)}, u32[]{:S(2)}, u32[]{:S(2)}) collective-permute-start(bf16[544,128]{1,0:T(8,128)(2,1)S(1)} %get-tuple-element.78), channel_id=1, source_target_pairs={{0,192},{64,0},{128,64},{192,128},{1,193},{65,1},{129,65},{193,129... | collective-permute-start | bytes 417800 | tf_op jit(solution)/shard_map/scatter/ppermute | solution.py:21
  160.6 3.1 %all-to-all-done.1 = bf16[8,128,128]{2,1,0:T(8,128)(2,1)S(1)} async-done(((bf16[8,128,128]{2,1,0:T(8,128)(2,1)}), bf16[8,128,128]{2,1,0:T(8,128)(2,1)S(1)}, u32[]{:S(2)}, u32[]{:S(2)}) %all-to-all-start.1) | async-done | bytes 262176 | tf_op jit(solution)/shard_map/scatter/all_to_all | solution.py:302
  164.2 1.5 collective-permute-start.36
  166.4 15.8 %all-gather = f32[320,128]{1,0:T(8,128)} all-gather(f32[80,128]{1,0:T(8,128)S(1)} %add_add_fusion), channel_id=2, replica_groups=mesh['x'=4,'z'=8,'y'=2,'near'=2,'core'=2] {'near','core'}, dimensions={0}, use_global_device_ids=true | all-gather | bytes 204800 | tf_op jit(solution)/shard_map/scatter/all_gather | solution.py:351
  182.8 1.8 last.1
  (130 shorter events, 17.1 us)
Async XLA Ops:
  0.6 5.7 %collective-permute-start = (bf16[2,128,128]{2,1,0:T(8,128)(2,1)}, bf16[2,128,128]{2,1,0:T(8,128)(2,1)S(1)}, u32[]{:S(2)}, u32[]{:S(2)}) collective-permute-start(bf16[2,128,128]{2,1,0:T(8,128)(2,1)} %bitcast.58), channel_id=1, source_target_pairs={{0,4},{4,0},{1,5},{5,1},{2,6},{6,2},{3,7},{7,3},{8,12},{12,8},{9,1... | collective-permute-start | bytes 196616 | tf_op jit(solution)/shard_map/gather/ppermute | solution.py:30
  7.2 4.8 %collective-permute-start.1 = (bf16[3,128,128]{2,1,0:T(8,128)(2,1)S(1)}, bf16[3,128,128]{2,1,0:T(8,128)(2,1)S(1)}, u32[]{:S(2)}, u32[]{:S(2)}) collective-permute-start(bf16[3,128,128]{2,1,0:T(8,128)(2,1)S(1)} %pad_maximum_fusion.15), channel_id=1, source_target_pairs={{0,64},{64,128},{128,192},{192,0},{1,65},{65,129},{129,193},{193,1... | collective-permute-start | bytes 294920 | tf_op jit(solution)/shard_map/gather/ppermute | solution.py:21
  8.5 7.2 %collective-permute-start.3 = (bf16[3,128,128]{2,1,0:T(8,128)(2,1)S(1)}, bf16[3,128,128]{2,1,0:T(8,128)(2,1)S(1)}, u32[]{:S(2)}, u32[]{:S(2)}) collective-permute-start(bf16[3,128,128]{2,1,0:T(8,128)(2,1)S(1)} %pad_maximum_fusion.15), channel_id=1, source_target_pairs={{0,192},{64,0},{128,64},{192,128},{1,193},{65,1},{129,65},{193,129... | collective-permute-start | bytes 294920 | tf_op jit(solution)/shard_map/gather/ppermute | solution.py:21
  10.0 5.8 %collective-permute-start.2 = (bf16[3,128,128]{2,1,0:T(8,128)(2,1)S(1)}, bf16[3,128,128]{2,1,0:T(8,128)(2,1)S(1)}, u32[]{:S(2)}, u32[]{:S(2)}) collective-permute-start(bf16[3,128,128]{2,1,0:T(8,128)(2,1)S(1)} %pad_maximum_fusion.15), channel_id=1, source_target_pairs={{0,128},{64,192},{128,0},{192,64},{1,129},{65,193},{129,1},{193,65... | collective-permute-start | bytes 294920 | tf_op jit(solution)/shard_map/gather/ppermute | solution.py:21
  12.0 75.4 %copy-start = (bf16[256,256]{1,0:T(8,128)(2,1)S(1)}, bf16[256,256]{1,0:T(8,128)(2,1)}, u32[]{:S(2)}) copy-start(bf16[256,256]{1,0:T(8,128)(2,1)} %cot_ref.1) | copy-start | bytes 393220
  12.0 75.4 %copy-start.1 = (bf16[128,256]{1,0:T(8,128)(2,1)S(1)}, bf16[128,256]{1,0:T(8,128)(2,1)}, u32[]{:S(2)}) copy-start(bf16[128,256]{1,0:T(8,128)(2,1)} %weight_ref.1) | copy-start | bytes 196612
  12.0 75.4 %copy-start.3 = (f32[256]{0:T(256)S(1)}, f32[256]{0:T(256)}, u32[]{:S(2)}) copy-start(f32[256]{0:T(256)} %param.9) | copy-start | bytes 3076
  15.8 45.2 %copy-start.7 = (bf16[12,128,128]{2,1,0:T(8,128)(2,1)}, bf16[12,128,128]{2,1,0:T(8,128)(2,1)S(1)}, u32[]{:S(2)}) copy-start(bf16[12,128,128]{2,1,0:T(8,128)(2,1)S(1)} %constant_dynamic-update-slice_fusion.rest_0_) | copy-start | bytes 1179652
  15.8 11.3 %collective-permute-start.8 = (bf16[12,128,128]{2,1,0:T(8,128)(2,1)S(1)}, bf16[12,128,128]{2,1,0:T(8,128)(2,1)S(1)}, u32[]{:S(2)}, u32[]{:S(2)}) collective-permute-start(bf16[12,128,128]{2,1,0:T(8,128)(2,1)S(1)} %constant_dynamic-update-slice_fusion.rest_0_), channel_id=1, source_target_pairs={{0,56},{8,0},{16,8},{24,16},{32,24},{40,32},{48,40},{56,48},{1,57}... | collective-permute-start | bytes 1179656 | tf_op jit(solution)/shard_map/gather/ppermute | solution.py:25
  21.4 9.0 %collective-permute-start.7 = (bf16[12,128,128]{2,1,0:T(8,128)(2,1)S(1)}, bf16[12,128,128]{2,1,0:T(8,128)(2,1)S(1)}, u32[]{:S(2)}, u32[]{:S(2)}) collective-permute-start(bf16[12,128,128]{2,1,0:T(8,128)(2,1)S(1)} %constant_dynamic-update-slice_fusion.rest_0_), channel_id=1, source_target_pairs={{0,8},{8,16},{16,24},{24,32},{32,40},{40,48},{48,56},{56,0},{1,9},... | collective-permute-start | bytes 1179656 | tf_op jit(solution)/shard_map/gather/ppermute | solution.py:25
  27.1 33.9 %copy-start.8 = (bf16[12,128,128]{2,1,0:T(8,128)(2,1)}, bf16[12,128,128]{2,1,0:T(8,128)(2,1)S(1)}, u32[]{:S(2)}) copy-start(bf16[12,128,128]{2,1,0:T(8,128)(2,1)S(1)} %collective-permute-done.8.rest_6_) | copy-start | bytes 1179652
  27.1 8.1 %collective-permute-start.10 = (bf16[12,128,128]{2,1,0:T(8,128)(2,1)S(1)}, bf16[12,128,128]{2,1,0:T(8,128)(2,1)S(1)}, u32[]{:S(2)}, u32[]{:S(2)}) collective-permute-start(bf16[12,128,128]{2,1,0:T(8,128)(2,1)S(1)} %collective-permute-done.8.rest_6_), channel_id=1, source_target_pairs={{0,56},{8,0},{16,8},{24,16},{32,24},{40,32},{48,40},{56,48},{1,57}... | collective-permute-start | bytes 1179656 | tf_op jit(solution)/shard_map/gather/ppermute | solution.py:25
  30.5 30.5 %copy-start.9 = (bf16[12,128,128]{2,1,0:T(8,128)(2,1)}, bf16[12,128,128]{2,1,0:T(8,128)(2,1)S(1)}, u32[]{:S(2)}) copy-start(bf16[12,128,128]{2,1,0:T(8,128)(2,1)S(1)} %collective-permute-done.7.rest_5_) | copy-start | bytes 1179652
  30.5 7.8 %collective-permute-start.9 = (bf16[12,128,128]{2,1,0:T(8,128)(2,1)S(1)}, bf16[12,128,128]{2,1,0:T(8,128)(2,1)S(1)}, u32[]{:S(2)}, u32[]{:S(2)}) collective-permute-start(bf16[12,128,128]{2,1,0:T(8,128)(2,1)S(1)} %collective-permute-done.7.rest_5_), channel_id=1, source_target_pairs={{0,8},{8,16},{16,24},{24,32},{32,40},{40,48},{48,56},{56,0},{1,9},... | collective-permute-start | bytes 1179656 | tf_op jit(solution)/shard_map/gather/ppermute | solution.py:25
  31.3 13.4 %all-to-all-start = ((bf16[8,128,128]{2,1,0:T(8,128)(2,1)}), bf16[8,128,128]{2,1,0:T(8,128)(2,1)S(1)}, u32[]{:S(2)}, u32[]{:S(2)}) async-start(bf16[8,128,128]{2,1,0:T(8,128)(2,1)} %broadcast_in_dim.8), calls=%async_computation | async-start | bytes 524288 | tf_op jit(solution)/shard_map/gather/all_to_all | solution.py:247
  35.2 14.0 %collective-permute-start.12 = (bf16[12,128,128]{2,1,0:T(8,128)(2,1)S(1)}, bf16[12,128,128]{2,1,0:T(8,128)(2,1)S(1)}, u32[]{:S(2)}, u32[]{:S(2)}) collective-permute-start(bf16[12,128,128]{2,1,0:T(8,128)(2,1)S(1)} %collective-permute-done.10.rest_8_), channel_id=1, source_target_pairs={{0,56},{8,0},{16,8},{24,16},{32,24},{40,32},{48,40},{56,48},{1,57}... | collective-permute-start | bytes 1179656 | tf_op jit(solution)/shard_map/gather/ppermute | solution.py:25
  38.3 14.3 %collective-permute-start.11 = (bf16[12,128,128]{2,1,0:T(8,128)(2,1)S(1)}, bf16[12,128,128]{2,1,0:T(8,128)(2,1)S(1)}, u32[]{:S(2)}, u32[]{:S(2)}) collective-permute-start(bf16[12,128,128]{2,1,0:T(8,128)(2,1)S(1)} %collective-permute-done.9.rest_7_), channel_id=1, source_target_pairs={{0,8},{8,16},{16,24},{24,32},{32,40},{40,48},{48,56},{56,0},{1,9},... | collective-permute-start | bytes 1179656 | tf_op jit(solution)/shard_map/gather/ppermute | solution.py:25
  44.7 8.6 %collective-permute-start.6 = (bf16[8,128,128]{2,1,0:T(8,128)(2,1)S(1)}, bf16[8,128,128]{2,1,0:T(8,128)(2,1)S(1)}, u32[]{:S(2)}, u32[]{:S(2)}) collective-permute-start(bf16[8,128,128]{2,1,0:T(8,128)(2,1)S(1)} %all-to-all-done.rest_1_), channel_id=1, source_target_pairs={{0,192},{64,0},{128,64},{192,128},{1,193},{65,1},{129,65},{193,129... | collective-permute-start | bytes 786440 | tf_op jit(solution)/shard_map/gather/ppermute | solution.py:21
  46.4 6.9 %collective-permute-start.5 = (bf16[8,128,128]{2,1,0:T(8,128)(2,1)S(1)}, bf16[8,128,128]{2,1,0:T(8,128)(2,1)}, u32[]{:S(2)}, u32[]{:S(2)}) collective-permute-start(bf16[8,128,128]{2,1,0:T(8,128)(2,1)S(1)} %all-to-all-done.rest_1_), channel_id=1, source_target_pairs={{0,128},{64,192},{128,0},{192,64},{1,129},{65,193},{129,1},{193,65... | collective-permute-start | bytes 786440 | tf_op jit(solution)/shard_map/gather/ppermute | solution.py:21
  46.7 9.5 %collective-permute-start.4 = (bf16[8,128,128]{2,1,0:T(8,128)(2,1)S(1)}, bf16[8,128,128]{2,1,0:T(8,128)(2,1)}, u32[]{:S(2)}, u32[]{:S(2)}) collective-permute-start(bf16[8,128,128]{2,1,0:T(8,128)(2,1)S(1)} %all-to-all-done.rest_1_), channel_id=1, source_target_pairs={{0,64},{64,128},{128,192},{192,0},{1,65},{65,129},{129,193},{193,1... | collective-permute-start | bytes 786440 | tf_op jit(solution)/shard_map/gather/ppermute | solution.py:21
  49.3 7.9 %collective-permute-start.14 = (bf16[6,128,128]{2,1,0:T(8,128)(2,1)S(1)}, bf16[6,128,128]{2,1,0:T(8,128)(2,1)S(1)}, u32[]{:S(2)}, u32[]{:S(2)}) collective-permute-start(bf16[6,128,128]{2,1,0:T(8,128)(2,1)S(1)} %slice.278), channel_id=1, source_target_pairs={{0,56},{8,0},{16,8},{24,16},{32,24},{40,32},{48,40},{56,48},{1,57}... | collective-permute-start | bytes 589832 | tf_op jit(solution)/shard_map/gather/ppermute | solution.py:25
  52.6 8.4 %collective-permute-start.13 = (bf16[6,128,128]{2,1,0:T(8,128)(2,1)S(1)}, bf16[6,128,128]{2,1,0:T(8,128)(2,1)S(1)}, u32[]{:S(2)}, u32[]{:S(2)}) collective-permute-start(bf16[6,128,128]{2,1,0:T(8,128)(2,1)S(1)} %slice.277), channel_id=1, source_target_pairs={{0,8},{8,16},{16,24},{24,32},{32,40},{40,48},{48,56},{56,0},{1,9},... | collective-permute-start | bytes 589832 | tf_op jit(solution)/shard_map/gather/ppermute | solution.py:25
  74.0 9.5 %collective-permute-start.15 = (bf16[2,128,128]{2,1,0:T(8,128)(2,1)}, bf16[2,128,128]{2,1,0:T(8,128)(2,1)S(1)}, u32[]{:S(2)}, u32[]{:S(2)}) collective-permute-start(bf16[2,128,128]{2,1,0:T(8,128)(2,1)} %get-tuple-element.30), channel_id=1, source_target_pairs={{0,1},{1,0},{2,3},{3,2},{4,5},{5,4},{6,7},{7,6},{8,9},{9,8},{10,11... | collective-permute-start | bytes 196616 | tf_op jit(solution)/shard_map/sections/ppermute | solution.py:30
  81.8 3.9 %collective-permute-start.16 = (bf16[2,128,128]{2,1,0:T(8,128)(2,1)}, bf16[2,128,128]{2,1,0:T(8,128)(2,1)S(1)}, u32[]{:S(2)}, u32[]{:S(2)}) collective-permute-start(bf16[2,128,128]{2,1,0:T(8,128)(2,1)} %get-tuple-element.31), channel_id=1, source_target_pairs={{0,2},{2,0},{1,3},{3,1},{4,6},{6,4},{5,7},{7,5},{8,10},{10,8},{9,1... | collective-permute-start | bytes 196616 | tf_op jit(solution)/shard_map/sections/ppermute | solution.py:30
  83.1 4.3 %collective-permute-start.17 = (bf16[2,128,128]{2,1,0:T(8,128)(2,1)}, bf16[2,128,128]{2,1,0:T(8,128)(2,1)S(1)}, u32[]{:S(2)}, u32[]{:S(2)}) collective-permute-start(bf16[2,128,128]{2,1,0:T(8,128)(2,1)} %get-tuple-element.32), channel_id=1, source_target_pairs={{0,3},{1,2},{2,1},{3,0},{4,7},{5,6},{6,5},{7,4},{8,11},{9,10},{10,... | collective-permute-start | bytes 196616 | tf_op jit(solution)/shard_map/sections/ppermute | solution.py:30
  89.9 19.8 %collective-permute-start.18 = (f32[2,80,128]{2,1,0:T(8,128)S(1)}, f32[2,80,128]{2,1,0:T(8,128)S(1)}, u32[]{:S(2)}, u32[]{:S(2)}) collective-permute-start(f32[2,80,128]{2,1,0:T(8,128)S(1)} %get-tuple-element.38), channel_id=1, source_target_pairs={{0,1},{1,0},{2,3},{3,2},{4,5},{5,4},{6,7},{7,6},{8,9},{9,8},{10,11... | collective-permute-start | bytes 245768 | tf_op jit(solution)/shard_map/weights/ppermute | solution.py:30
  109.4 35.6 %copy-start.14 = (bf16[12,128,128]{2,1,0:T(8,128)(2,1)S(1)}, bf16[12,128,128]{2,1,0:T(8,128)(2,1)}, u32[]{:S(2)}) copy-start(bf16[12,128,128]{2,1,0:T(8,128)(2,1)} %get-tuple-element.42) | copy-start | bytes 1179652
  109.4 36.8 %copy-start.13 = (bf16[12,128,128]{2,1,0:T(8,128)(2,1)S(1)}, bf16[12,128,128]{2,1,0:T(8,128)(2,1)}, u32[]{:S(2)}) copy-start(bf16[12,128,128]{2,1,0:T(8,128)(2,1)} %get-tuple-element.46) | copy-start | bytes 1179652
  109.4 40.8 %collective-permute-start.33 = (bf16[1024,128]{1,0:T(8,128)(2,1)}, bf16[1024,128]{1,0:T(8,128)(2,1)S(1)}, u32[]{:S(2)}, u32[]{:S(2)}) collective-permute-start(bf16[1024,128]{1,0:T(8,128)(2,1)} %bitcast.68), channel_id=1, source_target_pairs={{0,64},{64,128},{128,192},{192,0},{1,65},{65,129},{129,193},{193,1... | collective-permute-start | bytes 786440 | tf_op jit(solution)/shard_map/scatter/ppermute | solution.py:21
  109.5 40.7 %collective-permute-start.34 = (bf16[1024,128]{1,0:T(8,128)(2,1)}, bf16[1024,128]{1,0:T(8,128)(2,1)S(1)}, u32[]{:S(2)}, u32[]{:S(2)}) collective-permute-start(bf16[1024,128]{1,0:T(8,128)(2,1)} %bitcast.67), channel_id=1, source_target_pairs={{0,128},{64,192},{128,0},{192,64},{1,129},{65,193},{129,1},{193,65... | collective-permute-start | bytes 786440 | tf_op jit(solution)/shard_map/scatter/ppermute | solution.py:21
  109.6 9.8 %collective-permute-start.21 = (f32[80,128]{1,0:T(8,128)S(1)}, f32[80,128]{1,0:T(8,128)S(1)}, u32[]{:S(2)}, u32[]{:S(2)}) collective-permute-start(f32[80,128]{1,0:T(8,128)S(1)} %get-tuple-element.72), channel_id=1, source_target_pairs={{0,6},{2,4},{4,2},{6,0},{1,7},{3,5},{5,3},{7,1},{8,14},{10,12},{12... | collective-permute-start | bytes 122888 | tf_op jit(solution)/shard_map/weights/ppermute | solution.py:30
  114.6 4.9 %collective-permute-start.19 = (f32[80,128]{1,0:T(8,128)S(1)}, f32[80,128]{1,0:T(8,128)S(1)}, u32[]{:S(2)}, u32[]{:S(2)}) collective-permute-start(f32[80,128]{1,0:T(8,128)S(1)} %get-tuple-element.72), channel_id=1, source_target_pairs={{0,2},{2,0},{1,3},{3,1},{4,6},{6,4},{5,7},{7,5},{8,10},{10,8},{9,1... | collective-permute-start | bytes 122888 | tf_op jit(solution)/shard_map/weights/ppermute | solution.py:30
  114.7 4.7 %collective-permute-start.20 = (f32[80,128]{1,0:T(8,128)S(1)}, f32[80,128]{1,0:T(8,128)S(1)}, u32[]{:S(2)}, u32[]{:S(2)}) collective-permute-start(f32[80,128]{1,0:T(8,128)S(1)} %get-tuple-element.71), channel_id=1, source_target_pairs={{0,4},{4,0},{1,5},{5,1},{2,6},{6,2},{3,7},{7,3},{8,12},{12,8},{9,1... | collective-permute-start | bytes 122888 | tf_op jit(solution)/shard_map/weights/ppermute | solution.py:30
  119.4 30.9 %copy-start.18 = (bf16[8,128,128]{2,1,0:T(8,128)(2,1)S(1)}, bf16[8,128,128]{2,1,0:T(8,128)(2,1)}, u32[]{:S(2)}) copy-start(bf16[8,128,128]{2,1,0:T(8,128)(2,1)} %get-tuple-element.47) | copy-start | bytes 786436
  119.4 30.9 %collective-permute-start.35 = (bf16[1024,128]{1,0:T(8,128)(2,1)}, bf16[1024,128]{1,0:T(8,128)(2,1)S(1)}, u32[]{:S(2)}, u32[]{:S(2)}) collective-permute-start(bf16[1024,128]{1,0:T(8,128)(2,1)} %bitcast.66), channel_id=1, source_target_pairs={{0,192},{64,0},{128,64},{192,128},{1,193},{65,1},{129,65},{193,129... | collective-permute-start | bytes 786440 | tf_op jit(solution)/shard_map/scatter/ppermute | solution.py:21
  120.5 6.2 %collective-permute-start.22 = (bf16[928,128]{1,0:T(8,128)(2,1)S(1)}, bf16[928,128]{1,0:T(8,128)(2,1)S(1)}, u32[]{:S(2)}, u32[]{:S(2)}) collective-permute-start(bf16[928,128]{1,0:T(8,128)(2,1)S(1)} %get-tuple-element.79), channel_id=1, source_target_pairs={{0,8},{8,16},{16,24},{24,32},{32,40},{40,48},{48,56},{56,0},{1,9},... | collective-permute-start | bytes 712712 | tf_op jit(solution)/shard_map/scatter/ppermute | solution.py:25
  121.7 5.8 %collective-permute-start.26 = (bf16[928,128]{1,0:T(8,128)(2,1)S(1)}, bf16[928,128]{1,0:T(8,128)(2,1)S(1)}, u32[]{:S(2)}, u32[]{:S(2)}) collective-permute-start(bf16[928,128]{1,0:T(8,128)(2,1)S(1)} %get-tuple-element.80), channel_id=1, source_target_pairs={{0,56},{8,0},{16,8},{24,16},{32,24},{40,32},{48,40},{56,48},{1,57}... | collective-permute-start | bytes 712712 | tf_op jit(solution)/shard_map/scatter/ppermute | solution.py:25
  126.9 9.5 %collective-permute-start.23 = (bf16[1696,128]{1,0:T(8,128)(2,1)S(1)}, bf16[1696,128]{1,0:T(8,128)(2,1)S(1)}, u32[]{:S(2)}, u32[]{:S(2)}) collective-permute-start(bf16[1696,128]{1,0:T(8,128)(2,1)S(1)} %pad_maximum_fusion), channel_id=1, source_target_pairs={{0,8},{8,16},{16,24},{24,32},{32,40},{40,48},{48,56},{56,0},{1,9},... | collective-permute-start | bytes 1302536 | tf_op jit(solution)/shard_map/scatter/ppermute | solution.py:25
  128.2 8.9 %collective-permute-start.27 = (bf16[1696,128]{1,0:T(8,128)(2,1)S(1)}, bf16[1696,128]{1,0:T(8,128)(2,1)S(1)}, u32[]{:S(2)}, u32[]{:S(2)}) collective-permute-start(bf16[1696,128]{1,0:T(8,128)(2,1)S(1)} %pad_maximum_fusion.3), channel_id=1, source_target_pairs={{0,56},{8,0},{16,8},{24,16},{32,24},{40,32},{48,40},{56,48},{1,57}... | collective-permute-start | bytes 1302536 | tf_op jit(solution)/shard_map/scatter/ppermute | solution.py:25
  136.6 8.4 %collective-permute-start.24 = (bf16[1696,128]{1,0:T(8,128)(2,1)S(1)}, bf16[1696,128]{1,0:T(8,128)(2,1)S(1)}, u32[]{:S(2)}, u32[]{:S(2)}) collective-permute-start(bf16[1696,128]{1,0:T(8,128)(2,1)S(1)} %pad_maximum_fusion.1), channel_id=1, source_target_pairs={{0,8},{8,16},{16,24},{24,32},{32,40},{40,48},{48,56},{56,0},{1,9},... | collective-permute-start | bytes 1302536 | tf_op jit(solution)/shard_map/scatter/ppermute | solution.py:25
  137.3 8.9 %collective-permute-start.28 = (bf16[1696,128]{1,0:T(8,128)(2,1)S(1)}, bf16[1696,128]{1,0:T(8,128)(2,1)S(1)}, u32[]{:S(2)}, u32[]{:S(2)}) collective-permute-start(bf16[1696,128]{1,0:T(8,128)(2,1)S(1)} %pad_maximum_fusion.4), channel_id=1, source_target_pairs={{0,56},{8,0},{16,8},{24,16},{32,24},{40,32},{48,40},{56,48},{1,57}... | collective-permute-start | bytes 1302536 | tf_op jit(solution)/shard_map/scatter/ppermute | solution.py:25
  145.2 9.4 %collective-permute-start.25 = (bf16[1696,128]{1,0:T(8,128)(2,1)S(1)}, bf16[1696,128]{1,0:T(8,128)(2,1)S(1)}, u32[]{:S(2)}, u32[]{:S(2)}) collective-permute-start(bf16[1696,128]{1,0:T(8,128)(2,1)S(1)} %pad_maximum_fusion.2), channel_id=1, source_target_pairs={{0,8},{8,16},{16,24},{24,32},{32,40},{40,48},{48,56},{56,0},{1,9},... | collective-permute-start | bytes 1302536 | tf_op jit(solution)/shard_map/scatter/ppermute | solution.py:25
  147.1 8.3 %collective-permute-start.29 = (bf16[1536,128]{1,0:T(8,128)(2,1)}, bf16[1536,128]{1,0:T(8,128)(2,1)}, u32[]{:S(2)}, u32[]{:S(2)}) collective-permute-start(bf16[1536,128]{1,0:T(8,128)(2,1)} %fusion), channel_id=1, source_target_pairs={{0,56},{8,0},{16,8},{24,16},{32,24},{40,32},{48,40},{56,48},{1,57}... | collective-permute-start | bytes 1179656 | tf_op jit(solution)/shard_map/scatter/ppermute | solution.py:25
  151.1 12.7 %all-to-all-start.1 = ((bf16[8,128,128]{2,1,0:T(8,128)(2,1)}), bf16[8,128,128]{2,1,0:T(8,128)(2,1)S(1)}, u32[]{:S(2)}, u32[]{:S(2)}) async-start(bf16[8,128,128]{2,1,0:T(8,128)(2,1)} %bitcast.23), calls=%async_computation.1 | async-start | bytes 524288 | tf_op jit(solution)/shard_map/scatter/all_to_all | solution.py:302
  156.7 7.1 %collective-permute-start.30 = (bf16[544,128]{1,0:T(8,128)(2,1)S(1)}, bf16[544,128]{1,0:T(8,128)(2,1)S(1)}, u32[]{:S(2)}, u32[]{:S(2)}) collective-permute-start(bf16[544,128]{1,0:T(8,128)(2,1)S(1)} %get-tuple-element.76), channel_id=1, source_target_pairs={{0,64},{64,128},{128,192},{192,0},{1,65},{65,129},{129,193},{193,1... | collective-permute-start | bytes 417800 | tf_op jit(solution)/shard_map/scatter/ppermute | solution.py:21
  158.1 5.7 %collective-permute-start.31 = (bf16[544,128]{1,0:T(8,128)(2,1)S(1)}, bf16[544,128]{1,0:T(8,128)(2,1)S(1)}, u32[]{:S(2)}, u32[]{:S(2)}) collective-permute-start(bf16[544,128]{1,0:T(8,128)(2,1)S(1)} %get-tuple-element.77), channel_id=1, source_target_pairs={{0,128},{64,192},{128,0},{192,64},{1,129},{65,193},{129,1},{193,65... | collective-permute-start | bytes 417800 | tf_op jit(solution)/shard_map/scatter/ppermute | solution.py:21
  158.3 5.8 %collective-permute-start.32 = (bf16[544,128]{1,0:T(8,128)(2,1)S(1)}, bf16[544,128]{1,0:T(8,128)(2,1)S(1)}, u32[]{:S(2)}, u32[]{:S(2)}) collective-permute-start(bf16[544,128]{1,0:T(8,128)(2,1)S(1)} %get-tuple-element.78), channel_id=1, source_target_pairs={{0,192},{64,0},{128,64},{192,128},{1,193},{65,1},{129,65},{193,129... | collective-permute-start | bytes 417800 | tf_op jit(solution)/shard_map/scatter/ppermute | solution.py:21
  164.2 18.0 %collective-permute-start.36 = (bf16[256,128]{1,0:T(8,128)(2,1)S(1)}, bf16[256,128]{1,0:T(8,128)(2,1)S(1)}, u32[]{:S(2)}, u32[]{:S(2)}) collective-permute-start(bf16[256,128]{1,0:T(8,128)(2,1)S(1)} %pad_maximum_fusion.16), channel_id=1, source_target_pairs={{0,4},{4,0},{1,5},{5,1},{2,6},{6,2},{3,7},{7,3},{8,12},{12,8},{9,1... | collective-permute-start | bytes 196616 | tf_op jit(solution)/shard_map/scatter/ppermute | solution.py:30
  (14 other events, 182.9 us)
where the time goes:
time: 186 us; the launch traced here: 185 us
  starting transfers between devices  68.7 us (37%)
  waiting for transfers between devices  47.1 us (25%)
  Pallas kernels  28.5 us (15%)
  blocking collectives  22.1 us (12%)
  other arithmetic  9.05 us (5%)
  local copies, waits for them, and re-layouts  7.97 us (4%)
    ppermute x16, starting transfers between devices, shift_z(): return lax.ppermute(value, 'z', [(i, (i + k) % NZ) for i in range(NZ)])  28.6 us
    ppermute x16, waiting for transfers between devices, shift_z(): return lax.ppermute(value, 'z', [(i, (i + k) % NZ) for i in range(NZ)])  24.9 us
    ppermute x9, starting transfers between devices, swap(): return lax.ppermute(value, axes, pairs)  21.4 us
    all_gather x1, blocking collectives, shards(): quarters = lax.all_gather(grad, ('near', 'core'), axis=0)  15.8 us
    pallas_call x1, Pallas kernels, backward(): pl.pallas_call(functools.partial(backward_kernel, places), grid=(rows,),...  12.9 us
    pallas_call x1, Pallas kernels, forward(): pl.pallas_call(functools.partial(forward_kernel, places), grid=(rows,), o...  12.3 us
    ppermute x12, starting transfers between devices, shift_x(): return lax.ppermute(value, 'x', [(i, (i + k) % NX) for i in range(NX)])  11.4 us
    ppermute x12, waiting for transfers between devices, shift_x(): return lax.ppermute(value, 'x', [(i, (i + k) % NX) for i in range(NX)])  7.34 us
  transfers between devices with their start and end apart: 39, of which 22 were waited for; matrix products, arithmetic and copies ran while one was open for 7% of the time, Pallas kernels for 7%

commit v1 on v0

--- a/solution.py
+++ b/solution.py
@@ -41,59 +41,70 @@
     return add32(*values).astype(BF)
 
 
-def forward_kernel(places, rep_ref, count_ref, pos_ref, edge_ref, *rest):
+def each_row(count_ref, edge_ref, body):
+    rows, _, slots = edge_ref.shape[:3]
+
+    def row(t, carry):
+        count = count_ref[t]
+
+        @pl.when(count > GROUP)
+        def _():
+            body(t, count, slots)
+
+        @pl.when(count <= GROUP)
+        def _():
+            body(t, count, GROUP)
+
+        return carry
+
+    lax.fori_loop(0, rows, row, 0)
+
+
+def live_tile(edges, t, s, count):
+    tile = edges[t, 0, s]
+    return jnp.where(s < count, tile, jnp.zeros_like(tile))
+
+
+def forward_kernel(places, rep_ref, count_ref, pos_ref, edges, *rest):
     pieces = rest[: len(places)]
-    outs = rest[len(places):-2]
-    table, sems = rest[-2:]
-    step = pl.program_id(0)
-
-    @pl.when(step == 0)
-    def _():
-        copies = []
-        for i, (start, size) in enumerate(places):
-            copies.append(pltpu.make_async_copy(pieces[i], table.at[pl.ds(start, size)], sems.at[i]))
-        for copy in copies:
-            copy.start()
-        for copy in copies:
-            copy.wait()
-
-    count = count_ref[step]
-    slots = edge_ref.shape[2]
-
-    def body(g, acc):
-        left, right = [], []
-        for i in range(GROUP):
-            s = g * GROUP + i
-            tile = edge_ref[0, 0, s]
-            left.append(jnp.where(s < count, tile, jnp.zeros_like(tile)))
-            right.append(table[pos_ref[step * slots + s]])
-        return acc + jnp.dot(
+    outs, table = rest[len(places):-1], rest[-1]
+    slots = edges.shape[2]
+    for piece, (place, size) in zip(pieces, places):
+
+        def copy(i, carry, piece=piece, place=place):
+            table[pl.ds(place + i * 4, 4)] = piece[pl.ds(i * 4, 4)]
+            return carry
+
+        lax.fori_loop(0, size // 4, copy, 0)
+
+    def body(t, count, size):
+        left = [live_tile(edges, t, s, count) for s in range(size)]
+        right = [table[pos_ref[t * slots + s]] for s in range(size)]
+        total = jnp.dot(
             jnp.concatenate(left, axis=1), jnp.concatenate(right, axis=0), preferred_element_type=F32
-        )
-
-    groups = (count + (GROUP - 1)) // GROUP
-    acc = lax.fori_loop(0, groups, body, jnp.zeros((TILE, TILE), F32))
-    for q in range(len(outs)):
-
-        @pl.when((step // 2) ^ rep_ref[0] == q)
-        def _(q=q):
-            outs[q][step % 2] = acc.astype(BF)
+        ).astype(BF)
+        for q in range(len(outs)):
+
+            @pl.when((t // 2) ^ rep_ref[0] == q)
+            def _(q=q):
+                outs[q][t % 2] = total
+
+    each_row(count_ref, edges, body)
 
 
 def forward(rep, counts, positions, edge_tiles, pieces):
-    places = tuple((start, piece.shape[0]) for start, piece in pieces)
+    places = tuple((place, piece.shape[0]) for place, piece in pieces)
     arrays = [piece for _, piece in pieces]
     rows, _, slots = edge_tiles.shape[:3]
+    vmem = pl.BlockSpec(memory_space=VMEM)
     return pl.pallas_call(
         functools.partial(forward_kernel, places),
-        grid=(rows,),
         out_shape=(jax.ShapeDtypeStruct((2, TILE, TILE), BF),) * 4,
-        in_specs=[pl.BlockSpec(memory_space=SMEM)] * 3
-        + [pl.BlockSpec((1, 1, slots, TILE, TILE), lambda t: (t, 0, 0, 0, 0))]
-        + [pl.BlockSpec(memory_space=pl.ANY)] * len(arrays),
-        out_specs=(pl.BlockSpec((2, TILE, TILE), lambda t: (0, 0, 0)),) * 4,
-        scratch_shapes=[VMEM((2 * NX * NZ * NY, TILE, TILE), BF), pltpu.SemaphoreType.DMA((len(arrays),))],
-        compiler_params=pltpu.CompilerParams(vmem_limit_bytes=56 * 2**20),
+        in_specs=[pl.BlockSpec(memory_space=SMEM)] * 3 + [vmem] * (1 + len(arrays)),
+        out_specs=(vmem,) * 4,
+        scratch_shapes=[VMEM((2 * NX * NZ * NY, TILE, TILE), BF)],
+        compiler_params=pltpu.CompilerParams(vmem_limit_bytes=24 * 2**20),
+        cost_estimate=pl.CostEstimate(flops=2 * rows * slots * TILE**3, bytes_accessed=11 * 2**20, transcendentals=0),
         name="forward",
     )(rep, counts, positions, edge_tiles, *arrays)
 
@@ -153,63 +164,49 @@
     )(rep, *parts, weight, bias.reshape(1, -1), cotangent)
 
 
-def backward_kernel(places, count_ref, pos_ref, edge_ref, slope_ref, *rest):
+def backward_kernel(places, count_ref, pos_ref, edges, slope_ref, *rest):
     outs, totals = rest[:-1], rest[-1]
-    step = pl.program_id(0)
-
-    @pl.when(step == 0)
-    def _():
-        def clear(i, carry):
-            totals[pl.ds(i * 8, 8)] = jnp.zeros((8, TILE, TILE), F32)
+    slots = edges.shape[2]
+
+    def clear(i, carry):
+        totals[pl.ds(i * 8, 8)] = jnp.zeros((8, TILE, TILE), F32)
+        return carry
+
+    lax.fori_loop(0, totals.shape[0] // 8, clear, 0)
+
+    def body(t, count, size):
+        slope = slope_ref[t]
+        for g in range(size // GROUP):
+            which = range(g * GROUP, (g + 1) * GROUP)
+            tiles = [live_tile(edges, t, s, count) for s in which]
+            terms = jnp.dot(slope, jnp.concatenate(tiles, axis=1), preferred_element_type=F32)
+            where = [pos_ref[t * slots + s] for s in which]
+            old = [totals[w] for w in where]
+            for i, w in enumerate(where):
+                totals[w] = old[i] + terms[:, i * TILE:(i + 1) * TILE]
+
+    each_row(count_ref, edges, body)
+
+    for out, (place, size) in zip(outs, places):
+
+        def store(i, carry, out=out, place=place):
+            out[pl.ds(i * 4, 4)] = totals[pl.ds(place + i * 4, 4)].astype(out.dtype)
             return carry
 
-        lax.fori_loop(0, totals.shape[0] // 8, clear, 0)
-
-    count = count_ref[step]
-    slots = edge_ref.shape[2]
-    slope = slope_ref[step]
-
-    def body(g, carry):
-        tiles, where = [], []
-        for i in range(GROUP):
-            s = g * GROUP + i
-            tile = edge_ref[0, 0, s]
-            tiles.append(jnp.where(s < count, tile, jnp.zeros_like(tile)))
-            where.append(pos_ref[step * slots + s])
-        terms = jnp.dot(slope, jnp.concatenate(tiles, axis=1), preferred_element_type=F32)
-        old = [totals[w] for w in where]
-        for i in range(GROUP):
-            totals[where[i]] = old[i] + terms[:, i * TILE:(i + 1) * TILE]
-        return carry
-
-    lax.fori_loop(0, (count + (GROUP - 1)) // GROUP, body, 0)
-
-    @pl.when(step == pl.num_programs(0) - 1)
-    def _():
-        for out, (start, size) in zip(outs, places):
-            def store(i, carry, out=out, start=start):
-                out[i] = totals[start + i].astype(out.dtype)
-                return carry
-
-            lax.fori_loop(0, size, store, 0)
+        lax.fori_loop(0, size // 4, store, 0)
 
 
 def backward(counts, positions, edge_tiles, slope, places):
     rows, _, slots = edge_tiles.shape[:3]
-    whole = lambda t: (0, 0, 0)
+    vmem = pl.BlockSpec(memory_space=VMEM)
     return pl.pallas_call(
         functools.partial(backward_kernel, places),
-        grid=(rows,),
         out_shape=tuple(jax.ShapeDtypeStruct((size, TILE, TILE), BF) for _, size in places),
-        in_specs=[
-            pl.BlockSpec(memory_space=SMEM),
-            pl.BlockSpec(memory_space=SMEM),
-            pl.BlockSpec((1, 1, slots, TILE, TILE), lambda t: (t, 0, 0, 0, 0)),
-            pl.BlockSpec(slope.shape, whole),
-        ],
-        out_specs=tuple(pl.BlockSpec((size, TILE, TILE), whole) for _, size in places),
+        in_specs=[pl.BlockSpec(memory_space=SMEM)] * 2 + [vmem, vmem],
+        out_specs=(vmem,) * len(places),
         scratch_shapes=[VMEM((2 * NX * NZ * NY, TILE, TILE), F32)],
-        compiler_params=pltpu.CompilerParams(vmem_limit_bytes=56 * 2**20),
+        compiler_params=pltpu.CompilerParams(vmem_limit_bytes=28 * 2**20),
+        cost_estimate=pl.CostEstimate(flops=2 * rows * slots * TILE**3, bytes_accessed=15 * 2**20, transcendentals=0),
         name="backward",
     )(counts, positions, edge_tiles, slope)
 
@@ -242,23 +239,22 @@
 
 def gather_features(own):
     other = swap(own, "y")
-    base = jnp.concatenate([own, other[:1]])
-    spread = jnp.broadcast_to(other[None, 1], (NZ, TILE, TILE))
+    plane = jnp.concatenate([own, shift_x(own, 1), shift_x(own, 2), shift_x(own, -1)])
+    spread = jnp.broadcast_to(other[None], (NZ,) + other.shape).reshape(2 * NZ, TILE, TILE)
     line = lax.all_to_all(spread, "z", 0, 0, tiled=True)
-    plane = jnp.concatenate([base, shift_x(base, 1), shift_x(base, 2), shift_x(base, -1)])
-    pieces = [(0, plane), (96, line)]
+    pieces = [(0, plane), (64, line)]
     for k, hop in ((1, 1), (2, 2), (3, -1)):
-        pieces.append((96 + 8 * k, shift_x(line, hop)))
+        pieces.append((64 + 16 * k, shift_x(line, hop)))
     up = down = plane
     for k in (1, 2, 3):
         up, down = shift_z(up, 1), shift_z(down, -1)
-        pieces += [(12 * k, up), (12 * (8 - k), down)]
-    pieces += [(48, shift_z(up[:6], 1)), (54, shift_z(down[6:], -1))]
+        pieces += [(8 * k, up), (8 * (8 - k), down)]
+    pieces += [(32, shift_z(up[:4], 1)), (36, shift_z(down[4:], -1))]
     return pieces
 
 
-A_PLACES = ((48, 6), (54, 6)) + tuple((12 * k, 12) for k in (3, 5, 2, 6, 1, 7, 0))
-B_PLACES = tuple((96 + 8 * k, 8) for k in range(4))
+A_PLACES = ((32, 4), (36, 4)) + tuple((8 * k, 8) for k in (3, 5, 2, 6, 1, 7, 0))
+B_PLACES = tuple((64 + 16 * k, 16) for k in range(4))
 
 
 def split(value):
@@ -276,12 +272,14 @@
     up, down = rows[0], rows[1]
     ups, downs = [None, rows[2], rows[4], rows[6]], [None, rows[3], rows[5], rows[7]]
     b = rows[9:]
-    got_b = [shift_x(b[1], 1), shift_x(b[2], 2), shift_x(b[3], -1)]
-    half, full = 6 * TILE, 12 * TILE
+    line = add(b[0], shift_x(b[1], 1), shift_x(b[2], 2), shift_x(b[3], -1))
+    half, full = 4 * TILE, 8 * TILE
     wide = split(grad)
     grads = [grad]
     ride_up = ride_down = wide
     for step in range(4):
+        if step == 2:
+            up, line = lax.optimization_barrier((up, line))
         up = shift_z(jnp.concatenate([up, ride_up]), 1)
         if step < 3:
             down = shift_z(jnp.concatenate([down, ride_down]), -1)
@@ -298,19 +296,17 @@
             down = shift_z(down, -1)
             grads.append(join(up[full:]))
             up = up[:full]
-    line = add(b[0], *got_b)
-    line = lax.all_to_all(line.reshape(NZ, TILE, TILE), "z", 0, 0, tiled=True)
+    line = lax.all_to_all(line.reshape(2 * NZ, TILE, TILE), "z", 0, 0, tiled=True)
+    theirs = swap(add(*[line[2 * k:2 * k + 2] for k in range(NZ)]), "y")
     grad = add32(*grads)
     wide = split(grad)
-    part = 3 * TILE
+    part = 2 * TILE
     total = add32(rows[8], up, down)
     sent = [total[k * part:(k + 1) * part].astype(BF) for k in (1, 2, 3)]
     got = [shift_x(jnp.concatenate([v, wide]), hop) for v, hop in zip(sent, (1, 2, -1))]
     total = add32(total[:part], *[g[:part] for g in got])
     grad = add32(grad, *[join(g[part:]) for g in got])
-    last_b = add(*[line[k] for k in range(NZ)])
-    theirs = swap(jnp.concatenate([total[2 * TILE:].astype(BF), last_b]), "y")
-    return total[:2 * TILE].reshape(2, TILE, TILE), theirs.reshape(2, TILE, TILE), grad
+    return total.reshape(2, TILE, TILE), theirs, grad
 
 
 def shards(features, weight, bias_vector, edge_tiles, tile_columns, live_counts, cotangent):
@@ -319,10 +315,9 @@
     columns = tile_columns.reshape(-1)
     owner, which = columns // 2, columns % 2
     ox, oz, oy = owner // (NZ * NY), (owner // NY) % NZ, owner % NY
-    kind = (oy ^ y) * 2 + which
 
     def places(dx, dz):
-        return jnp.where(kind < 3, (dz * NX + dx) * 3 + kind, 96 + dx * NZ + oz).astype(jnp.int32)
+        return (jnp.where(oy == y, dz * NX + dx, 32 + dx * NZ + oz) * 2 + which).astype(jnp.int32)
 
     behind = places((x - ox) % NX, (z - oz) % NZ)
     ahead = places((ox - x) % NX, (oz - z) % NZ)
@@ -339,12 +334,14 @@
             swap(partial[3], "near", "core"),
         ]
     hidden_out, slope, near, pair, far = middle(rep, parts, weight, bias_vector, cotangent)
+    with jax.named_scope("weights"):
+        pair = swap(pair, "core")
+        near, far, slope = lax.optimization_barrier((near + pair[0], far + pair[1], slope))
+        grads = [swap(far, "near"), swap(near, "y"), swap(far, "y", "near")]
     with jax.named_scope("slopes"):
         slopes = lax.all_gather(slope, ("near", "core"), axis=0, tiled=True)
-    with jax.named_scope("weights"):
-        pair = swap(pair, "core")
-        near, far = near + pair[0], far + pair[1]
-        grad = near + swap(far, "near") + swap(near, "y") + swap(far, "y", "near")
+        grad = add32(near, *grads)
+        slopes, grad = lax.optimization_barrier((slopes, grad))
     totals = backward(counts, ahead, edge_tiles, slopes, A_PLACES + B_PLACES)
     with jax.named_scope("scatter"):
         mine, theirs, grad = scatter_totals(totals, grad)

time: 186 us -> 171 us (0.919)
  Pallas kernels: 28.5 us -> 13.4 us
  waiting for transfers between devices: 47.1 us -> 58.8 us
  blocking collectives: 22.1 us -> 16.2 us
  other arithmetic: 9.05 us -> 5.01 us
  local copies, waits for them, and re-layouts: 7.97 us -> 5.68 us
    ppermute x12, waiting for transfers between devices: 7.34 us -> 22.5 us  [shift_x(): return lax.ppermute(value, 'x', [(i, (i + k) % NX) for i in range(NX)])]
    pallas_call x2, Pallas kernels: 25.1 us -> 10 us  [the longest x1 5.16 us: backward(): pl.pallas_call(functools.partial(backward_kernel, places), out_shape=tupl...]
    ppermute x12, starting transfers between devices: 11.4 us -> 20.7 us  [shift_x(): return lax.ppermute(value, 'x', [(i, (i + k) % NX) for i in range(NX)])]
    ppermute x9, starting transfers between devices: 21.4 us -> 14.7 us  [swap(): return lax.ppermute(value, axes, pairs)]
    ppermute x16, starting transfers between devices: 28.6 us -> 22.5 us  [shift_z(): return lax.ppermute(value, 'z', [(i, (i + k) % NZ) for i in range(NZ)])]
    all_gather x1, blocking collectives: 15.8 us -> 9.86 us  [shards(): quarters = lax.all_gather(grad, ('near', 'core'), axis=0)]
    all_to_all x1, starting transfers between devices: 3.89 us -> 8.37 us  [gather_features(): line = lax.all_to_all(spread, 'z', 0, 0, tiled=True)]
    all_to_all x1, waiting for transfers between devices: 4.39 us -> 0.01 us  [gather_features(): line = lax.all_to_all(spread, 'z', 0, 0, tiled=True)]
  transfers between devices with their start and end apart: 39 -> 39, of which waited for: 22 -> 21; matrix products, arithmetic and copies ran while one was open for 7% -> 3% of each run, Pallas kernels for 7% -> 0%
where the time goes in v1:
time: 171 us
  starting transfers between devices  70.5 us (41%)
  waiting for transfers between devices  58.8 us (34%)
  blocking collectives  16.2 us (9%)
  Pallas kernels  13.4 us (8%)
  local copies, waits for them, and re-layouts  5.68 us (3%)
  other arithmetic  5.01 us (3%)
    ppermute x16, waiting for transfers between devices, shift_z(): return lax.ppermute(value, 'z', [(i, (i + k) % NZ) for i in range(NZ)])  26.7 us
    ppermute x16, starting transfers between devices, shift_z(): return lax.ppermute(value, 'z', [(i, (i + k) % NZ) for i in range(NZ)])  22.5 us
    ppermute x12, waiting for transfers between devices, shift_x(): return lax.ppermute(value, 'x', [(i, (i + k) % NX) for i in range(NX)])  22.5 us
    ppermute x12, starting transfers between devices, shift_x(): return lax.ppermute(value, 'x', [(i, (i + k) % NX) for i in range(NX)])  20.7 us
    ppermute x9, starting transfers between devices, swap(): return lax.ppermute(value, axes, pairs)  14.7 us
    all_gather x1, blocking collectives, shards(): quarters = lax.all_gather(grad, ('near', 'core'), axis=0)  9.86 us
    all_to_all x1, starting transfers between devices, gather_features(): line = lax.all_to_all(spread, 'z', 0, 0, tiled=True)  8.37 us
    ppermute x9, waiting for transfers between devices, swap(): return lax.ppermute(value, axes, pairs)  6.45 us
  transfers between devices with their start and end apart: 39, of which 21 were waited for; matrix products, arithmetic and copies ran while one was open for 3% of the time, Pallas kernels for 0%

profile of v1, /device:TPU:1, one launch (start us, length us, event | category | flops | bytes accessed | tf_op | source)
XLA Modules:
  0.0 170.6 jit_solution(3784484453171356646)
XLA Ops:
  0.6 3.8 %collective-permute-start.3 = (bf16[2,128,128]{2,1,0:T(8,128)(2,1)}, bf16[2,128,128]{2,1,0:T(8,128)(2,1)S(1)}, u32[]{:S(2)}, u32[]{:S(2)}) collective-permute-start(bf16[2,128,128]{2,1,0:T(8,128)(2,1)} %bitcast.61), channel_id=1, source_target_pairs={{0,4},{4,0},{1,5},{5,1},{2,6},{6,2},{3,7},{7,3},{8,12},{12,8},{9,1... | collective-permute-start | bytes 196616 | tf_op jit(solution)/shard_map/gather/ppermute | solution.py:30
  4.5 1.9 %collective-permute-done.3 = bf16[2,128,128]{2,1,0:T(8,128)(2,1)S(1)} collective-permute-done((bf16[2,128,128]{2,1,0:T(8,128)(2,1)}, bf16[2,128,128]{2,1,0:T(8,128)(2,1)S(1)}, u32[]{:S(2)}, u32[]{:S(2)}) %collective-permute-start.3) | collective-permute-done | bytes 65568 | tf_op jit(solution)/shard_map/gather/ppermute | solution.py:30
  7.3 8.4 %all-to-all-start = ((bf16[16,128,128]{2,1,0:T(8,128)(2,1)}), bf16[16,128,128]{2,1,0:T(8,128)(2,1)S(1)}, u32[]{:S(2)}, u32[]{:S(2)}) async-start(bf16[16,128,128]{2,1,0:T(8,128)(2,1)} %bitcast.3), calls=%async_computation | async-start | bytes 1048576 | tf_op jit(solution)/shard_map/gather/all_to_all | solution.py:244
  16.8 2.5 %collective-permute-start.1 = (bf16[2,128,128]{2,1,0:T(8,128)(2,1)}, bf16[2,128,128]{2,1,0:T(8,128)(2,1)S(1)}, u32[]{:S(2)}, u32[]{:S(2)}) collective-permute-start(bf16[2,128,128]{2,1,0:T(8,128)(2,1)} %bitcast.63), channel_id=1, source_target_pairs={{0,128},{64,192},{128,0},{192,64},{1,129},{65,193},{129,1},{193,65... | collective-permute-start | bytes 196616 | tf_op jit(solution)/shard_map/gather/ppermute | solution.py:21
  20.4 1.4 collective-permute-done.1
  23.8 1.5 collective-permute-start.7
  25.3 1.3 collective-permute-start.8
  26.6 7.7 %collective-permute-done.7.rest_5_ = bf16[8,128,128]{2,1,0:T(8,128)(2,1)S(1)} collective-permute-done((bf16[8,128,128]{2,1,0:T(8,128)(2,1)S(1)}, bf16[8,128,128]{2,1,0:T(8,128)(2,1)S(1)}, u32[]{:S(2)}, u32[]{:S(2)}) %collective-permute-start.7) | collective-permute-done | bytes 262176 | tf_op jit(solution)/shard_map/gather/ppermute | solution.py:25
  34.3 2.7 %collective-permute-start.10 = (bf16[8,128,128]{2,1,0:T(8,128)(2,1)S(1)}, bf16[8,128,128]{2,1,0:T(8,128)(2,1)}, u32[]{:S(2)}, u32[]{:S(2)}) collective-permute-start(bf16[8,128,128]{2,1,0:T(8,128)(2,1)S(1)} %collective-permute-done.8.rest_6_), channel_id=1, source_target_pairs={{0,56},{8,0},{16,8},{24,16},{32,24},{40,32},{48,40},{56,48},{1,57}... | collective-permute-start | bytes 786440 | tf_op jit(solution)/shard_map/gather/ppermute | solution.py:25
  37.0 2.0 %collective-permute-start.4 = (bf16[16,128,128]{2,1,0:T(8,128)(2,1)S(1)}, bf16[16,128,128]{2,1,0:T(8,128)(2,1)S(1)}, u32[]{:S(2)}, u32[]{:S(2)}) collective-permute-start(bf16[16,128,128]{2,1,0:T(8,128)(2,1)S(1)} %all-to-all-done.rest_1_), channel_id=1, source_target_pairs={{0,64},{64,128},{128,192},{192,0},{1,65},{65,129},{129,193},{193,1... | collective-permute-start | bytes 1572872 | tf_op jit(solution)/shard_map/gather/ppermute | solution.py:21
  39.0 1.9 %collective-permute-start.5 = (bf16[16,128,128]{2,1,0:T(8,128)(2,1)S(1)}, bf16[16,128,128]{2,1,0:T(8,128)(2,1)S(1)}, u32[]{:S(2)}, u32[]{:S(2)}) collective-permute-start(bf16[16,128,128]{2,1,0:T(8,128)(2,1)S(1)} %all-to-all-done.rest_1_), channel_id=1, source_target_pairs={{0,128},{64,192},{128,0},{192,64},{1,129},{65,193},{129,1},{193,65... | collective-permute-start | bytes 1572872 | tf_op jit(solution)/shard_map/gather/ppermute | solution.py:21
  41.0 2.1 %collective-permute-start.6 = (bf16[16,128,128]{2,1,0:T(8,128)(2,1)S(1)}, bf16[16,128,128]{2,1,0:T(8,128)(2,1)S(1)}, u32[]{:S(2)}, u32[]{:S(2)}) collective-permute-start(bf16[16,128,128]{2,1,0:T(8,128)(2,1)S(1)} %all-to-all-done.rest_1_), channel_id=1, source_target_pairs={{0,192},{64,0},{128,64},{192,128},{1,193},{65,1},{129,65},{193,129... | collective-permute-start | bytes 1572872 | tf_op jit(solution)/shard_map/gather/ppermute | solution.py:21
  43.0 2.7 %collective-permute-start.12 = (bf16[8,128,128]{2,1,0:T(8,128)(2,1)}, bf16[8,128,128]{2,1,0:T(8,128)(2,1)S(1)}, u32[]{:S(2)}, u32[]{:S(2)}) collective-permute-start(bf16[8,128,128]{2,1,0:T(8,128)(2,1)} %collective-permute-done.10.rest_8_), channel_id=1, source_target_pairs={{0,56},{8,0},{16,8},{24,16},{32,24},{40,32},{48,40},{56,48},{1,57}... | collective-permute-start | bytes 786440 | tf_op jit(solution)/shard_map/gather/ppermute | solution.py:25
  46.2 1.3 reduce.3
  47.7 2.3 %collective-permute-done.11.rest_9_ = bf16[8,128,128]{2,1,0:T(8,128)(2,1)S(1)} collective-permute-done((bf16[8,128,128]{2,1,0:T(8,128)(2,1)}, bf16[8,128,128]{2,1,0:T(8,128)(2,1)S(1)}, u32[]{:S(2)}, u32[]{:S(2)}) %collective-permute-start.11) | collective-permute-done | bytes 262176 | tf_op jit(solution)/shard_map/gather/ppermute | solution.py:25
  50.1 2.7 %collective-permute-start.14 = (bf16[4,128,128]{2,1,0:T(8,128)(2,1)S(1)}, bf16[4,128,128]{2,1,0:T(8,128)(2,1)S(1)}, u32[]{:S(2)}, u32[]{:S(2)}) collective-permute-start(bf16[4,128,128]{2,1,0:T(8,128)(2,1)S(1)} %slice.259), channel_id=1, source_target_pairs={{0,56},{8,0},{16,8},{24,16},{32,24},{40,32},{48,40},{56,48},{1,57}... | collective-permute-start | bytes 393224 | tf_op jit(solution)/shard_map/gather/ppermute | solution.py:25
  52.9 2.2 %collective-permute-done.13.rest_11_ = bf16[4,128,128]{2,1,0:T(8,128)(2,1)S(1)} collective-permute-done((bf16[4,128,128]{2,1,0:T(8,128)(2,1)S(1)}, bf16[4,128,128]{2,1,0:T(8,128)(2,1)S(1)}, u32[]{:S(2)}, u32[]{:S(2)}) %collective-permute-start.13) | collective-permute-done | bytes 131104 | tf_op jit(solution)/shard_map/gather/ppermute | solution.py:25
  55.1 6.1 %collective-permute-done.5.rest_3_ = bf16[16,128,128]{2,1,0:T(8,128)(2,1)S(1)} collective-permute-done((bf16[16,128,128]{2,1,0:T(8,128)(2,1)S(1)}, bf16[16,128,128]{2,1,0:T(8,128)(2,1)S(1)}, u32[]{:S(2)}, u32[]{:S(2)}) %collective-permute-start.5) | collective-permute-done | bytes 524320 | tf_op jit(solution)/shard_map/gather/ppermute | solution.py:21
  61.2 2.0 %collective-permute-done.6.rest_4_ = bf16[16,128,128]{2,1,0:T(8,128)(2,1)S(1)} collective-permute-done((bf16[16,128,128]{2,1,0:T(8,128)(2,1)S(1)}, bf16[16,128,128]{2,1,0:T(8,128)(2,1)S(1)}, u32[]{:S(2)}, u32[]{:S(2)}) %collective-permute-start.6) | collective-permute-done | bytes 524320 | tf_op jit(solution)/shard_map/gather/ppermute | solution.py:21
  63.2 2.8 %copy-done = bf16[8,1,24,128,128]{4,3,2,1,0:T(8,128)(2,1)S(1)} copy-done((bf16[8,1,24,128,128]{4,3,2,1,0:T(8,128)(2,1)S(1)}, bf16[8,1,24,128,128]{4,3,2,1,0:T(8,128)(2,1)}, u32[]{:S(2)}) %copy-start) | copy-done | bytes 6291480
  66.7 4.9 %forward.1 = (bf16[2,128,128]{2,1,0:T(8,128)(2,1)S(1)}, bf16[2,128,128]{2,1,0:T(8,128)(2,1)S(1)}, bf16[2,128,128]{2,1,0:T(8,128)(2,1)S(1)}, bf16[2,128,128]{2,1,0:T(8,128)(2,1)S(1)}) custom-call(s32[1]{0:T(128)} %bitcast.rep_ref, s32[8]{0:T(128)S(1)} %bitcast.51, s32[192]{0:T(256)S(1)} %multiply_add_fusion.1.pos_ref, ...), custom_call_target="tpu_custom_call" | custom-call | flops 805306368 | bytes 11534336 | tf_op jit(solution)/shard_map/forward/pallas_call | solution.py:100
  71.6 2.1 %collective-permute-start.15 = (bf16[2,128,128]{2,1,0:T(8,128)(2,1)S(1)}, bf16[2,128,128]{2,1,0:T(8,128)(2,1)S(1)}, u32[]{:S(2)}, u32[]{:S(2)}) collective-permute-start(bf16[2,128,128]{2,1,0:T(8,128)(2,1)S(1)} %get-tuple-element.37), channel_id=1, source_target_pairs={{0,1},{1,0},{2,3},{3,2},{4,5},{5,4},{6,7},{7,6},{8,9},{9,8},{10,11... | collective-permute-start | bytes 196616 | tf_op jit(solution)/shard_map/sections/ppermute | solution.py:30
  73.7 1.3 collective-permute-start.16
  75.4 1.9 %collective-permute-done.16.p2 = bf16[2,128,128]{2,1,0:T(8,128)(2,1)S(1)} collective-permute-done((bf16[2,128,128]{2,1,0:T(8,128)(2,1)S(1)}, bf16[2,128,128]{2,1,0:T(8,128)(2,1)S(1)}, u32[]{:S(2)}, u32[]{:S(2)}) %collective-permute-start.16) | collective-permute-done | bytes 65568 | tf_op jit(solution)/shard_map/sections/ppermute | solution.py:30
  77.3 1.7 %collective-permute-done.17.p3 = bf16[2,128,128]{2,1,0:T(8,128)(2,1)S(1)} collective-permute-done((bf16[2,128,128]{2,1,0:T(8,128)(2,1)S(1)}, bf16[2,128,128]{2,1,0:T(8,128)(2,1)S(1)}, u32[]{:S(2)}, u32[]{:S(2)}) %collective-permute-start.17) | collective-permute-done | bytes 65568 | tf_op jit(solution)/shard_map/sections/ppermute | solution.py:30
  79.0 1.6 middle.1
  82.0 1.2 collective-permute-start.19
  83.2 2.0 %collective-permute-start.21 = (f32[80,128]{1,0:T(8,128)S(1)}, f32[80,128]{1,0:T(8,128)S(1)}, u32[]{:S(2)}, u32[]{:S(2)}) collective-permute-start(f32[80,128]{1,0:T(8,128)S(1)} %get-tuple-element.47), channel_id=1, source_target_pairs={{0,6},{2,4},{4,2},{6,0},{1,7},{3,5},{5,3},{7,1},{8,14},{10,12},{12... | collective-permute-start | bytes 122888 | tf_op jit(solution)/shard_map/weights/ppermute | solution.py:30
  85.9 6.4 %all_gather.9.slope_ref = bf16[8,128,128]{2,1,0:T(8,128)(2,1)S(1)} all-gather(bf16[2,128,128]{2,1,0:T(8,128)(2,1)S(1)} %get-tuple-element.45), channel_id=1, replica_groups=mesh['x'=4,'z'=8,'y'=2,'near'=2,'core'=2] {'near','core'}, dimensions={0}, use_global_device_ids=true | all-gather | bytes 327680 | tf_op jit(solution)/shard_map/slopes/all_gather | solution.py:342
  92.3 5.2 %backward.1 = (bf16[4,128,128]{2,1,0:T(8,128)(2,1)S(1)}, bf16[4,128,128]{2,1,0:T(8,128)(2,1)S(1)}, bf16[8,128,128]{2,1,0:T(8,128)(2,1)S(1)}, bf16[8,128,128]{2,1...) custom-call(s32[8]{0:T(128)S(1)} %bitcast.52, ...), custom_call_target="tpu_custom_call" | custom-call | flops 805306368 | bytes 15728640 | tf_op jit(solution)/shard_map/backward/pallas_call | solution.py:202
  97.6 1.7 collective-permute-start.25
  99.2 2.0 %collective-permute-start.26 = (bf16[2048,128]{1,0:T(8,128)(2,1)S(1)}, bf16[2048,128]{1,0:T(8,128)(2,1)S(1)}, u32[]{:S(2)}, u32[]{:S(2)}) collective-permute-start(bf16[2048,128]{1,0:T(8,128)(2,1)S(1)} %bitcast.54), channel_id=1, source_target_pairs={{0,192},{64,0},{128,64},{192,128},{1,193},{65,1},{129,65},{193,129... | collective-permute-start | bytes 1572872 | tf_op jit(solution)/shard_map/scatter/ppermute | solution.py:21
  101.4 2.7 %collective-permute-start.29 = (bf16[672,128]{1,0:T(8,128)(2,1)S(1)}, bf16[672,128]{1,0:T(8,128)(2,1)S(1)}, u32[]{:S(2)}, u32[]{:S(2)}) collective-permute-start(bf16[672,128]{1,0:T(8,128)(2,1)S(1)} %get-tuple-element.88), channel_id=1, source_target_pairs={{0,56},{8,0},{16,8},{24,16},{32,24},{40,32},{48,40},{56,48},{1,57}... | collective-permute-start | bytes 516104 | tf_op jit(solution)/shard_map/scatter/ppermute | solution.py:25
  104.1 3.3 %collective-permute-done.22 = bf16[672,128]{1,0:T(8,128)(2,1)S(1)} collective-permute-done((bf16[672,128]{1,0:T(8,128)(2,1)S(1)}, bf16[672,128]{1,0:T(8,128)(2,1)S(1)}, u32[]{:S(2)}, u32[]{:S(2)}) %collective-permute-start.22) | collective-permute-done | bytes 172064 | tf_op jit(solution)/shard_map/scatter/ppermute | solution.py:25
  107.7 2.7 %collective-permute-start.30 = (bf16[1184,128]{1,0:T(8,128)(2,1)S(1)}, bf16[1184,128]{1,0:T(8,128)(2,1)S(1)}, u32[]{:S(2)}, u32[]{:S(2)}) collective-permute-start(bf16[1184,128]{1,0:T(8,128)(2,1)S(1)} %pad_maximum_fusion.3), channel_id=1, source_target_pairs={{0,56},{8,0},{16,8},{24,16},{32,24},{40,32},{48,40},{56,48},{1,57}... | collective-permute-start | bytes 909320 | tf_op jit(solution)/shard_map/scatter/ppermute | solution.py:25
  110.4 5.1 %collective-permute-done.23 = bf16[1184,128]{1,0:T(8,128)(2,1)S(1)} collective-permute-done((bf16[1184,128]{1,0:T(8,128)(2,1)S(1)}, bf16[1184,128]{1,0:T(8,128)(2,1)S(1)}, u32[]{:S(2)}, u32[]{:S(2)}) %collective-permute-start.23) | collective-permute-done | bytes 303136 | tf_op jit(solution)/shard_map/scatter/ppermute | solution.py:25
  115.6 7.7 %collective-permute-done.24 = bf16[2048,128]{1,0:T(8,128)(2,1)S(1)} collective-permute-done((bf16[2048,128]{1,0:T(8,128)(2,1)S(1)}, bf16[2048,128]{1,0:T(8,128)(2,1)S(1)}, u32[]{:S(2)}, u32[]{:S(2)}) %collective-permute-start.24) | collective-permute-done | bytes 524320 | tf_op jit(solution)/shard_map/scatter/ppermute | solution.py:21
  125.0 3.0 %collective-permute-start.31 = (bf16[1184,128]{1,0:T(8,128)(2,1)S(1)}, bf16[1184,128]{1,0:T(8,128)(2,1)S(1)}, u32[]{:S(2)}, u32[]{:S(2)}) collective-permute-start(bf16[1184,128]{1,0:T(8,128)(2,1)S(1)} %pad_maximum_fusion.4), channel_id=1, source_target_pairs={{0,56},{8,0},{16,8},{24,16},{32,24},{40,32},{48,40},{56,48},{1,57}... | collective-permute-start | bytes 909320 | tf_op jit(solution)/shard_map/scatter/ppermute | solution.py:25
  128.0 5.5 %collective-permute-done.27 = bf16[1184,128]{1,0:T(8,128)(2,1)S(1)} collective-permute-done((bf16[1184,128]{1,0:T(8,128)(2,1)S(1)}, bf16[1184,128]{1,0:T(8,128)(2,1)S(1)}, u32[]{:S(2)}, u32[]{:S(2)}) %collective-permute-start.27) | collective-permute-done | bytes 303136 | tf_op jit(solution)/shard_map/scatter/ppermute | solution.py:25
  133.8 2.7 %collective-permute-start.32 = (bf16[1024,128]{1,0:T(8,128)(2,1)S(1)}, bf16[1024,128]{1,0:T(8,128)(2,1)S(1)}, u32[]{:S(2)}, u32[]{:S(2)}) collective-permute-start(bf16[1024,128]{1,0:T(8,128)(2,1)S(1)} %fusion.3), channel_id=1, source_target_pairs={{0,56},{8,0},{16,8},{24,16},{32,24},{40,32},{48,40},{56,48},{1,57}... | collective-permute-start | bytes 786440 | tf_op jit(solution)/shard_map/scatter/ppermute | solution.py:25
  136.5 4.2 %all-to-all-start.1 = ((bf16[16,128,128]{2,1,0:T(8,128)(2,1)}), bf16[16,128,128]{2,1,0:T(8,128)(2,1)S(1)}, u32[]{:S(2)}, u32[]{:S(2)}) async-start(bf16[16,128,128]{2,1,0:T(8,128)(2,1)} %bitcast.23), calls=%async_computation.1 | async-start | bytes 1048576 | tf_op jit(solution)/shard_map/scatter/all_to_all | solution.py:299
  141.6 3.6 %collective-permute-start.33 = (bf16[416,128]{1,0:T(8,128)(2,1)S(1)}, bf16[416,128]{1,0:T(8,128)(2,1)S(1)}, u32[]{:S(2)}, u32[]{:S(2)}) collective-permute-start(bf16[416,128]{1,0:T(8,128)(2,1)S(1)} %get-tuple-element.84), channel_id=1, source_target_pairs={{0,64},{64,128},{128,192},{192,0},{1,65},{65,129},{129,193},{193,1... | collective-permute-start | bytes 319496 | tf_op jit(solution)/shard_map/scatter/ppermute | solution.py:21
  145.2 2.6 %collective-permute-start.34 = (bf16[416,128]{1,0:T(8,128)(2,1)S(1)}, bf16[416,128]{1,0:T(8,128)(2,1)S(1)}, u32[]{:S(2)}, u32[]{:S(2)}) collective-permute-start(bf16[416,128]{1,0:T(8,128)(2,1)S(1)} %get-tuple-element.85), channel_id=1, source_target_pairs={{0,128},{64,192},{128,0},{192,64},{1,129},{65,193},{129,1},{193,65... | collective-permute-start | bytes 319496 | tf_op jit(solution)/shard_map/scatter/ppermute | solution.py:21
  148.7 2.6 %collective-permute-done.34 = bf16[416,128]{1,0:T(8,128)(2,1)S(1)} collective-permute-done((bf16[416,128]{1,0:T(8,128)(2,1)S(1)}, bf16[416,128]{1,0:T(8,128)(2,1)S(1)}, u32[]{:S(2)}, u32[]{:S(2)}) %collective-permute-start.34) | collective-permute-done | bytes 106528 | tf_op jit(solution)/shard_map/scatter/ppermute | solution.py:21
  152.3 3.1 %all-to-all-done.1 = bf16[16,128,128]{2,1,0:T(8,128)(2,1)S(1)} async-done(((bf16[16,128,128]{2,1,0:T(8,128)(2,1)}), bf16[16,128,128]{2,1,0:T(8,128)(2,1)S(1)}, u32[]{:S(2)}, u32[]{:S(2)}) %all-to-all-start.1) | async-done | bytes 524320 | tf_op jit(solution)/shard_map/scatter/all_to_all | solution.py:299
  155.5 2.9 %collective-permute-start.36 = (bf16[2,128,128]{2,1,0:T(8,128)(2,1)S(1)}, bf16[2,128,128]{2,1,0:T(8,128)(2,1)S(1)}, u32[]{:S(2)}, u32[]{:S(2)}) collective-permute-start(bf16[2,128,128]{2,1,0:T(8,128)(2,1)S(1)} %add_convert_fusion), channel_id=1, source_target_pairs={{0,4},{4,0},{1,5},{5,1},{2,6},{6,2},{3,7},{7,3},{8,12},{12,8},{9,1... | collective-permute-start | bytes 196616 | tf_op jit(solution)/shard_map/scatter/ppermute | solution.py:30
  158.4 9.9 %all-gather = f32[320,128]{1,0:T(8,128)} all-gather(f32[80,128]{1,0:T(8,128)S(1)} %add_add_fusion), channel_id=2, replica_groups=mesh['x'=4,'z'=8,'y'=2,'near'=2,'core'=2] {'near','core'}, dimensions={0}, use_global_device_ids=true | all-gather | bytes 204800 | tf_op jit(solution)/shard_map/scatter/all_gather | solution.py:348
  168.9 1.8 %last.1 = (bf16[1,256,128]{2,1,0:T(8,128)(2,1)}, f32[128,256]{1,0:T(8,128)}, f32[1,256]{1,0:T(1,128)}) custom-call(f32[2,128,128]{2,1,0:T(8,128)} %bitcast.58, bf16[2,128,128]{2,1,0:T(8,128)(2,1)} %copy-done.7, f32[4,80,128]{2,1,0:T(8,128)} %bitcast.57), custom_call_target="tpu_custom_call" | custom-call | tf_op jit(solution)/shard_map/last/pallas_call | solution.py:227
  (92 shorter events, 15.0 us)
Async XLA Ops:
  0.6 5.7 %collective-permute-start.3 = (bf16[2,128,128]{2,1,0:T(8,128)(2,1)}, bf16[2,128,128]{2,1,0:T(8,128)(2,1)S(1)}, u32[]{:S(2)}, u32[]{:S(2)}) collective-permute-start(bf16[2,128,128]{2,1,0:T(8,128)(2,1)} %bitcast.61), channel_id=1, source_target_pairs={{0,4},{4,0},{1,5},{5,1},{2,6},{6,2},{3,7},{7,3},{8,12},{12,8},{9,1... | collective-permute-start | bytes 196616 | tf_op jit(solution)/shard_map/gather/ppermute | solution.py:30
  7.2 71.8 %copy-start.2 = (bf16[256,256]{1,0:T(8,128)(2,1)S(1)}, bf16[256,256]{1,0:T(8,128)(2,1)}, u32[]{:S(2)}) copy-start(bf16[256,256]{1,0:T(8,128)(2,1)} %cot_ref.1) | copy-start | bytes 393220
  7.2 71.8 %copy-start.6 = (f32[256]{0:T(256)S(1)}, f32[256]{0:T(256)}, u32[]{:S(2)}) copy-start(f32[256]{0:T(256)} %param.9) | copy-start | bytes 3076
  7.3 29.8 %all-to-all-start = ((bf16[16,128,128]{2,1,0:T(8,128)(2,1)}), bf16[16,128,128]{2,1,0:T(8,128)(2,1)S(1)}, u32[]{:S(2)}, u32[]{:S(2)}) async-start(bf16[16,128,128]{2,1,0:T(8,128)(2,1)} %bitcast.3), calls=%async_computation | async-start | bytes 1048576 | tf_op jit(solution)/shard_map/gather/all_to_all | solution.py:244
  15.6 4.8 %collective-permute-start = (bf16[2,128,128]{2,1,0:T(8,128)(2,1)}, bf16[2,128,128]{2,1,0:T(8,128)(2,1)S(1)}, u32[]{:S(2)}, u32[]{:S(2)}) collective-permute-start(bf16[2,128,128]{2,1,0:T(8,128)(2,1)} %bitcast.62), channel_id=1, source_target_pairs={{0,64},{64,128},{128,192},{192,0},{1,65},{65,129},{129,193},{193,1... | collective-permute-start | bytes 196616 | tf_op jit(solution)/shard_map/gather/ppermute | solution.py:21
  16.8 5.0 %collective-permute-start.1 = (bf16[2,128,128]{2,1,0:T(8,128)(2,1)}, bf16[2,128,128]{2,1,0:T(8,128)(2,1)S(1)}, u32[]{:S(2)}, u32[]{:S(2)}) collective-permute-start(bf16[2,128,128]{2,1,0:T(8,128)(2,1)} %bitcast.63), channel_id=1, source_target_pairs={{0,128},{64,192},{128,0},{192,64},{1,129},{65,193},{129,1},{193,65... | collective-permute-start | bytes 196616 | tf_op jit(solution)/shard_map/gather/ppermute | solution.py:21
  19.3 3.6 %collective-permute-start.2 = (bf16[2,128,128]{2,1,0:T(8,128)(2,1)}, bf16[2,128,128]{2,1,0:T(8,128)(2,1)S(1)}, u32[]{:S(2)}, u32[]{:S(2)}) collective-permute-start(bf16[2,128,128]{2,1,0:T(8,128)(2,1)} %bitcast.64), channel_id=1, source_target_pairs={{0,192},{64,0},{128,64},{192,128},{1,193},{65,1},{129,65},{193,129... | collective-permute-start | bytes 196616 | tf_op jit(solution)/shard_map/gather/ppermute | solution.py:21
  23.8 68.5 %copy-start.5 = (s32[8,1]{0,1:T(1,128)S(1)}, s32[8,1]{0,1:T(1,128)}, u32[]{:S(2)}) copy-start(s32[8,1]{0,1:T(1,128)} %param.12) | copy-start | bytes 100
  23.8 10.5 %collective-permute-start.7 = (bf16[8,128,128]{2,1,0:T(8,128)(2,1)S(1)}, bf16[8,128,128]{2,1,0:T(8,128)(2,1)S(1)}, u32[]{:S(2)}, u32[]{:S(2)}) collective-permute-start(bf16[8,128,128]{2,1,0:T(8,128)(2,1)S(1)} %pad_maximum_fusion.5.rest_0_), channel_id=1, source_target_pairs={{0,8},{8,16},{16,24},{24,32},{32,40},{40,48},{48,56},{56,0},{1,9},... | collective-permute-start | bytes 786440 | tf_op jit(solution)/shard_map/gather/ppermute | solution.py:25
  25.3 9.0 %collective-permute-start.8 = (bf16[8,128,128]{2,1,0:T(8,128)(2,1)S(1)}, bf16[8,128,128]{2,1,0:T(8,128)(2,1)S(1)}, u32[]{:S(2)}, u32[]{:S(2)}) collective-permute-start(bf16[8,128,128]{2,1,0:T(8,128)(2,1)S(1)} %pad_maximum_fusion.5.rest_0_), channel_id=1, source_target_pairs={{0,56},{8,0},{16,8},{24,16},{32,24},{40,32},{48,40},{56,48},{1,57}... | collective-permute-start | bytes 786440 | tf_op jit(solution)/shard_map/gather/ppermute | solution.py:25
  34.3 8.7 %collective-permute-start.9 = (bf16[8,128,128]{2,1,0:T(8,128)(2,1)S(1)}, bf16[8,128,128]{2,1,0:T(8,128)(2,1)}, u32[]{:S(2)}, u32[]{:S(2)}) collective-permute-start(bf16[8,128,128]{2,1,0:T(8,128)(2,1)S(1)} %collective-permute-done.7.rest_5_), channel_id=1, source_target_pairs={{0,8},{8,16},{16,24},{24,32},{32,40},{40,48},{48,56},{56,0},{1,9},... | collective-permute-start | bytes 786440 | tf_op jit(solution)/shard_map/gather/ppermute | solution.py:25
  34.3 8.7 %collective-permute-start.10 = (bf16[8,128,128]{2,1,0:T(8,128)(2,1)S(1)}, bf16[8,128,128]{2,1,0:T(8,128)(2,1)}, u32[]{:S(2)}, u32[]{:S(2)}) collective-permute-start(bf16[8,128,128]{2,1,0:T(8,128)(2,1)S(1)} %collective-permute-done.8.rest_6_), channel_id=1, source_target_pairs={{0,56},{8,0},{16,8},{24,16},{32,24},{40,32},{48,40},{56,48},{1,57}... | collective-permute-start | bytes 786440 | tf_op jit(solution)/shard_map/gather/ppermute | solution.py:25
  37.0 18.1 %collective-permute-start.4 = (bf16[16,128,128]{2,1,0:T(8,128)(2,1)S(1)}, bf16[16,128,128]{2,1,0:T(8,128)(2,1)S(1)}, u32[]{:S(2)}, u32[]{:S(2)}) collective-permute-start(bf16[16,128,128]{2,1,0:T(8,128)(2,1)S(1)} %all-to-all-done.rest_1_), channel_id=1, source_target_pairs={{0,64},{64,128},{128,192},{192,0},{1,65},{65,129},{129,193},{193,1... | collective-permute-start | bytes 1572872 | tf_op jit(solution)/shard_map/gather/ppermute | solution.py:21
  39.0 22.2 %collective-permute-start.5 = (bf16[16,128,128]{2,1,0:T(8,128)(2,1)S(1)}, bf16[16,128,128]{2,1,0:T(8,128)(2,1)S(1)}, u32[]{:S(2)}, u32[]{:S(2)}) collective-permute-start(bf16[16,128,128]{2,1,0:T(8,128)(2,1)S(1)} %all-to-all-done.rest_1_), channel_id=1, source_target_pairs={{0,128},{64,192},{128,0},{192,64},{1,129},{65,193},{129,1},{193,65... | collective-permute-start | bytes 1572872 | tf_op jit(solution)/shard_map/gather/ppermute | solution.py:21
  41.0 22.3 %collective-permute-start.6 = (bf16[16,128,128]{2,1,0:T(8,128)(2,1)S(1)}, bf16[16,128,128]{2,1,0:T(8,128)(2,1)S(1)}, u32[]{:S(2)}, u32[]{:S(2)}) collective-permute-start(bf16[16,128,128]{2,1,0:T(8,128)(2,1)S(1)} %all-to-all-done.rest_1_), channel_id=1, source_target_pairs={{0,192},{64,0},{128,64},{192,128},{1,193},{65,1},{129,65},{193,129... | collective-permute-start | bytes 1572872 | tf_op jit(solution)/shard_map/gather/ppermute | solution.py:21
  43.0 6.9 %collective-permute-start.11 = (bf16[8,128,128]{2,1,0:T(8,128)(2,1)}, bf16[8,128,128]{2,1,0:T(8,128)(2,1)S(1)}, u32[]{:S(2)}, u32[]{:S(2)}) collective-permute-start(bf16[8,128,128]{2,1,0:T(8,128)(2,1)} %collective-permute-done.9.rest_7_), channel_id=1, source_target_pairs={{0,8},{8,16},{16,24},{24,32},{32,40},{40,48},{48,56},{56,0},{1,9},... | collective-permute-start | bytes 786440 | tf_op jit(solution)/shard_map/gather/ppermute | solution.py:25
  43.0 7.0 %collective-permute-start.12 = (bf16[8,128,128]{2,1,0:T(8,128)(2,1)}, bf16[8,128,128]{2,1,0:T(8,128)(2,1)S(1)}, u32[]{:S(2)}, u32[]{:S(2)}) collective-permute-start(bf16[8,128,128]{2,1,0:T(8,128)(2,1)} %collective-permute-done.10.rest_8_), channel_id=1, source_target_pairs={{0,56},{8,0},{16,8},{24,16},{32,24},{40,32},{48,40},{56,48},{1,57}... | collective-permute-start | bytes 786440 | tf_op jit(solution)/shard_map/gather/ppermute | solution.py:25
  47.6 31.4 %copy-start.3 = (bf16[128,256]{1,0:T(8,128)(2,1)S(1)}, bf16[128,256]{1,0:T(8,128)(2,1)}, u32[]{:S(2)}) copy-start(bf16[128,256]{1,0:T(8,128)(2,1)} %weight_ref.1) | copy-start | bytes 196612
  50.0 5.1 %collective-permute-start.13 = (bf16[4,128,128]{2,1,0:T(8,128)(2,1)S(1)}, bf16[4,128,128]{2,1,0:T(8,128)(2,1)S(1)}, u32[]{:S(2)}, u32[]{:S(2)}) collective-permute-start(bf16[4,128,128]{2,1,0:T(8,128)(2,1)S(1)} %slice.258), channel_id=1, source_target_pairs={{0,8},{8,16},{16,24},{24,32},{32,40},{40,48},{48,56},{56,0},{1,9},... | collective-permute-start | bytes 393224 | tf_op jit(solution)/shard_map/gather/ppermute | solution.py:25
  50.1 5.0 %collective-permute-start.14 = (bf16[4,128,128]{2,1,0:T(8,128)(2,1)S(1)}, bf16[4,128,128]{2,1,0:T(8,128)(2,1)S(1)}, u32[]{:S(2)}, u32[]{:S(2)}) collective-permute-start(bf16[4,128,128]{2,1,0:T(8,128)(2,1)S(1)} %slice.259), channel_id=1, source_target_pairs={{0,56},{8,0},{16,8},{24,16},{32,24},{40,32},{48,40},{56,48},{1,57}... | collective-permute-start | bytes 393224 | tf_op jit(solution)/shard_map/gather/ppermute | solution.py:25
  63.2 2.8 %copy-start = (bf16[8,1,24,128,128]{4,3,2,1,0:T(8,128)(2,1)S(1)}, bf16[8,1,24,128,128]{4,3,2,1,0:T(8,128)(2,1)}, u32[]{:S(2)}) copy-start(bf16[8,1,24,128,128]{4,3,2,1,0:T(8,128)(2,1)} %edges.3) | copy-start | bytes 18874372
  66.0 0.7 copy-start.4
  66.7 25.6 %copy-start.1 = (bf16[8,1,24,128,128]{4,3,2,1,0:T(8,128)(2,1)S(1)}, bf16[8,1,24,128,128]{4,3,2,1,0:T(8,128)(2,1)}, u32[]{:S(2)}) copy-start(bf16[8,1,24,128,128]{4,3,2,1,0:T(8,128)(2,1)} %edges.3) | copy-start | bytes 18874372
  71.6 3.8 %collective-permute-start.15 = (bf16[2,128,128]{2,1,0:T(8,128)(2,1)S(1)}, bf16[2,128,128]{2,1,0:T(8,128)(2,1)S(1)}, u32[]{:S(2)}, u32[]{:S(2)}) collective-permute-start(bf16[2,128,128]{2,1,0:T(8,128)(2,1)S(1)} %get-tuple-element.37), channel_id=1, source_target_pairs={{0,1},{1,0},{2,3},{3,2},{4,5},{5,4},{6,7},{7,6},{8,9},{9,8},{10,11... | collective-permute-start | bytes 196616 | tf_op jit(solution)/shard_map/sections/ppermute | solution.py:30
  73.7 3.7 %collective-permute-start.16 = (bf16[2,128,128]{2,1,0:T(8,128)(2,1)S(1)}, bf16[2,128,128]{2,1,0:T(8,128)(2,1)S(1)}, u32[]{:S(2)}, u32[]{:S(2)}) collective-permute-start(bf16[2,128,128]{2,1,0:T(8,128)(2,1)S(1)} %get-tuple-element.38), channel_id=1, source_target_pairs={{0,2},{2,0},{1,3},{3,1},{4,6},{6,4},{5,7},{7,5},{8,10},{10,8},{9,1... | collective-permute-start | bytes 196616 | tf_op jit(solution)/shard_map/sections/ppermute | solution.py:30
  75.0 4.1 %collective-permute-start.17 = (bf16[2,128,128]{2,1,0:T(8,128)(2,1)S(1)}, bf16[2,128,128]{2,1,0:T(8,128)(2,1)S(1)}, u32[]{:S(2)}, u32[]{:S(2)}) collective-permute-start(bf16[2,128,128]{2,1,0:T(8,128)(2,1)S(1)} %get-tuple-element.39), channel_id=1, source_target_pairs={{0,3},{1,2},{2,1},{3,0},{4,7},{5,6},{6,5},{7,4},{8,11},{9,10},{10,... | collective-permute-start | bytes 196616 | tf_op jit(solution)/shard_map/sections/ppermute | solution.py:30
  80.7 1.3 collective-permute-start.18
  82.0 10.2 %collective-permute-start.19 = (f32[80,128]{1,0:T(8,128)S(1)}, f32[80,128]{1,0:T(8,128)S(1)}, u32[]{:S(2)}, u32[]{:S(2)}) collective-permute-start(f32[80,128]{1,0:T(8,128)S(1)} %get-tuple-element.47), channel_id=1, source_target_pairs={{0,2},{2,0},{1,3},{3,1},{4,6},{6,4},{5,7},{7,5},{8,10},{10,8},{9,1... | collective-permute-start | bytes 122888 | tf_op jit(solution)/shard_map/weights/ppermute | solution.py:30
  83.2 9.0 %collective-permute-start.21 = (f32[80,128]{1,0:T(8,128)S(1)}, f32[80,128]{1,0:T(8,128)S(1)}, u32[]{:S(2)}, u32[]{:S(2)}) collective-permute-start(f32[80,128]{1,0:T(8,128)S(1)} %get-tuple-element.47), channel_id=1, source_target_pairs={{0,6},{2,4},{4,2},{6,0},{1,7},{3,5},{5,3},{7,1},{8,14},{10,12},{12... | collective-permute-start | bytes 122888 | tf_op jit(solution)/shard_map/weights/ppermute | solution.py:30
  85.3 7.0 %collective-permute-start.20 = (f32[80,128]{1,0:T(8,128)S(1)}, f32[80,128]{1,0:T(8,128)S(1)}, u32[]{:S(2)}, u32[]{:S(2)}) collective-permute-start(f32[80,128]{1,0:T(8,128)S(1)} %get-tuple-element.46), channel_id=1, source_target_pairs={{0,4},{4,0},{1,5},{5,1},{2,6},{6,2},{3,7},{7,3},{8,12},{12,8},{9,1... | collective-permute-start | bytes 122888 | tf_op jit(solution)/shard_map/weights/ppermute | solution.py:30
  97.5 25.9 %collective-permute-start.24 = (bf16[2048,128]{1,0:T(8,128)(2,1)S(1)}, bf16[2048,128]{1,0:T(8,128)(2,1)S(1)}, u32[]{:S(2)}, u32[]{:S(2)}) collective-permute-start(bf16[2048,128]{1,0:T(8,128)(2,1)S(1)} %bitcast.56), channel_id=1, source_target_pairs={{0,64},{64,128},{128,192},{192,0},{1,65},{65,129},{129,193},{193,1... | collective-permute-start | bytes 1572872 | tf_op jit(solution)/shard_map/scatter/ppermute | solution.py:21
  97.6 25.8 %collective-permute-start.25 = (bf16[2048,128]{1,0:T(8,128)(2,1)S(1)}, bf16[2048,128]{1,0:T(8,128)(2,1)S(1)}, u32[]{:S(2)}, u32[]{:S(2)}) collective-permute-start(bf16[2048,128]{1,0:T(8,128)(2,1)S(1)} %bitcast.55), channel_id=1, source_target_pairs={{0,128},{64,192},{128,0},{192,64},{1,129},{65,193},{129,1},{193,65... | collective-permute-start | bytes 1572872 | tf_op jit(solution)/shard_map/scatter/ppermute | solution.py:21
  99.2 24.4 %collective-permute-start.26 = (bf16[2048,128]{1,0:T(8,128)(2,1)S(1)}, bf16[2048,128]{1,0:T(8,128)(2,1)S(1)}, u32[]{:S(2)}, u32[]{:S(2)}) collective-permute-start(bf16[2048,128]{1,0:T(8,128)(2,1)S(1)} %bitcast.54), channel_id=1, source_target_pairs={{0,192},{64,0},{128,64},{192,128},{1,193},{65,1},{129,65},{193,129... | collective-permute-start | bytes 1572872 | tf_op jit(solution)/shard_map/scatter/ppermute | solution.py:21
  101.2 6.2 %collective-permute-start.22 = (bf16[672,128]{1,0:T(8,128)(2,1)S(1)}, bf16[672,128]{1,0:T(8,128)(2,1)S(1)}, u32[]{:S(2)}, u32[]{:S(2)}) collective-permute-start(bf16[672,128]{1,0:T(8,128)(2,1)S(1)} %get-tuple-element.87), channel_id=1, source_target_pairs={{0,8},{8,16},{16,24},{24,32},{32,40},{40,48},{48,56},{56,0},{1,9},... | collective-permute-start | bytes 516104 | tf_op jit(solution)/shard_map/scatter/ppermute | solution.py:25
  101.4 6.2 %collective-permute-start.29 = (bf16[672,128]{1,0:T(8,128)(2,1)S(1)}, bf16[672,128]{1,0:T(8,128)(2,1)S(1)}, u32[]{:S(2)}, u32[]{:S(2)}) collective-permute-start(bf16[672,128]{1,0:T(8,128)(2,1)S(1)} %get-tuple-element.88), channel_id=1, source_target_pairs={{0,56},{8,0},{16,8},{24,16},{32,24},{40,32},{48,40},{56,48},{1,57}... | collective-permute-start | bytes 516104 | tf_op jit(solution)/shard_map/scatter/ppermute | solution.py:25
  107.5 8.0 %collective-permute-start.23 = (bf16[1184,128]{1,0:T(8,128)(2,1)S(1)}, bf16[1184,128]{1,0:T(8,128)(2,1)S(1)}, u32[]{:S(2)}, u32[]{:S(2)}) collective-permute-start(bf16[1184,128]{1,0:T(8,128)(2,1)S(1)} %pad_maximum_fusion), channel_id=1, source_target_pairs={{0,8},{8,16},{16,24},{24,32},{32,40},{40,48},{48,56},{56,0},{1,9},... | collective-permute-start | bytes 909320 | tf_op jit(solution)/shard_map/scatter/ppermute | solution.py:25
  107.7 17.2 %collective-permute-start.30 = (bf16[1184,128]{1,0:T(8,128)(2,1)S(1)}, bf16[1184,128]{1,0:T(8,128)(2,1)S(1)}, u32[]{:S(2)}, u32[]{:S(2)}) collective-permute-start(bf16[1184,128]{1,0:T(8,128)(2,1)S(1)} %pad_maximum_fusion.3), channel_id=1, source_target_pairs={{0,56},{8,0},{16,8},{24,16},{32,24},{40,32},{48,40},{56,48},{1,57}... | collective-permute-start | bytes 909320 | tf_op jit(solution)/shard_map/scatter/ppermute | solution.py:25
  124.8 8.7 %collective-permute-start.27 = (bf16[1184,128]{1,0:T(8,128)(2,1)S(1)}, bf16[1184,128]{1,0:T(8,128)(2,1)S(1)}, u32[]{:S(2)}, u32[]{:S(2)}) collective-permute-start(bf16[1184,128]{1,0:T(8,128)(2,1)S(1)} %pad_maximum_fusion.1), channel_id=1, source_target_pairs={{0,8},{8,16},{16,24},{24,32},{32,40},{40,48},{48,56},{56,0},{1,9},... | collective-permute-start | bytes 909320 | tf_op jit(solution)/shard_map/scatter/ppermute | solution.py:25
  125.0 8.7 %collective-permute-start.31 = (bf16[1184,128]{1,0:T(8,128)(2,1)S(1)}, bf16[1184,128]{1,0:T(8,128)(2,1)S(1)}, u32[]{:S(2)}, u32[]{:S(2)}) collective-permute-start(bf16[1184,128]{1,0:T(8,128)(2,1)S(1)} %pad_maximum_fusion.4), channel_id=1, source_target_pairs={{0,56},{8,0},{16,8},{24,16},{32,24},{40,32},{48,40},{56,48},{1,57}... | collective-permute-start | bytes 909320 | tf_op jit(solution)/shard_map/scatter/ppermute | solution.py:25
  133.6 7.8 %collective-permute-start.28 = (bf16[1184,128]{1,0:T(8,128)(2,1)S(1)}, bf16[1184,128]{1,0:T(8,128)(2,1)S(1)}, u32[]{:S(2)}, u32[]{:S(2)}) collective-permute-start(bf16[1184,128]{1,0:T(8,128)(2,1)S(1)} %pad_maximum_fusion.2), channel_id=1, source_target_pairs={{0,8},{8,16},{16,24},{24,32},{32,40},{40,48},{48,56},{56,0},{1,9},... | collective-permute-start | bytes 909320 | tf_op jit(solution)/shard_map/scatter/ppermute | solution.py:25
  133.8 7.6 %collective-permute-start.32 = (bf16[1024,128]{1,0:T(8,128)(2,1)S(1)}, bf16[1024,128]{1,0:T(8,128)(2,1)S(1)}, u32[]{:S(2)}, u32[]{:S(2)}) collective-permute-start(bf16[1024,128]{1,0:T(8,128)(2,1)S(1)} %fusion.3), channel_id=1, source_target_pairs={{0,56},{8,0},{16,8},{24,16},{32,24},{40,32},{48,40},{56,48},{1,57}... | collective-permute-start | bytes 786440 | tf_op jit(solution)/shard_map/scatter/ppermute | solution.py:25
  136.5 18.9 %all-to-all-start.1 = ((bf16[16,128,128]{2,1,0:T(8,128)(2,1)}), bf16[16,128,128]{2,1,0:T(8,128)(2,1)S(1)}, u32[]{:S(2)}, u32[]{:S(2)}) async-start(bf16[16,128,128]{2,1,0:T(8,128)(2,1)} %bitcast.23), calls=%async_computation.1 | async-start | bytes 1048576 | tf_op jit(solution)/shard_map/scatter/all_to_all | solution.py:299
  141.6 7.1 %collective-permute-start.33 = (bf16[416,128]{1,0:T(8,128)(2,1)S(1)}, bf16[416,128]{1,0:T(8,128)(2,1)S(1)}, u32[]{:S(2)}, u32[]{:S(2)}) collective-permute-start(bf16[416,128]{1,0:T(8,128)(2,1)S(1)} %get-tuple-element.84), channel_id=1, source_target_pairs={{0,64},{64,128},{128,192},{192,0},{1,65},{65,129},{129,193},{193,1... | collective-permute-start | bytes 319496 | tf_op jit(solution)/shard_map/scatter/ppermute | solution.py:21
  145.2 6.1 %collective-permute-start.34 = (bf16[416,128]{1,0:T(8,128)(2,1)S(1)}, bf16[416,128]{1,0:T(8,128)(2,1)S(1)}, u32[]{:S(2)}, u32[]{:S(2)}) collective-permute-start(bf16[416,128]{1,0:T(8,128)(2,1)S(1)} %get-tuple-element.85), channel_id=1, source_target_pairs={{0,128},{64,192},{128,0},{192,64},{1,129},{65,193},{129,1},{193,65... | collective-permute-start | bytes 319496 | tf_op jit(solution)/shard_map/scatter/ppermute | solution.py:21
  147.8 3.9 %collective-permute-start.35 = (bf16[416,128]{1,0:T(8,128)(2,1)S(1)}, bf16[416,128]{1,0:T(8,128)(2,1)S(1)}, u32[]{:S(2)}, u32[]{:S(2)}) collective-permute-start(bf16[416,128]{1,0:T(8,128)(2,1)S(1)} %get-tuple-element.86), channel_id=1, source_target_pairs={{0,192},{64,0},{128,64},{192,128},{1,193},{65,1},{129,65},{193,129... | collective-permute-start | bytes 319496 | tf_op jit(solution)/shard_map/scatter/ppermute | solution.py:21
  155.5 12.7 %collective-permute-start.36 = (bf16[2,128,128]{2,1,0:T(8,128)(2,1)S(1)}, bf16[2,128,128]{2,1,0:T(8,128)(2,1)S(1)}, u32[]{:S(2)}, u32[]{:S(2)}) collective-permute-start(bf16[2,128,128]{2,1,0:T(8,128)(2,1)S(1)} %add_convert_fusion), channel_id=1, source_target_pairs={{0,4},{4,0},{1,5},{5,1},{2,6},{6,2},{3,7},{7,3},{8,12},{12,8},{9,1... | collective-permute-start | bytes 196616 | tf_op jit(solution)/shard_map/scatter/ppermute | solution.py:30
  168.3 0.6 copy-start.7

commit v2 on v1

v2 whole, which is shorter than its diff:
```python
import functools

import jax
import jax.numpy as jnp
from jax import lax
from jax.experimental import pallas as pl
from jax.experimental.pallas import tpu as pltpu
from jax.sharding import Mesh
from jax.sharding import PartitionSpec as P

NX, NZ, NY = 4, 8, 2
TILE = 128
GROUP = 6
BF = jnp.bfloat16
F32 = jnp.float32
VMEM = pltpu.VMEM
SMEM = pltpu.SMEM


def shift_x(value, k):
    return lax.ppermute(value, "x", [(i, (i + k) % NX) for i in range(NX)])


def shift_z(value, k):
    return lax.ppermute(value, "z", [(i, (i + k) % NZ) for i in range(NZ)])


def swap(value, *axes):
    pairs = [(i, (1 << len(axes)) - 1 - i) for i in range(1 << len(axes))]
    return lax.ppermute(value, axes, pairs)


def add32(*values):
    total = values[0].astype(F32)
    for value in values[1:]:
        total = total + value.astype(F32)
    return total


def add(*values):
    return add32(*values).astype(BF)


def each_row(meta_ref, edges, body):
    rows, _, slots = edges.shape[:3]

    def row(t, carry):
        count = meta_ref[t]

        @pl.when(count > GROUP)
        def _():
            body(t, count, slots)

        @pl.when(count <= GROUP)
        def _():
            body(t, count, GROUP)

        return carry

    lax.fori_loop(0, rows, row, 0)


def live_tile(edges, t, s, count):
    tile = edges[t, 0, s]
    return jnp.where(s < count, tile, jnp.zeros_like(tile))


def forward_kernel(places, rep_ref, meta_ref, edges, *rest):
    pieces = rest[: len(places)]
    outs, table = rest[len(places):-1], rest[-1]
    rows, _, slots = edges.shape[:3]
    for piece, (place, size) in zip(pieces, places):

        def copy(i, carry, piece=piece, place=place):
            table[pl.ds(place + i * 4, 4)] = piece[pl.ds(i * 4, 4)]
            return carry

        lax.fori_loop(0, size // 4, copy, 0)

    def body(t, count, size):
        left = [live_tile(edges, t, s, count) for s in range(size)]
        right = [table[meta_ref[rows + t * slots + s]] for s in range(size)]
        total = jnp.dot(
            jnp.concatenate(left, axis=1), jnp.concatenate(right, axis=0), preferred_element_type=F32
        ).astype(BF)
        for q in range(len(outs)):

            @pl.when((t // 2) ^ rep_ref[0] == q)
            def _(q=q):
                outs[q][t % 2] = total

    each_row(meta_ref, edges, body)


def forward(rep, meta, edges, pieces):
    places = tuple((place, piece.shape[0]) for place, piece in pieces)
    arrays = [piece for _, piece in pieces]
    rows, _, slots = edges.shape[:3]
    vmem = pl.BlockSpec(memory_space=VMEM)
    return pl.pallas_call(
        functools.partial(forward_kernel, places),
        out_shape=(jax.ShapeDtypeStruct((2, TILE, TILE), BF),) * 4,
        in_specs=[pl.BlockSpec(memory_space=SMEM)] * 2 + [vmem] * (1 + len(arrays)),
        out_specs=(vmem,) * 4,
        scratch_shapes=[VMEM((2 * NX * NZ * NY, TILE, TILE), BF)],
        compiler_params=pltpu.CompilerParams(vmem_limit_bytes=24 * 2**20),
        cost_estimate=pl.CostEstimate(flops=2 * rows * slots * TILE**3, bytes_accessed=11 * 2**20, transcendentals=0),
        name="forward",
    )(rep, meta, edges, *arrays)


def middle_kernel(rep_ref, p0, p1, p2, p3, weight_ref, bias_ref, cot_ref, hidden_ref, slope_ref, mine_ref, theirs_ref):
    agg = add32(*[jnp.concatenate([p[0], p[1]], axis=0) for p in (p0, p1, p2, p3)])
    weight = weight_ref[...]
    preact = (
        jnp.dot(agg, weight.astype(F32), preferred_element_type=F32, precision=lax.Precision.HIGHEST)
        + bias_ref[...]
    )
    gate = jax.nn.sigmoid(preact)
    hidden_ref[...] = (preact * gate).astype(BF)
    outgrad = (cot_ref[...].astype(F32) * gate * (1.0 + preact * (1.0 - gate))).astype(BF)
    slope = lax.dot_general(weight, outgrad, (((1,), (1,)), ((), ())), preferred_element_type=F32).astype(BF)
    for i in range(slope_ref.shape[0]):
        slope_ref[i] = slope[:, i * TILE:(i + 1) * TILE]
    wide = outgrad.astype(F32)
    grad = lax.dot_general(
        agg, wide, (((0,), (0,)), ((), ())), preferred_element_type=F32, precision=lax.Precision.HIGHEST
    )
    bias = jnp.sum(wide, axis=0, keepdims=True)
    for ref, same in ((mine_ref, True), (theirs_ref, False)):
        for half in range(2):

            @pl.when(((rep_ref[0] % 2) == half) == same)
            def _(ref=ref, half=half):
                ref[0:64, :] = grad[half * 64:(half + 1) * 64, 0:TILE]
                ref[64:128, :] = grad[half * 64:(half + 1) * 64, TILE:]

        ref[128:144, :] = jnp.broadcast_to(bias[:, 0:TILE], (16, TILE))
        ref[144:160, :] = jnp.broadcast_to(bias[:, TILE:], (16, TILE))


def middle(rep, parts, weight, bias, cotangent):
    nodes, width = cotangent.shape
    vmem = pl.BlockSpec(memory_space=VMEM)
    half = jax.ShapeDtypeStruct((160, TILE), F32)
    return pl.pallas_call(
        middle_kernel,
        out_shape=(
            jax.ShapeDtypeStruct((nodes, width), BF),
            jax.ShapeDtypeStruct((nodes // TILE, TILE, TILE), BF),
            half,
            half,
        ),
        in_specs=[pl.BlockSpec(memory_space=SMEM)] + [vmem] * 7,
        out_specs=(vmem,) * 4,
        compiler_params=pltpu.CompilerParams(vmem_limit_bytes=32 * 2**20),
        name="middle",
    )(rep, *parts, weight, bias.reshape(1, -1), cotangent)


def backward_kernel(places, rep_ref, meta_ref, edges, s0, s1, s2, s3, *rest):
    outs, totals, slope_ref = rest[:-2], rest[-2], rest[-1]
    for q, part in enumerate((s0, s1, s2, s3)):
        for i in range(2):
            slope_ref[(rep_ref[0] ^ q) * 2 + i] = part[i]
    rows, _, slots = edges.shape[:3]

    def clear(i, carry):
        totals[pl.ds(i * 8, 8)] = jnp.zeros((8, TILE, TILE), F32)
        return carry

    lax.fori_loop(0, totals.shape[0] // 8, clear, 0)

    def body(t, count, size):
        slope = slope_ref[t]
        for g in range(size // GROUP):
            which = range(g * GROUP, (g + 1) * GROUP)
            tiles = [live_tile(edges, t, s, count) for s in which]
            terms = jnp.dot(slope, jnp.concatenate(tiles, axis=1), preferred_element_type=F32)
            where = [meta_ref[rows + t * slots + s] for s in which]
            old = [totals[w] for w in where]
            for i, w in enumerate(where):
                totals[w] = old[i] + terms[:, i * TILE:(i + 1) * TILE]

    each_row(meta_ref, edges, body)

    for out, segments in zip(outs, places):
        offset = 0
        for place, size in segments:

            def store(i, carry, out=out, place=place, offset=offset):
                out[pl.ds(offset + i * 4, 4)] = totals[pl.ds(place + i * 4, 4)].astype(out.dtype)
                return carry

            lax.fori_loop(0, size // 4, store, 0)
            offset += size


def backward(rep, meta, edges, slopes, places):
    rows, _, slots = edges.shape[:3]
    vmem = pl.BlockSpec(memory_space=VMEM)
    return pl.pallas_call(
        functools.partial(backward_kernel, places),
        out_shape=tuple(
            jax.ShapeDtypeStruct((sum(size for _, size in segments), TILE, TILE), BF) for segments in places
        ),
        in_specs=[pl.BlockSpec(memory_space=SMEM)] * 2 + [vmem] * 5,
        out_specs=(vmem,) * len(places),
        scratch_shapes=[VMEM((2 * NX * NZ * NY, TILE, TILE), F32), VMEM((rows, TILE, TILE), BF)],
        compiler_params=pltpu.CompilerParams(vmem_limit_bytes=28 * 2**20),
        cost_estimate=pl.CostEstimate(flops=2 * rows * slots * TILE**3, bytes_accessed=15 * 2**20, transcendentals=0),
        name="backward",
    )(rep, meta, edges, *slopes)


def last_kernel(rep_ref, total_ref, mine_ref, theirs_ref, feature_ref, weight_ref, bias_ref):
    for i in range(2):
        feature_ref[0, i * TILE:(i + 1) * TILE, :] = total_ref[i].T.astype(BF)
    for ref, same in ((mine_ref, True), (theirs_ref, False)):
        for half in range(2):

            @pl.when(((rep_ref[0] % 2) == half) == same)
            def _(ref=ref, half=half):
                weight_ref[half * 64:(half + 1) * 64, 0:TILE] = ref[0:64, :]
                weight_ref[half * 64:(half + 1) * 64, TILE:] = ref[64:128, :]
                if half == 0:
                    bias_ref[:, 0:TILE] = ref[128:129, :]
                    bias_ref[:, TILE:] = ref[144:145, :]


def last(rep, total, mine, theirs):
    vmem = pl.BlockSpec(memory_space=VMEM)
    return pl.pallas_call(
        last_kernel,
        out_shape=(
            jax.ShapeDtypeStruct((1, 2 * TILE, TILE), BF),
            jax.ShapeDtypeStruct((TILE, 2 * TILE), F32),
            jax.ShapeDtypeStruct((1, 2 * TILE), F32),
        ),
        in_specs=[pl.BlockSpec(memory_space=SMEM)] + [vmem] * 3,
        out_specs=(vmem, vmem, vmem),
        name="last",
    )(rep, total, mine, theirs)


def gather_features(own):
    own, other = lax.optimization_barrier((own, swap(own, "y")))
    plane = jnp.concatenate([own, shift_x(own, 1), shift_x(own, 2), shift_x(own, -1)])
    spread = jnp.broadcast_to(other[None], (NZ,) + other.shape).reshape(2 * NZ, TILE, TILE)
    line = lax.all_to_all(spread, "z", 0, 0, tiled=True)
    pieces = [(0, plane), (64, line)]
    ahead, behind = shift_x(line, 1), shift_x(line, -1)
    up = down = plane
    for k in (1, 2, 3):
        up, down = shift_z(up, 1), shift_z(down, -1)
        pieces += [(8 * k, up), (8 * (8 - k), down)]
        if k == 2:
            up, ahead, behind = lax.optimization_barrier((up, ahead, behind))
    pieces += [(80, ahead), (112, behind), (96, shift_x(ahead[:8], 1)), (104, shift_x(behind[8:], -1))]
    pieces += [(32, shift_z(up[:4], 1)), (36, shift_z(down[4:], -1))]
    return pieces


OWN_PLACES = tuple(((8 * k, 8),) for k in (4, 3, 5, 2, 6, 1, 7, 0))
OTHER_PLACES = tuple(tuple((64 + 8 * k, 8) for k in ks) for ks in ((4,), (3, 5), (2, 6), (1, 7), (0,)))


def scatter_totals(parts, grad):
    rows = [p.reshape(-1, TILE) for p in parts]
    own, other = rows[:8], rows[8:]
    half, full = 4 * TILE, 8 * TILE
    first = swap(jnp.concatenate([other[0], grad.astype(BF)]), "y")
    wide = add(grad, first[full:])
    last = add(own[0], first[:full])
    up, down = last[:half], last[half:]
    ride_up = ride_down = wide
    grads = [wide]
    for step in range(4):
        moved_up = shift_z(jnp.concatenate([up, ride_up]), 1)
        moved_down = shift_z(down if step == 3 else jnp.concatenate([down, ride_down]), -1)
        met = swap(other[step + 1], "y")
        up, down, met = lax.optimization_barrier((moved_up, moved_down, met))
        size = half if step == 0 else full
        ride_up, ride_down = up[size:], down[size:]
        grads.append(ride_up)
        if step < 3:
            grads.append(ride_down)
        up, down = up[:size], down[:size]
        if step == 3:
            total = add32(own[7], met, up, down)
            break
        here_up, here_down = add32(own[2 * step + 1], met[:full]), add32(own[2 * step + 2], met[full:])
        if step == 0:
            up = jnp.concatenate([add(here_up[:half], up), here_up[half:].astype(BF)])
            down = jnp.concatenate([here_down[:half].astype(BF), add(here_down[half:], down)])
        else:
            up, down = add(here_up, up), add(here_down, down)
    wide = add(*grads)
    part = 2 * TILE
    sent = [total[k * part:(k + 1) * part].astype(BF) for k in (1, 2, 3)]
    got = [shift_x(jnp.concatenate([v, wide]), hop) for v, hop in zip(sent, (1, 2, -1))]
    total = add32(total[:part], *[g[:part] for g in got])
    grad = add32(wide, *[g[part:] for g in got])
    return total.reshape(2, TILE, TILE), grad


def shards(features, weight, bias_vector, edge_tiles, tile_columns, live_counts, cotangent):
    x, z, y = lax.axis_index("x"), lax.axis_index("z"), lax.axis_index("y")
    rep = (lax.axis_index("near") * 2 + lax.axis_index("core")).reshape(1)
    columns = tile_columns.reshape(-1)
    owner, which = columns // 2, columns % 2
    ox, oz, oy = owner // (NZ * NY), (owner // NY) % NZ, owner % NY

    def places(dx, dz, elsewhere):
        return (jnp.where(oy == y, dz * NX + dx, 32 + elsewhere) * 2 + which).astype(jnp.int32)

    counts = live_counts.reshape(-1)
    behind = jnp.concatenate([counts, places((x - ox) % NX, (z - oz) % NZ, (x - ox) % NX * NZ + oz)])
    ahead = jnp.concatenate([counts, places((ox - x) % NX, (oz - z) % NZ, (oz - z) % NZ * NX + (ox - x) % NX)])

    with jax.named_scope("gather"):
        pieces = gather_features(features.reshape(2, TILE, TILE))
    partial = forward(rep, behind, edge_tiles, pieces)
    with jax.named_scope("sections"):
        parts = [
            partial[0],
            swap(partial[1], "core"),
            swap(partial[2], "near"),
            swap(partial[3], "near", "core"),
        ]
    hidden_out, slope, mine, theirs = middle(rep, parts, weight, bias_vector, cotangent)
    with jax.named_scope("slopes"):
        slopes = [slope, swap(slope, "core"), swap(slope, "near"), swap(slope, "near", "core")]
    with jax.named_scope("weights"):
        mine = mine + swap(theirs, "core")
        grad = mine + swap(mine, "near")
    totals = backward(rep, ahead, edge_tiles, slopes, OWN_PLACES + OTHER_PLACES)
    with jax.named_scope("scatter"):
        total, grad = scatter_totals(totals, grad)
        halves = [grad, swap(grad, "core")]
    feature_grad, weight_grad, bias_grad = last(rep, total, *halves)
    return hidden_out, feature_grad, weight_grad, bias_grad.reshape(-1)


def solution(mesh):
    grid = Mesh(mesh.devices.reshape(NX, NZ, NY, 2, 2), ("x", "z", "y", "near", "core"))
    row, rep = ("x", "z", "y"), ("near", "core")
    in_specs = (
        P(rep, row, None),
        P(),
        P(),
        P(row, rep, None, None, None),
        P(row, rep, None),
        P(row, rep),
        P(row + rep, None),
    )
    out_specs = (P(row + rep, None), P(rep, row, None), P(), P())
    return jax.shard_map(shards, mesh=grid, in_specs=in_specs, out_specs=out_specs, check_vma=False)
```

time: 171 us -> 165 us (0.965)
  blocking collectives: 16.2 us -> 0 us
  local copies, waits for them, and re-layouts: 5.68 us -> 14 us
    ppermute x9 -> x15, waiting for transfers between devices: 6.45 us -> 38 us  [swap(): return lax.ppermute(value, axes, pairs)]
    ppermute x16, waiting for transfers between devices: 26.7 us -> 6.12 us  [shift_z(): return lax.ppermute(value, 'z', [(i, (i + k) % NZ) for i in range(NZ)])]
    ppermute x9 -> x15, starting transfers between devices: 14.7 us -> 33.4 us  [swap(): return lax.ppermute(value, axes, pairs)]
    all_gather x2 -> x0, blocking collectives: 16.2 us -> none  [the longest x1 9.86 us: shards(): quarters = lax.all_gather(grad, ('near', 'core'), axis=0)]
    ppermute x12 -> x10, starting transfers between devices: 20.7 us -> 10.6 us  [shift_x(): return lax.ppermute(value, 'x', [(i, (i + k) % NX) for i in range(NX)])]
    ppermute x12 -> x10, waiting for transfers between devices: 22.5 us -> 12.4 us  [shift_x(): return lax.ppermute(value, 'x', [(i, (i + k) % NX) for i in range(NX)])]
    all_to_all x1 -> x0, starting transfers between devices: 4.24 us -> none  [scatter_totals(): lax.all_to_all(line.reshape(2 * NZ, TILE, TILE), 'z', 0, 0, tiled=True)]
    all_to_all x1, waiting for transfers between devices: 0.01 us -> 3.83 us  [gather_features(): line = lax.all_to_all(spread, 'z', 0, 0, tiled=True)]
  transfers between devices with their start and end apart: 39 -> 42, of which waited for: 21 -> 23; matrix products, arithmetic and copies ran while one was open for 3% -> 6% of each run, Pallas kernels for 0% -> 3%
where the time goes in v2:
time: 165 us; the launch traced here: 164 us
  starting transfers between devices  71.4 us (43%)
  waiting for transfers between devices  60.3 us (37%)
  local copies, waits for them, and re-layouts  14 us (8%)
  Pallas kernels  13.6 us (8%)
  other arithmetic  4.06 us (2%)
    ppermute x15, waiting for transfers between devices, swap(): return lax.ppermute(value, axes, pairs)  38 us
    ppermute x15, starting transfers between devices, swap(): return lax.ppermute(value, axes, pairs)  33.4 us
    ppermute x16, starting transfers between devices, shift_z(): return lax.ppermute(value, 'z', [(i, (i + k) % NZ) for i in range(NZ)])  19.2 us
    ppermute x10, waiting for transfers between devices, shift_x(): return lax.ppermute(value, 'x', [(i, (i + k) % NX) for i in range(NX)])  12.4 us
    ppermute x10, starting transfers between devices, shift_x(): return lax.ppermute(value, 'x', [(i, (i + k) % NX) for i in range(NX)])  10.6 us
    unnamed x28, local copies, waits for them, and re-layouts  8.35 us
    all_to_all x1, starting transfers between devices, gather_features(): line = lax.all_to_all(spread, 'z', 0, 0, tiled=True)  8.23 us
    ppermute x16, waiting for transfers between devices, shift_z(): return lax.ppermute(value, 'z', [(i, (i + k) % NZ) for i in range(NZ)])  6.12 us
  transfers between devices with their start and end apart: 42, of which 23 were waited for; matrix products, arithmetic and copies ran while one was open for 6% of the time, Pallas kernels for 3%

profile of v2, /device:TPU:1, one launch (start us, length us, event | category | flops | bytes accessed | tf_op | source)
XLA Modules:
  0.0 164.4 jit_solution(9002889010483630047)
XLA Ops:
  0.6 3.8 %collective-permute-start = (bf16[2,128,128]{2,1,0:T(8,128)(2,1)}, bf16[2,128,128]{2,1,0:T(8,128)(2,1)S(1)}, u32[]{:S(2)}, u32[]{:S(2)}) collective-permute-start(bf16[2,128,128]{2,1,0:T(8,128)(2,1)} %bitcast.46), channel_id=1, source_target_pairs={{0,4},{4,0},{1,5},{5,1},{2,6},{6,2},{3,7},{7,3},{8,12},{12,8},{9,1... | collective-permute-start | bytes 196616 | tf_op jit(solution)/shard_map/gather/ppermute | solution.py:30
  4.5 1.9 %collective-permute-done = bf16[2,128,128]{2,1,0:T(8,128)(2,1)S(1)} collective-permute-done((bf16[2,128,128]{2,1,0:T(8,128)(2,1)}, bf16[2,128,128]{2,1,0:T(8,128)(2,1)S(1)}, u32[]{:S(2)}, u32[]{:S(2)}) %collective-permute-start) | collective-permute-done | bytes 65568 | tf_op jit(solution)/shard_map/gather/ppermute | solution.py:30
  7.2 8.2 %all-to-all-start = ((bf16[16,128,128]{2,1,0:T(8,128)(2,1)}), bf16[16,128,128]{2,1,0:T(8,128)(2,1)S(1)}, u32[]{:S(2)}, u32[]{:S(2)}) async-start(bf16[16,128,128]{2,1,0:T(8,128)(2,1)} %bitcast.3), calls=%async_computation | async-start | bytes 1048576 | tf_op jit(solution)/shard_map/gather/all_to_all | solution.py:250
  15.5 2.5 %collective-permute-start.3 = (bf16[2,128,128]{2,1,0:T(8,128)(2,1)}, bf16[2,128,128]{2,1,0:T(8,128)(2,1)S(1)}, u32[]{:S(2)}, u32[]{:S(2)}) collective-permute-start(bf16[2,128,128]{2,1,0:T(8,128)(2,1)} %bitcast.47), channel_id=1, source_target_pairs={{0,192},{64,0},{128,64},{192,128},{1,193},{65,1},{129,65},{193,129... | collective-permute-start | bytes 196616 | tf_op jit(solution)/shard_map/gather/ppermute | solution.py:21
  20.0 3.5 %collective-permute-done.1 = bf16[2,128,128]{2,1,0:T(8,128)(2,1)S(1)} collective-permute-done((bf16[2,128,128]{2,1,0:T(8,128)(2,1)}, bf16[2,128,128]{2,1,0:T(8,128)(2,1)S(1)}, u32[]{:S(2)}, u32[]{:S(2)}) %collective-permute-start.1) | collective-permute-done | bytes 65568 | tf_op jit(solution)/shard_map/gather/ppermute | solution.py:21
  23.6 3.0 %collective-permute-start.5 = (bf16[8,128,128]{2,1,0:T(8,128)(2,1)S(1)}, bf16[8,128,128]{2,1,0:T(8,128)(2,1)}, u32[]{:S(2)}, u32[]{:S(2)}) collective-permute-start(bf16[8,128,128]{2,1,0:T(8,128)(2,1)S(1)} %constant_dynamic-update-slice_fusion.rest_0_), channel_id=1, source_target_pairs={{0,56},{8,0},{16,8},{24,16},{32,24},{40,32},{48,40},{56,48},{1,57}... | collective-permute-start | bytes 786440 | tf_op jit(solution)/shard_map/gather/ppermute | solution.py:25
  27.3 3.8 %all-to-all-done.rest_1_ = bf16[16,128,128]{2,1,0:T(8,128)(2,1)S(1)} async-done(((bf16[16,128,128]{2,1,0:T(8,128)(2,1)}), bf16[16,128,128]{2,1,0:T(8,128)(2,1)S(1)}, u32[]{:S(2)}, u32[]{:S(2)}) %all-to-all-start) | async-done | bytes 524320 | tf_op jit(solution)/shard_map/gather/all_to_all | solution.py:250
  31.1 2.5 %collective-permute-start.9 = (bf16[16,128,128]{2,1,0:T(8,128)(2,1)S(1)}, bf16[16,128,128]{2,1,0:T(8,128)(2,1)S(1)}, u32[]{:S(2)}, u32[]{:S(2)}) collective-permute-start(bf16[16,128,128]{2,1,0:T(8,128)(2,1)S(1)} %all-to-all-done.rest_1_), channel_id=1, source_target_pairs={{0,192},{64,0},{128,64},{192,128},{1,193},{65,1},{129,65},{193,129... | collective-permute-start | bytes 1572872 | tf_op jit(solution)/shard_map/gather/ppermute | solution.py:21
  34.1 1.6 collective-permute-start.7
  35.6 4.2 %collective-permute-done.7.rest_5_ = bf16[8,128,128]{2,1,0:T(8,128)(2,1)} collective-permute-done((bf16[8,128,128]{2,1,0:T(8,128)(2,1)}, bf16[8,128,128]{2,1,0:T(8,128)(2,1)}, u32[]{:S(2)}, u32[]{:S(2)}) %collective-permute-start.7) | collective-permute-done | bytes 262176 | tf_op jit(solution)/shard_map/gather/ppermute | solution.py:25
  39.8 2.8 %collective-permute-start.11 = (bf16[8,128,128]{2,1,0:T(8,128)(2,1)}, bf16[8,128,128]{2,1,0:T(8,128)(2,1)S(1)}, u32[]{:S(2)}, u32[]{:S(2)}) collective-permute-start(bf16[8,128,128]{2,1,0:T(8,128)(2,1)} %collective-permute-done.7.rest_5_), channel_id=1, source_target_pairs={{0,56},{8,0},{16,8},{24,16},{32,24},{40,32},{48,40},{56,48},{1,57}... | collective-permute-start | bytes 786440 | tf_op jit(solution)/shard_map/gather/ppermute | solution.py:25
  42.6 1.4 collective-permute-done.8.rest_8_
  45.3 1.3 reduce.3
  47.7 2.5 %collective-permute-start.15 = (bf16[4,128,128]{2,1,0:T(8,128)(2,1)}, bf16[4,128,128]{2,1,0:T(8,128)(2,1)S(1)}, u32[]{:S(2)}, u32[]{:S(2)}) collective-permute-start(bf16[4,128,128]{2,1,0:T(8,128)(2,1)} %slice.174), channel_id=1, source_target_pairs={{0,56},{8,0},{16,8},{24,16},{32,24},{40,32},{48,40},{56,48},{1,57}... | collective-permute-start | bytes 393224 | tf_op jit(solution)/shard_map/gather/ppermute | solution.py:25
  50.1 1.7 %slice.131 = bf16[8,128,128]{2,1,0:T(8,128)(2,1)} slice(bf16[16,128,128]{2,1,0:T(8,128)(2,1)} %copy-done.1), slice={[0:8], [0:128], [0:128]} | slice | bytes 524288 | tf_op jit(solution)/shard_map/gather/slice | solution.py:259
  52.5 1.6 collective-permute-start.13
  54.1 1.6 slice.173
  58.2 2.6 %collective-permute-done.12.rest_10_ = bf16[8,128,128]{2,1,0:T(8,128)(2,1)} collective-permute-done((bf16[8,128,128]{2,1,0:T(8,128)(2,1)}, bf16[8,128,128]{2,1,0:T(8,128)(2,1)}, u32[]{:S(2)}, u32[]{:S(2)}) %collective-permute-start.12) | collective-permute-done | bytes 262176 | tf_op jit(solution)/shard_map/gather/ppermute | solution.py:21
  61.1 2.8 %copy-done = bf16[8,1,24,128,128]{4,3,2,1,0:T(8,128)(2,1)S(1)} copy-done((bf16[8,1,24,128,128]{4,3,2,1,0:T(8,128)(2,1)S(1)}, bf16[8,1,24,128,128]{4,3,2,1,0:T(8,128)(2,1)}, u32[]{:S(2)}) %copy-start) | copy-done | bytes 6291480
  63.8 1.0 copy-done.2
  65.8 5.2 %forward.1 = (bf16[2,128,128]{2,1,0:T(8,128)(2,1)S(1)}, bf16[2,128,128]{2,1,0:T(8,128)(2,1)S(1)}, bf16[2,128,128]{2,1,0:T(8,128)(2,1)S(1)}, bf16[2,128,128]{2,1,0:T(8,128)(2,1)S(1)}) custom-call(s32[1]{0:T(128)} %bitcast.rep_ref, s32[200]{0:T(256)S(1)} %get-tuple-element.110.meta_ref, bf16[8,1,24,128,128]{4,3,2,1,0:T(8,128)(2,1)S(1)} %copy-done, ...), custom_call_target="tpu_custom_call" | custom-call | flops 805306368 | bytes 11534336 | tf_op jit(solution)/shard_map/forward/pallas_call | solution.py:100
  71.0 8.5 %collective-permute-start.16 = (bf16[2,128,128]{2,1,0:T(8,128)(2,1)S(1)}, bf16[2,128,128]{2,1,0:T(8,128)(2,1)S(1)}, u32[]{:S(2)}, u32[]{:S(2)}) collective-permute-start(bf16[2,128,128]{2,1,0:T(8,128)(2,1)S(1)} %get-tuple-element.51), channel_id=1, source_target_pairs={{0,1},{1,0},{2,3},{3,2},{4,5},{5,4},{6,7},{7,6},{8,9},{9,8},{10,11... | collective-permute-start | bytes 196616 | tf_op jit(solution)/shard_map/sections/ppermute | solution.py:30
  79.6 1.3 collective-permute-start.17
  81.3 1.9 %collective-permute-done.17.p2 = bf16[2,128,128]{2,1,0:T(8,128)(2,1)S(1)} collective-permute-done((bf16[2,128,128]{2,1,0:T(8,128)(2,1)S(1)}, bf16[2,128,128]{2,1,0:T(8,128)(2,1)S(1)}, u32[]{:S(2)}, u32[]{:S(2)}) %collective-permute-start.17) | collective-permute-done | bytes 65568 | tf_op jit(solution)/shard_map/sections/ppermute | solution.py:30
  83.2 1.7 %collective-permute-done.18.p3 = bf16[2,128,128]{2,1,0:T(8,128)(2,1)S(1)} collective-permute-done((bf16[2,128,128]{2,1,0:T(8,128)(2,1)S(1)}, bf16[2,128,128]{2,1,0:T(8,128)(2,1)S(1)}, u32[]{:S(2)}, u32[]{:S(2)}) %collective-permute-start.18) | collective-permute-done | bytes 65568 | tf_op jit(solution)/shard_map/sections/ppermute | solution.py:30
  85.0 1.6 middle.1
  86.9 1.2 collective-permute-start.21
  89.0 1.1 collective-permute-start.23
  91.1 1.0 collective-permute-done.20.s2
  92.1 5.0 %backward.1 = (bf16[8,128,128]{2,1,0:T(8,128)(2,1)S(1)}, bf16[8,128,128]{2,1,0:T(8,128)(2,1)S(1)}, bf16[8,128,128]{2,1,0:T(8,128)(2,1)S(1)}, bf16[8,128,128]{2,1...) custom-call(s32[1]{0:T(128)} %bitcast.rep_ref, ...), custom_call_target="tpu_custom_call" | custom-call | flops 805306368 | bytes 15728640 | tf_op jit(solution)/shard_map/backward/pallas_call | solution.py:202
  97.2 2.8 %collective-permute-start.24 = (bf16[1184,128]{1,0:T(8,128)(2,1)S(1)}, bf16[1184,128]{1,0:T(8,128)(2,1)S(1)}, u32[]{:S(2)}, u32[]{:S(2)}) collective-permute-start(bf16[1184,128]{1,0:T(8,128)(2,1)S(1)} %pad_maximum_fusion), channel_id=1, source_target_pairs={{0,4},{4,0},{1,5},{5,1},{2,6},{6,2},{3,7},{7,3},{8,12},{12,8},{9,1... | collective-permute-start | bytes 909320 | tf_op jit(solution)/shard_map/scatter/ppermute | solution.py:30
  100.3 6.1 %collective-permute-done.24 = bf16[1184,128]{1,0:T(8,128)(2,1)S(1)} collective-permute-done((bf16[1184,128]{1,0:T(8,128)(2,1)S(1)}, bf16[1184,128]{1,0:T(8,128)(2,1)S(1)}, u32[]{:S(2)}, u32[]{:S(2)}) %collective-permute-start.24) | collective-permute-done | bytes 303136 | tf_op jit(solution)/shard_map/scatter/ppermute | solution.py:30
  106.6 1.5 collective-permute-start.25
  108.1 2.5 %collective-permute-start.30 = (bf16[2048,128]{1,0:T(8,128)(2,1)S(1)}, bf16[2048,128]{1,0:T(8,128)(2,1)S(1)}, u32[]{:S(2)}, u32[]{:S(2)}) collective-permute-start(bf16[2048,128]{1,0:T(8,128)(2,1)S(1)} %bitcast.42), channel_id=1, source_target_pairs={{0,4},{4,0},{1,5},{5,1},{2,6},{6,2},{3,7},{7,3},{8,12},{12,8},{9,1... | collective-permute-start | bytes 1572872 | tf_op jit(solution)/shard_map/scatter/ppermute | solution.py:30
  110.5 7.1 %collective-permute-done.27 = bf16[2048,128]{1,0:T(8,128)(2,1)S(1)} collective-permute-done((bf16[2048,128]{1,0:T(8,128)(2,1)S(1)}, bf16[2048,128]{1,0:T(8,128)(2,1)S(1)}, u32[]{:S(2)}, u32[]{:S(2)}) %collective-permute-start.27) | collective-permute-done | bytes 524320 | tf_op jit(solution)/shard_map/scatter/ppermute | solution.py:30
  118.1 2.7 %collective-permute-start.29 = (bf16[1184,128]{1,0:T(8,128)(2,1)S(1)}, bf16[1184,128]{1,0:T(8,128)(2,1)S(1)}, u32[]{:S(2)}, u32[]{:S(2)}) collective-permute-start(bf16[1184,128]{1,0:T(8,128)(2,1)S(1)} %pad_maximum_fusion.2), channel_id=1, source_target_pairs={{0,56},{8,0},{16,8},{24,16},{32,24},{40,32},{48,40},{56,48},{1,57}... | collective-permute-start | bytes 909320 | tf_op jit(solution)/shard_map/scatter/ppermute | solution.py:25
  120.8 2.5 %collective-permute-start.33 = (bf16[2048,128]{1,0:T(8,128)(2,1)S(1)}, bf16[2048,128]{1,0:T(8,128)(2,1)S(1)}, u32[]{:S(2)}, u32[]{:S(2)}) collective-permute-start(bf16[2048,128]{1,0:T(8,128)(2,1)S(1)} %bitcast.41), channel_id=1, source_target_pairs={{0,4},{4,0},{1,5},{5,1},{2,6},{6,2},{3,7},{7,3},{8,12},{12,8},{9,1... | collective-permute-start | bytes 1572872 | tf_op jit(solution)/shard_map/scatter/ppermute | solution.py:30
  123.2 5.6 %collective-permute-done.30 = bf16[2048,128]{1,0:T(8,128)(2,1)S(1)} collective-permute-done((bf16[2048,128]{1,0:T(8,128)(2,1)S(1)}, bf16[2048,128]{1,0:T(8,128)(2,1)S(1)}, u32[]{:S(2)}, u32[]{:S(2)}) %collective-permute-start.30) | collective-permute-done | bytes 524320 | tf_op jit(solution)/shard_map/scatter/ppermute | solution.py:30
  129.3 1.5 collective-permute-start.31
  130.8 9.3 %collective-permute-done.33 = bf16[2048,128]{1,0:T(8,128)(2,1)S(1)} collective-permute-done((bf16[2048,128]{1,0:T(8,128)(2,1)S(1)}, bf16[2048,128]{1,0:T(8,128)(2,1)S(1)}, u32[]{:S(2)}, u32[]{:S(2)}) %collective-permute-start.33) | collective-permute-done | bytes 524320 | tf_op jit(solution)/shard_map/scatter/ppermute | solution.py:30
  140.5 2.5 %collective-permute-start.36 = (bf16[1024,128]{1,0:T(8,128)(2,1)S(1)}, bf16[1024,128]{1,0:T(8,128)(2,1)S(1)}, u32[]{:S(2)}, u32[]{:S(2)}) collective-permute-start(bf16[1024,128]{1,0:T(8,128)(2,1)S(1)} %bitcast.44), channel_id=1, source_target_pairs={{0,4},{4,0},{1,5},{5,1},{2,6},{6,2},{3,7},{7,3},{8,12},{12,8},{9,1... | collective-permute-start | bytes 786440 | tf_op jit(solution)/shard_map/scatter/ppermute | solution.py:30
  143.0 2.6 %collective-permute-start.35 = (bf16[1024,128]{1,0:T(8,128)(2,1)S(1)}, bf16[1024,128]{1,0:T(8,128)(2,1)S(1)}, u32[]{:S(2)}, u32[]{:S(2)}) collective-permute-start(bf16[1024,128]{1,0:T(8,128)(2,1)S(1)} %get-tuple-element.93), channel_id=1, source_target_pairs={{0,56},{8,0},{16,8},{24,16},{32,24},{40,32},{48,40},{56,48},{1,57}... | collective-permute-start | bytes 786440 | tf_op jit(solution)/shard_map/scatter/ppermute | solution.py:25
  145.6 2.2 %collective-permute-done.36 = bf16[1024,128]{1,0:T(8,128)(2,1)S(1)} collective-permute-done((bf16[1024,128]{1,0:T(8,128)(2,1)S(1)}, bf16[1024,128]{1,0:T(8,128)(2,1)S(1)}, u32[]{:S(2)}, u32[]{:S(2)}) %collective-permute-start.36) | collective-permute-done | bytes 262176 | tf_op jit(solution)/shard_map/scatter/ppermute | solution.py:30
  147.8 1.1 collective-permute-done.35
  149.3 1.9 %collective-permute-start.38 = (bf16[416,128]{1,0:T(8,128)(2,1)S(1)}, bf16[416,128]{1,0:T(8,128)(2,1)S(1)}, u32[]{:S(2)}, u32[]{:S(2)}) collective-permute-start(bf16[416,128]{1,0:T(8,128)(2,1)S(1)} %get-tuple-element.105), channel_id=1, source_target_pairs={{0,128},{64,192},{128,0},{192,64},{1,129},{65,193},{129,1},{193,65... | collective-permute-start | bytes 319496 | tf_op jit(solution)/shard_map/scatter/ppermute | solution.py:21
  152.0 3.1 %collective-permute-done.37 = bf16[416,128]{1,0:T(8,128)(2,1)S(1)} collective-permute-done((bf16[416,128]{1,0:T(8,128)(2,1)S(1)}, bf16[416,128]{1,0:T(8,128)(2,1)S(1)}, u32[]{:S(2)}, u32[]{:S(2)}) %collective-permute-start.37) | collective-permute-done | bytes 106528 | tf_op jit(solution)/shard_map/scatter/ppermute | solution.py:21
  155.8 5.2 %collective-permute-start.40 = (f32[160,128]{1,0:T(8,128)S(1)}, f32[160,128]{1,0:T(8,128)S(1)}, u32[]{:S(2)}, u32[]{:S(2)}) collective-permute-start(f32[160,128]{1,0:T(8,128)S(1)} %convert_add_fusion.8.mine_ref), channel_id=1, source_target_pairs={{0,1},{1,0},{2,3},{3,2},{4,5},{5,4},{6,7},{7,6},{8,9},{9,8},{10,11... | collective-permute-start | bytes 245768 | tf_op jit(solution)/shard_map/scatter/ppermute | solution.py:30
  162.6 1.8 %last.1 = (bf16[1,256,128]{2,1,0:T(8,128)(2,1)}, f32[128,256]{1,0:T(8,128)}, f32[1,256]{1,0:T(1,128)}) custom-call(s32[1]{0:T(128)} %bitcast.rep_ref, f32[2,128,128]{2,1,0:T(8,128)} %bitcast.45, f32[160,128]{1,0:T(8,128)} %copy-done.8, f32[160,128]{1,0:T(8,128)} %copy-done.9), custom_call_target="tpu_custom_call" | custom-call | tf_op jit(solution)/shard_map/last/pallas_call | solution.py:233
  (110 shorter events, 18.5 us)
Async XLA Ops:
  0.6 5.7 %collective-permute-start = (bf16[2,128,128]{2,1,0:T(8,128)(2,1)}, bf16[2,128,128]{2,1,0:T(8,128)(2,1)S(1)}, u32[]{:S(2)}, u32[]{:S(2)}) collective-permute-start(bf16[2,128,128]{2,1,0:T(8,128)(2,1)} %bitcast.46), channel_id=1, source_target_pairs={{0,4},{4,0},{1,5},{5,1},{2,6},{6,2},{3,7},{7,3},{8,12},{12,8},{9,1... | collective-permute-start | bytes 196616 | tf_op jit(solution)/shard_map/gather/ppermute | solution.py:30
  6.3 85.8 %slice-start = ((s8[6291456]{0:T(1024)(128)(4,1)}), s8[2097152]{0:T(1024)(128)(4,1)S(1)}, s32[]{:S(2)}) async-start(s8[6291456]{0:T(1024)(128)(4,1)} %bitcast.37), calls=%async_computation.1 | async-start | bytes 4194304
  7.2 23.9 %all-to-all-start = ((bf16[16,128,128]{2,1,0:T(8,128)(2,1)}), bf16[16,128,128]{2,1,0:T(8,128)(2,1)S(1)}, u32[]{:S(2)}, u32[]{:S(2)}) async-start(bf16[16,128,128]{2,1,0:T(8,128)(2,1)} %bitcast.3), calls=%async_computation | async-start | bytes 1048576 | tf_op jit(solution)/shard_map/gather/all_to_all | solution.py:250
  15.5 8.1 %collective-permute-start.3 = (bf16[2,128,128]{2,1,0:T(8,128)(2,1)}, bf16[2,128,128]{2,1,0:T(8,128)(2,1)S(1)}, u32[]{:S(2)}, u32[]{:S(2)}) collective-permute-start(bf16[2,128,128]{2,1,0:T(8,128)(2,1)} %bitcast.47), channel_id=1, source_target_pairs={{0,192},{64,0},{128,64},{192,128},{1,193},{65,1},{129,65},{193,129... | collective-permute-start | bytes 196616 | tf_op jit(solution)/shard_map/gather/ppermute | solution.py:21
  18.0 5.5 %collective-permute-start.2 = (bf16[2,128,128]{2,1,0:T(8,128)(2,1)}, bf16[2,128,128]{2,1,0:T(8,128)(2,1)S(1)}, u32[]{:S(2)}, u32[]{:S(2)}) collective-permute-start(bf16[2,128,128]{2,1,0:T(8,128)(2,1)} %bitcast.48), channel_id=1, source_target_pairs={{0,128},{64,192},{128,0},{192,64},{1,129},{65,193},{129,1},{193,65... | collective-permute-start | bytes 196616 | tf_op jit(solution)/shard_map/gather/ppermute | solution.py:21
  18.5 5.0 %collective-permute-start.1 = (bf16[2,128,128]{2,1,0:T(8,128)(2,1)}, bf16[2,128,128]{2,1,0:T(8,128)(2,1)S(1)}, u32[]{:S(2)}, u32[]{:S(2)}) collective-permute-start(bf16[2,128,128]{2,1,0:T(8,128)(2,1)} %bitcast.49), channel_id=1, source_target_pairs={{0,64},{64,128},{128,192},{192,0},{1,65},{65,129},{129,193},{193,1... | collective-permute-start | bytes 196616 | tf_op jit(solution)/shard_map/gather/ppermute | solution.py:21
  20.0 65.0 %copy-start.7 = (f32[256]{0:T(256)S(1)}, f32[256]{0:T(256)}, u32[]{:S(2)}) copy-start(f32[256]{0:T(256)} %param.9) | copy-start | bytes 3076
  23.6 10.5 %collective-permute-start.5 = (bf16[8,128,128]{2,1,0:T(8,128)(2,1)S(1)}, bf16[8,128,128]{2,1,0:T(8,128)(2,1)}, u32[]{:S(2)}, u32[]{:S(2)}) collective-permute-start(bf16[8,128,128]{2,1,0:T(8,128)(2,1)S(1)} %constant_dynamic-update-slice_fusion.rest_0_), channel_id=1, source_target_pairs={{0,56},{8,0},{16,8},{24,16},{32,24},{40,32},{48,40},{56,48},{1,57}... | collective-permute-start | bytes 786440 | tf_op jit(solution)/shard_map/gather/ppermute | solution.py:25
  26.6 9.0 %collective-permute-start.4 = (bf16[8,128,128]{2,1,0:T(8,128)(2,1)S(1)}, bf16[8,128,128]{2,1,0:T(8,128)(2,1)}, u32[]{:S(2)}, u32[]{:S(2)}) collective-permute-start(bf16[8,128,128]{2,1,0:T(8,128)(2,1)S(1)} %constant_dynamic-update-slice_fusion.rest_0_), channel_id=1, source_target_pairs={{0,8},{8,16},{16,24},{24,32},{32,40},{40,48},{48,56},{56,0},{1,9},... | collective-permute-start | bytes 786440 | tf_op jit(solution)/shard_map/gather/ppermute | solution.py:25
  31.1 11.4 %collective-permute-start.9 = (bf16[16,128,128]{2,1,0:T(8,128)(2,1)S(1)}, bf16[16,128,128]{2,1,0:T(8,128)(2,1)S(1)}, u32[]{:S(2)}, u32[]{:S(2)}) collective-permute-start(bf16[16,128,128]{2,1,0:T(8,128)(2,1)S(1)} %all-to-all-done.rest_1_), channel_id=1, source_target_pairs={{0,192},{64,0},{128,64},{192,128},{1,193},{65,1},{129,65},{193,129... | collective-permute-start | bytes 1572872 | tf_op jit(solution)/shard_map/gather/ppermute | solution.py:21
  33.6 10.4 %collective-permute-start.8 = (bf16[16,128,128]{2,1,0:T(8,128)(2,1)S(1)}, bf16[16,128,128]{2,1,0:T(8,128)(2,1)S(1)}, u32[]{:S(2)}, u32[]{:S(2)}) collective-permute-start(bf16[16,128,128]{2,1,0:T(8,128)(2,1)S(1)} %all-to-all-done.rest_1_), channel_id=1, source_target_pairs={{0,64},{64,128},{128,192},{192,0},{1,65},{65,129},{129,193},{193,1... | collective-permute-start | bytes 1572872 | tf_op jit(solution)/shard_map/gather/ppermute | solution.py:21
  34.1 5.7 %collective-permute-start.7 = (bf16[8,128,128]{2,1,0:T(8,128)(2,1)}, bf16[8,128,128]{2,1,0:T(8,128)(2,1)}, u32[]{:S(2)}, u32[]{:S(2)}) collective-permute-start(bf16[8,128,128]{2,1,0:T(8,128)(2,1)} %collective-permute-done.5.rest_3_), channel_id=1, source_target_pairs={{0,56},{8,0},{16,8},{24,16},{32,24},{40,32},{48,40},{56,48},{1,57}... | collective-permute-start | bytes 786440 | tf_op jit(solution)/shard_map/gather/ppermute | solution.py:25
  35.6 6.9 %collective-permute-start.6 = (bf16[8,128,128]{2,1,0:T(8,128)(2,1)}, bf16[8,128,128]{2,1,0:T(8,128)(2,1)}, u32[]{:S(2)}, u32[]{:S(2)}) collective-permute-start(bf16[8,128,128]{2,1,0:T(8,128)(2,1)} %collective-permute-done.4.rest_2_), channel_id=1, source_target_pairs={{0,8},{8,16},{16,24},{24,32},{32,40},{40,48},{48,56},{56,0},{1,9},... | collective-permute-start | bytes 786440 | tf_op jit(solution)/shard_map/gather/ppermute | solution.py:25
  39.8 7.2 %collective-permute-start.11 = (bf16[8,128,128]{2,1,0:T(8,128)(2,1)}, bf16[8,128,128]{2,1,0:T(8,128)(2,1)S(1)}, u32[]{:S(2)}, u32[]{:S(2)}) collective-permute-start(bf16[8,128,128]{2,1,0:T(8,128)(2,1)} %collective-permute-done.7.rest_5_), channel_id=1, source_target_pairs={{0,56},{8,0},{16,8},{24,16},{32,24},{40,32},{48,40},{56,48},{1,57}... | collective-permute-start | bytes 786440 | tf_op jit(solution)/shard_map/gather/ppermute | solution.py:25
  44.8 9.3 %collective-permute-start.10 = (bf16[8,128,128]{2,1,0:T(8,128)(2,1)}, bf16[8,128,128]{2,1,0:T(8,128)(2,1)}, u32[]{:S(2)}, u32[]{:S(2)}) collective-permute-start(bf16[8,128,128]{2,1,0:T(8,128)(2,1)} %collective-permute-done.6.rest_4_), channel_id=1, source_target_pairs={{0,8},{8,16},{16,24},{24,32},{32,40},{40,48},{48,56},{56,0},{1,9},... | collective-permute-start | bytes 786440 | tf_op jit(solution)/shard_map/gather/ppermute | solution.py:25
  47.7 9.6 %collective-permute-start.15 = (bf16[4,128,128]{2,1,0:T(8,128)(2,1)}, bf16[4,128,128]{2,1,0:T(8,128)(2,1)S(1)}, u32[]{:S(2)}, u32[]{:S(2)}) collective-permute-start(bf16[4,128,128]{2,1,0:T(8,128)(2,1)} %slice.174), channel_id=1, source_target_pairs={{0,56},{8,0},{16,8},{24,16},{32,24},{40,32},{48,40},{56,48},{1,57}... | collective-permute-start | bytes 393224 | tf_op jit(solution)/shard_map/gather/ppermute | solution.py:25
  52.5 5.7 %collective-permute-start.13 = (bf16[8,128,128]{2,1,0:T(8,128)(2,1)}, bf16[8,128,128]{2,1,0:T(8,128)(2,1)}, u32[]{:S(2)}, u32[]{:S(2)}) collective-permute-start(bf16[8,128,128]{2,1,0:T(8,128)(2,1)} %slice.132), channel_id=1, source_target_pairs={{0,192},{64,0},{128,64},{192,128},{1,193},{65,1},{129,65},{193,129... | collective-permute-start | bytes 786440 | tf_op jit(solution)/shard_map/gather/ppermute | solution.py:21
  54.1 6.7 %collective-permute-start.12 = (bf16[8,128,128]{2,1,0:T(8,128)(2,1)}, bf16[8,128,128]{2,1,0:T(8,128)(2,1)}, u32[]{:S(2)}, u32[]{:S(2)}) collective-permute-start(bf16[8,128,128]{2,1,0:T(8,128)(2,1)} %slice.131), channel_id=1, source_target_pairs={{0,64},{64,128},{128,192},{192,0},{1,65},{65,129},{129,193},{193,1... | collective-permute-start | bytes 786440 | tf_op jit(solution)/shard_map/gather/ppermute | solution.py:21
  55.7 5.3 %collective-permute-start.14 = (bf16[4,128,128]{2,1,0:T(8,128)(2,1)}, bf16[4,128,128]{2,1,0:T(8,128)(2,1)}, u32[]{:S(2)}, u32[]{:S(2)}) collective-permute-start(bf16[4,128,128]{2,1,0:T(8,128)(2,1)} %slice.173), channel_id=1, source_target_pairs={{0,8},{8,16},{16,24},{24,32},{32,40},{40,48},{48,56},{56,0},{1,9},... | collective-permute-start | bytes 393224 | tf_op jit(solution)/shard_map/gather/ppermute | solution.py:25
  65.8 19.1 %copy-start.5 = (bf16[256,256]{1,0:T(8,128)(2,1)S(1)}, bf16[256,256]{1,0:T(8,128)(2,1)}, u32[]{:S(2)}) copy-start(bf16[256,256]{1,0:T(8,128)(2,1)} %cot_ref.1) | copy-start | bytes 393220
  65.8 19.1 %copy-start.6 = (bf16[128,256]{1,0:T(8,128)(2,1)S(1)}, bf16[128,256]{1,0:T(8,128)(2,1)}, u32[]{:S(2)}) copy-start(bf16[128,256]{1,0:T(8,128)(2,1)} %weight_ref.1) | copy-start | bytes 196612
  65.8 26.3 %slice-start.1 = ((s8[6291456]{0:T(1024)(128)(4,1)}), s8[4194304]{0:T(1024)(128)(4,1)S(1)}, s32[]{:S(2)}) async-start(s8[6291456]{0:T(1024)(128)(4,1)} %bitcast.37), calls=%async_computation.2 | async-start | bytes 8388608
  71.0 10.3 %collective-permute-start.16 = (bf16[2,128,128]{2,1,0:T(8,128)(2,1)S(1)}, bf16[2,128,128]{2,1,0:T(8,128)(2,1)S(1)}, u32[]{:S(2)}, u32[]{:S(2)}) collective-permute-start(bf16[2,128,128]{2,1,0:T(8,128)(2,1)S(1)} %get-tuple-element.51), channel_id=1, source_target_pairs={{0,1},{1,0},{2,3},{3,2},{4,5},{5,4},{6,7},{7,6},{8,9},{9,8},{10,11... | collective-permute-start | bytes 196616 | tf_op jit(solution)/shard_map/sections/ppermute | solution.py:30
  79.6 3.7 %collective-permute-start.17 = (bf16[2,128,128]{2,1,0:T(8,128)(2,1)S(1)}, bf16[2,128,128]{2,1,0:T(8,128)(2,1)S(1)}, u32[]{:S(2)}, u32[]{:S(2)}) collective-permute-start(bf16[2,128,128]{2,1,0:T(8,128)(2,1)S(1)} %get-tuple-element.52), channel_id=1, source_target_pairs={{0,2},{2,0},{1,3},{3,1},{4,6},{6,4},{5,7},{7,5},{8,10},{10,8},{9,1... | collective-permute-start | bytes 196616 | tf_op jit(solution)/shard_map/sections/ppermute | solution.py:30
  80.9 4.1 %collective-permute-start.18 = (bf16[2,128,128]{2,1,0:T(8,128)(2,1)S(1)}, bf16[2,128,128]{2,1,0:T(8,128)(2,1)S(1)}, u32[]{:S(2)}, u32[]{:S(2)}) collective-permute-start(bf16[2,128,128]{2,1,0:T(8,128)(2,1)S(1)} %get-tuple-element.53), channel_id=1, source_target_pairs={{0,3},{1,2},{2,1},{3,0},{4,7},{5,6},{6,5},{7,4},{8,11},{9,10},{10,... | collective-permute-start | bytes 196616 | tf_op jit(solution)/shard_map/sections/ppermute | solution.py:30
  86.5 2.5 %collective-permute-start.22 = (f32[160,128]{1,0:T(8,128)S(1)}, f32[160,128]{1,0:T(8,128)S(1)}, u32[]{:S(2)}, u32[]{:S(2)}) collective-permute-start(f32[160,128]{1,0:T(8,128)S(1)} %get-tuple-element.63), channel_id=1, source_target_pairs={{0,1},{1,0},{2,3},{3,2},{4,5},{5,4},{6,7},{7,6},{8,9},{9,8},{10,11... | collective-permute-start | bytes 245768 | tf_op jit(solution)/shard_map/weights/ppermute | solution.py:30
  86.9 4.2 %collective-permute-start.21 = (bf16[2,128,128]{2,1,0:T(8,128)(2,1)S(1)}, bf16[2,128,128]{2,1,0:T(8,128)(2,1)S(1)}, u32[]{:S(2)}, u32[]{:S(2)}) collective-permute-start(bf16[2,128,128]{2,1,0:T(8,128)(2,1)S(1)} %get-tuple-element.55.s0), channel_id=1, source_target_pairs={{0,3},{1,2},{2,1},{3,0},{4,7},{5,6},{6,5},{7,4},{8,11},{9,10},{10,... | collective-permute-start | bytes 196616 | tf_op jit(solution)/shard_map/slopes/ppermute | solution.py:30
  88.1 4.0 %collective-permute-start.20 = (bf16[2,128,128]{2,1,0:T(8,128)(2,1)S(1)}, bf16[2,128,128]{2,1,0:T(8,128)(2,1)S(1)}, u32[]{:S(2)}, u32[]{:S(2)}) collective-permute-start(bf16[2,128,128]{2,1,0:T(8,128)(2,1)S(1)} %get-tuple-element.55.s0), channel_id=1, source_target_pairs={{0,2},{2,0},{1,3},{3,1},{4,6},{6,4},{5,7},{7,5},{8,10},{10,8},{9,1... | collective-permute-start | bytes 196616 | tf_op jit(solution)/shard_map/slopes/ppermute | solution.py:30
  88.4 3.7 %collective-permute-start.19 = (bf16[2,128,128]{2,1,0:T(8,128)(2,1)S(1)}, bf16[2,128,128]{2,1,0:T(8,128)(2,1)S(1)}, u32[]{:S(2)}, u32[]{:S(2)}) collective-permute-start(bf16[2,128,128]{2,1,0:T(8,128)(2,1)S(1)} %get-tuple-element.55.s0), channel_id=1, source_target_pairs={{0,1},{1,0},{2,3},{3,2},{4,5},{5,4},{6,7},{7,6},{8,9},{9,8},{10,11... | collective-permute-start | bytes 196616 | tf_op jit(solution)/shard_map/slopes/ppermute | solution.py:30
  89.0 8.1 %collective-permute-start.23 = (f32[160,128]{1,0:T(8,128)S(1)}, f32[160,128]{1,0:T(8,128)S(1)}, u32[]{:S(2)}, u32[]{:S(2)}) collective-permute-start(f32[160,128]{1,0:T(8,128)S(1)} %add.175), channel_id=1, source_target_pairs={{0,2},{2,0},{1,3},{3,1},{4,6},{6,4},{5,7},{7,5},{8,10},{10,8},{9,1... | collective-permute-start | bytes 245768 | tf_op jit(solution)/shard_map/weights/ppermute | solution.py:30
  97.2 9.1 %collective-permute-start.24 = (bf16[1184,128]{1,0:T(8,128)(2,1)S(1)}, bf16[1184,128]{1,0:T(8,128)(2,1)S(1)}, u32[]{:S(2)}, u32[]{:S(2)}) collective-permute-start(bf16[1184,128]{1,0:T(8,128)(2,1)S(1)} %pad_maximum_fusion), channel_id=1, source_target_pairs={{0,4},{4,0},{1,5},{5,1},{2,6},{6,2},{3,7},{7,3},{8,12},{12,8},{9,1... | collective-permute-start | bytes 909320 | tf_op jit(solution)/shard_map/scatter/ppermute | solution.py:30
  100.0 17.6 %collective-permute-start.27 = (bf16[2048,128]{1,0:T(8,128)(2,1)S(1)}, bf16[2048,128]{1,0:T(8,128)(2,1)S(1)}, u32[]{:S(2)}, u32[]{:S(2)}) collective-permute-start(bf16[2048,128]{1,0:T(8,128)(2,1)S(1)} %bitcast.43), channel_id=1, source_target_pairs={{0,4},{4,0},{1,5},{5,1},{2,6},{6,2},{3,7},{7,3},{8,12},{12,8},{9,1... | collective-permute-start | bytes 1572872 | tf_op jit(solution)/shard_map/scatter/ppermute | solution.py:30
  106.5 11.1 %collective-permute-start.26 = (bf16[672,128]{1,0:T(8,128)(2,1)S(1)}, bf16[672,128]{1,0:T(8,128)(2,1)S(1)}, u32[]{:S(2)}, u32[]{:S(2)}) collective-permute-start(bf16[672,128]{1,0:T(8,128)(2,1)S(1)} %get-tuple-element.107), channel_id=1, source_target_pairs={{0,56},{8,0},{16,8},{24,16},{32,24},{40,32},{48,40},{56,48},{1,57}... | collective-permute-start | bytes 516104 | tf_op jit(solution)/shard_map/scatter/ppermute | solution.py:25
  106.6 11.0 %collective-permute-start.25 = (bf16[672,128]{1,0:T(8,128)(2,1)S(1)}, bf16[672,128]{1,0:T(8,128)(2,1)S(1)}, u32[]{:S(2)}, u32[]{:S(2)}) collective-permute-start(bf16[672,128]{1,0:T(8,128)(2,1)S(1)} %get-tuple-element.108), channel_id=1, source_target_pairs={{0,8},{8,16},{16,24},{24,32},{32,40},{40,48},{48,56},{56,0},{1,9},... | collective-permute-start | bytes 516104 | tf_op jit(solution)/shard_map/scatter/ppermute | solution.py:25
  108.1 20.8 %collective-permute-start.30 = (bf16[2048,128]{1,0:T(8,128)(2,1)S(1)}, bf16[2048,128]{1,0:T(8,128)(2,1)S(1)}, u32[]{:S(2)}, u32[]{:S(2)}) collective-permute-start(bf16[2048,128]{1,0:T(8,128)(2,1)S(1)} %bitcast.42), channel_id=1, source_target_pairs={{0,4},{4,0},{1,5},{5,1},{2,6},{6,2},{3,7},{7,3},{8,12},{12,8},{9,1... | collective-permute-start | bytes 1572872 | tf_op jit(solution)/shard_map/scatter/ppermute | solution.py:30
  117.9 10.9 %collective-permute-start.28 = (bf16[1184,128]{1,0:T(8,128)(2,1)S(1)}, bf16[1184,128]{1,0:T(8,128)(2,1)S(1)}, u32[]{:S(2)}, u32[]{:S(2)}) collective-permute-start(bf16[1184,128]{1,0:T(8,128)(2,1)S(1)} %pad_maximum_fusion.1), channel_id=1, source_target_pairs={{0,8},{8,16},{16,24},{24,32},{32,40},{40,48},{48,56},{56,0},{1,9},... | collective-permute-start | bytes 909320 | tf_op jit(solution)/shard_map/scatter/ppermute | solution.py:25
  118.1 10.8 %collective-permute-start.29 = (bf16[1184,128]{1,0:T(8,128)(2,1)S(1)}, bf16[1184,128]{1,0:T(8,128)(2,1)S(1)}, u32[]{:S(2)}, u32[]{:S(2)}) collective-permute-start(bf16[1184,128]{1,0:T(8,128)(2,1)S(1)} %pad_maximum_fusion.2), channel_id=1, source_target_pairs={{0,56},{8,0},{16,8},{24,16},{32,24},{40,32},{48,40},{56,48},{1,57}... | collective-permute-start | bytes 909320 | tf_op jit(solution)/shard_map/scatter/ppermute | solution.py:25
  120.8 19.3 %collective-permute-start.33 = (bf16[2048,128]{1,0:T(8,128)(2,1)S(1)}, bf16[2048,128]{1,0:T(8,128)(2,1)S(1)}, u32[]{:S(2)}, u32[]{:S(2)}) collective-permute-start(bf16[2048,128]{1,0:T(8,128)(2,1)S(1)} %bitcast.41), channel_id=1, source_target_pairs={{0,4},{4,0},{1,5},{5,1},{2,6},{6,2},{3,7},{7,3},{8,12},{12,8},{9,1... | collective-permute-start | bytes 1572872 | tf_op jit(solution)/shard_map/scatter/ppermute | solution.py:30
  129.1 10.9 %collective-permute-start.32 = (bf16[1184,128]{1,0:T(8,128)(2,1)S(1)}, bf16[1184,128]{1,0:T(8,128)(2,1)S(1)}, u32[]{:S(2)}, u32[]{:S(2)}) collective-permute-start(bf16[1184,128]{1,0:T(8,128)(2,1)S(1)} %pad_maximum_fusion.4), channel_id=1, source_target_pairs={{0,56},{8,0},{16,8},{24,16},{32,24},{40,32},{48,40},{56,48},{1,57}... | collective-permute-start | bytes 909320 | tf_op jit(solution)/shard_map/scatter/ppermute | solution.py:25
  129.3 10.8 %collective-permute-start.31 = (bf16[1184,128]{1,0:T(8,128)(2,1)S(1)}, bf16[1184,128]{1,0:T(8,128)(2,1)S(1)}, u32[]{:S(2)}, u32[]{:S(2)}) collective-permute-start(bf16[1184,128]{1,0:T(8,128)(2,1)S(1)} %pad_maximum_fusion.3), channel_id=1, source_target_pairs={{0,8},{8,16},{16,24},{24,32},{32,40},{40,48},{48,56},{56,0},{1,9},... | collective-permute-start | bytes 909320 | tf_op jit(solution)/shard_map/scatter/ppermute | solution.py:25
  140.4 8.5 %collective-permute-start.34 = (bf16[1184,128]{1,0:T(8,128)(2,1)S(1)}, bf16[1184,128]{1,0:T(8,128)(2,1)S(1)}, u32[]{:S(2)}, u32[]{:S(2)}) collective-permute-start(bf16[1184,128]{1,0:T(8,128)(2,1)S(1)} %pad_maximum_fusion.5), channel_id=1, source_target_pairs={{0,8},{8,16},{16,24},{24,32},{32,40},{40,48},{48,56},{56,0},{1,9},... | collective-permute-start | bytes 909320 | tf_op jit(solution)/shard_map/scatter/ppermute | solution.py:25
  140.5 7.3 %collective-permute-start.36 = (bf16[1024,128]{1,0:T(8,128)(2,1)S(1)}, bf16[1024,128]{1,0:T(8,128)(2,1)S(1)}, u32[]{:S(2)}, u32[]{:S(2)}) collective-permute-start(bf16[1024,128]{1,0:T(8,128)(2,1)S(1)} %bitcast.44), channel_id=1, source_target_pairs={{0,4},{4,0},{1,5},{5,1},{2,6},{6,2},{3,7},{7,3},{8,12},{12,8},{9,1... | collective-permute-start | bytes 786440 | tf_op jit(solution)/shard_map/scatter/ppermute | solution.py:30
  143.0 5.9 %collective-permute-start.35 = (bf16[1024,128]{1,0:T(8,128)(2,1)S(1)}, bf16[1024,128]{1,0:T(8,128)(2,1)S(1)}, u32[]{:S(2)}, u32[]{:S(2)}) collective-permute-start(bf16[1024,128]{1,0:T(8,128)(2,1)S(1)} %get-tuple-element.93), channel_id=1, source_target_pairs={{0,56},{8,0},{16,8},{24,16},{32,24},{40,32},{48,40},{56,48},{1,57}... | collective-permute-start | bytes 786440 | tf_op jit(solution)/shard_map/scatter/ppermute | solution.py:25
  149.2 6.0 %collective-permute-start.37 = (bf16[416,128]{1,0:T(8,128)(2,1)S(1)}, bf16[416,128]{1,0:T(8,128)(2,1)S(1)}, u32[]{:S(2)}, u32[]{:S(2)}) collective-permute-start(bf16[416,128]{1,0:T(8,128)(2,1)S(1)} %get-tuple-element.104), channel_id=1, source_target_pairs={{0,64},{64,128},{128,192},{192,0},{1,65},{65,129},{129,193},{193,1... | collective-permute-start | bytes 319496 | tf_op jit(solution)/shard_map/scatter/ppermute | solution.py:21
  149.3 5.9 %collective-permute-start.38 = (bf16[416,128]{1,0:T(8,128)(2,1)S(1)}, bf16[416,128]{1,0:T(8,128)(2,1)S(1)}, u32[]{:S(2)}, u32[]{:S(2)}) collective-permute-start(bf16[416,128]{1,0:T(8,128)(2,1)S(1)} %get-tuple-element.105), channel_id=1, source_target_pairs={{0,128},{64,192},{128,0},{192,64},{1,129},{65,193},{129,1},{193,65... | collective-permute-start | bytes 319496 | tf_op jit(solution)/shard_map/scatter/ppermute | solution.py:21
  151.2 4.6 %collective-permute-start.39 = (bf16[416,128]{1,0:T(8,128)(2,1)S(1)}, bf16[416,128]{1,0:T(8,128)(2,1)S(1)}, u32[]{:S(2)}, u32[]{:S(2)}) collective-permute-start(bf16[416,128]{1,0:T(8,128)(2,1)S(1)} %get-tuple-element.106), channel_id=1, source_target_pairs={{0,192},{64,0},{128,64},{192,128},{1,193},{65,1},{129,65},{193,129... | collective-permute-start | bytes 319496 | tf_op jit(solution)/shard_map/scatter/ppermute | solution.py:21
  155.8 6.1 %copy-start.8 = (f32[160,128]{1,0:T(8,128)}, f32[160,128]{1,0:T(8,128)S(1)}, u32[]{:S(2)}) copy-start(f32[160,128]{1,0:T(8,128)S(1)} %convert_add_fusion.8.mine_ref) | copy-start | bytes 245764
  155.8 6.1 %collective-permute-start.40 = (f32[160,128]{1,0:T(8,128)S(1)}, f32[160,128]{1,0:T(8,128)S(1)}, u32[]{:S(2)}, u32[]{:S(2)}) collective-permute-start(f32[160,128]{1,0:T(8,128)S(1)} %convert_add_fusion.8.mine_ref), channel_id=1, source_target_pairs={{0,1},{1,0},{2,3},{3,2},{4,5},{5,4},{6,7},{7,6},{8,9},{9,8},{10,11... | collective-permute-start | bytes 245768 | tf_op jit(solution)/shard_map/scatter/ppermute | solution.py:30
  (6 other events, 6.9 us)

commit v3 on v2

--- a/solution.py
+++ b/solution.py
@@ -256,7 +256,7 @@
         pieces += [(8 * k, up), (8 * (8 - k), down)]
         if k == 2:
             up, ahead, behind = lax.optimization_barrier((up, ahead, behind))
-    pieces += [(80, ahead), (112, behind), (96, shift_x(ahead[:8], 1)), (104, shift_x(behind[8:], -1))]
+    pieces += [(80, ahead), (112, behind), (96, shift_x(ahead, 1))]
     pieces += [(32, shift_z(up[:4], 1)), (36, shift_z(down[4:], -1))]
     return pieces
 

time: 165 us -> 158 us (0.958)
  local copies, waits for them, and re-layouts: 14 us -> 7.28 us
  waiting for transfers between devices: 60.3 us -> 64.8 us
  starting transfers between devices: 71.4 us -> 67.6 us
    ppermute x16, waiting for transfers between devices: 6.12 us -> 13.2 us  [shift_z(): return lax.ppermute(value, 'z', [(i, (i + k) % NZ) for i in range(NZ)])]
    unnamed x28 -> x18, local copies, waits for them, and re-layouts: 8.35 us -> 4.85 us
    ppermute x10 -> x9, waiting for transfers between devices: 12.4 us -> 9.13 us  [shift_x(): return lax.ppermute(value, 'x', [(i, (i + k) % NX) for i in range(NX)])]
    slice x2 -> x0, local copies, waits for them, and re-layouts: 2.37 us -> none  [the longest x1 1.66 us: gather_features(): ahead[:8]]
    ppermute x10 -> x9, starting transfers between devices: 10.6 us -> 8.88 us  [shift_x(): return lax.ppermute(value, 'x', [(i, (i + k) % NX) for i in range(NX)])]
  transfers between devices with their start and end apart: 42 -> 41, of which waited for: 23 -> 23; matrix products, arithmetic and copies ran while one was open for 6% -> 4% of each run, Pallas kernels for 3% -> 3%
where the time goes in v3:
time: 158 us
  starting transfers between devices  67.6 us (43%)
  waiting for transfers between devices  64.8 us (41%)
  Pallas kernels  13.3 us (8%)
  local copies, waits for them, and re-layouts  7.28 us (5%)
  other arithmetic  4.08 us (3%)
    ppermute x15, waiting for transfers between devices, swap(): return lax.ppermute(value, axes, pairs)  38 us
    ppermute x15, starting transfers between devices, swap(): return lax.ppermute(value, axes, pairs)  32.2 us
    ppermute x16, starting transfers between devices, shift_z(): return lax.ppermute(value, 'z', [(i, (i + k) % NZ) for i in range(NZ)])  18.1 us
    ppermute x16, waiting for transfers between devices, shift_z(): return lax.ppermute(value, 'z', [(i, (i + k) % NZ) for i in range(NZ)])  13.2 us
    ppermute x9, waiting for transfers between devices, shift_x(): return lax.ppermute(value, 'x', [(i, (i + k) % NX) for i in range(NX)])  9.13 us
    ppermute x9, starting transfers between devices, shift_x(): return lax.ppermute(value, 'x', [(i, (i + k) % NX) for i in range(NX)])  8.88 us
    all_to_all x1, starting transfers between devices, gather_features(): line = lax.all_to_all(spread, 'z', 0, 0, tiled=True)  8.37 us
    pallas_call x1, Pallas kernels, backward(): pl.pallas_call(functools.partial(backward_kernel, places), out_shape=tupl...  5.14 us
  transfers between devices with their start and end apart: 41, of which 23 were waited for; matrix products, arithmetic and copies ran while one was open for 4% of the time, Pallas kernels for 3%

profile of v3, /device:TPU:1, one launch (start us, length us, event | category | flops | bytes accessed | tf_op | source)
XLA Modules:
  0.0 158.0 jit_solution(2472188271072268724)
XLA Ops:
  0.6 3.8 %collective-permute-start = (bf16[2,128,128]{2,1,0:T(8,128)(2,1)}, bf16[2,128,128]{2,1,0:T(8,128)(2,1)S(1)}, u32[]{:S(2)}, u32[]{:S(2)}) collective-permute-start(bf16[2,128,128]{2,1,0:T(8,128)(2,1)} %bitcast.44), channel_id=1, source_target_pairs={{0,4},{4,0},{1,5},{5,1},{2,6},{6,2},{3,7},{7,3},{8,12},{12,8},{9,1... | collective-permute-start | bytes 196616 | tf_op jit(solution)/shard_map/gather/ppermute | solution.py:30
  4.5 1.9 %collective-permute-done = bf16[2,128,128]{2,1,0:T(8,128)(2,1)S(1)} collective-permute-done((bf16[2,128,128]{2,1,0:T(8,128)(2,1)}, bf16[2,128,128]{2,1,0:T(8,128)(2,1)S(1)}, u32[]{:S(2)}, u32[]{:S(2)}) %collective-permute-start) | collective-permute-done | bytes 65568 | tf_op jit(solution)/shard_map/gather/ppermute | solution.py:30
  6.3 0.9 broadcast_in_dim.2
  7.2 8.4 %all-to-all-start = ((bf16[16,128,128]{2,1,0:T(8,128)(2,1)}), bf16[16,128,128]{2,1,0:T(8,128)(2,1)S(1)}, u32[]{:S(2)}, u32[]{:S(2)}) async-start(bf16[16,128,128]{2,1,0:T(8,128)(2,1)} %bitcast.3), calls=%async_computation | async-start | bytes 1048576 | tf_op jit(solution)/shard_map/gather/all_to_all | solution.py:250
  15.6 2.5 %collective-permute-start.3 = (bf16[2,128,128]{2,1,0:T(8,128)(2,1)}, bf16[2,128,128]{2,1,0:T(8,128)(2,1)S(1)}, u32[]{:S(2)}, u32[]{:S(2)}) collective-permute-start(bf16[2,128,128]{2,1,0:T(8,128)(2,1)} %bitcast.45), channel_id=1, source_target_pairs={{0,192},{64,0},{128,64},{192,128},{1,193},{65,1},{129,65},{193,129... | collective-permute-start | bytes 196616 | tf_op jit(solution)/shard_map/gather/ppermute | solution.py:21
  20.1 3.5 %collective-permute-done.1 = bf16[2,128,128]{2,1,0:T(8,128)(2,1)S(1)} collective-permute-done((bf16[2,128,128]{2,1,0:T(8,128)(2,1)}, bf16[2,128,128]{2,1,0:T(8,128)(2,1)S(1)}, u32[]{:S(2)}, u32[]{:S(2)}) %collective-permute-start.1) | collective-permute-done | bytes 65568 | tf_op jit(solution)/shard_map/gather/ppermute | solution.py:21
  23.7 3.0 %collective-permute-start.5 = (bf16[8,128,128]{2,1,0:T(8,128)(2,1)S(1)}, bf16[8,128,128]{2,1,0:T(8,128)(2,1)S(1)}, u32[]{:S(2)}, u32[]{:S(2)}) collective-permute-start(bf16[8,128,128]{2,1,0:T(8,128)(2,1)S(1)} %constant_dynamic-update-slice_fusion.rest_0_), channel_id=1, source_target_pairs={{0,56},{8,0},{16,8},{24,16},{32,24},{40,32},{48,40},{56,48},{1,57}... | collective-permute-start | bytes 786440 | tf_op jit(solution)/shard_map/gather/ppermute | solution.py:25
  26.7 4.5 %all-to-all-done.rest_1_ = bf16[16,128,128]{2,1,0:T(8,128)(2,1)S(1)} async-done(((bf16[16,128,128]{2,1,0:T(8,128)(2,1)}), bf16[16,128,128]{2,1,0:T(8,128)(2,1)S(1)}, u32[]{:S(2)}, u32[]{:S(2)}) %all-to-all-start) | async-done | bytes 524320 | tf_op jit(solution)/shard_map/gather/all_to_all | solution.py:250
  31.3 2.5 %collective-permute-start.9 = (bf16[16,128,128]{2,1,0:T(8,128)(2,1)S(1)}, bf16[16,128,128]{2,1,0:T(8,128)(2,1)S(1)}, u32[]{:S(2)}, u32[]{:S(2)}) collective-permute-start(bf16[16,128,128]{2,1,0:T(8,128)(2,1)S(1)} %all-to-all-done.rest_1_), channel_id=1, source_target_pairs={{0,192},{64,0},{128,64},{192,128},{1,193},{65,1},{129,65},{193,129... | collective-permute-start | bytes 1572872 | tf_op jit(solution)/shard_map/gather/ppermute | solution.py:21
  34.1 1.6 collective-permute-start.7
  35.7 4.0 %collective-permute-done.7.rest_5_ = bf16[8,128,128]{2,1,0:T(8,128)(2,1)} collective-permute-done((bf16[8,128,128]{2,1,0:T(8,128)(2,1)S(1)}, bf16[8,128,128]{2,1,0:T(8,128)(2,1)}, u32[]{:S(2)}, u32[]{:S(2)}) %collective-permute-start.7) | collective-permute-done | bytes 262176 | tf_op jit(solution)/shard_map/gather/ppermute | solution.py:25
  39.6 2.8 %collective-permute-start.11 = (bf16[8,128,128]{2,1,0:T(8,128)(2,1)}, bf16[8,128,128]{2,1,0:T(8,128)(2,1)S(1)}, u32[]{:S(2)}, u32[]{:S(2)}) collective-permute-start(bf16[8,128,128]{2,1,0:T(8,128)(2,1)} %collective-permute-done.7.rest_5_), channel_id=1, source_target_pairs={{0,56},{8,0},{16,8},{24,16},{32,24},{40,32},{48,40},{56,48},{1,57}... | collective-permute-start | bytes 786440 | tf_op jit(solution)/shard_map/gather/ppermute | solution.py:25
  42.4 1.7 %collective-permute-done.8.rest_8_ = bf16[16,128,128]{2,1,0:T(8,128)(2,1)S(1)} collective-permute-done((bf16[16,128,128]{2,1,0:T(8,128)(2,1)S(1)}, bf16[16,128,128]{2,1,0:T(8,128)(2,1)S(1)}, u32[]{:S(2)}, u32[]{:S(2)}) %collective-permute-start.8) | collective-permute-done | bytes 524320 | tf_op jit(solution)/shard_map/gather/ppermute | solution.py:21
  44.7 1.3 reduce.3
  47.6 2.1 %collective-permute-start.14 = (bf16[4,128,128]{2,1,0:T(8,128)(2,1)}, bf16[4,128,128]{2,1,0:T(8,128)(2,1)S(1)}, u32[]{:S(2)}, u32[]{:S(2)}) collective-permute-start(bf16[4,128,128]{2,1,0:T(8,128)(2,1)} %slice.166), channel_id=1, source_target_pairs={{0,56},{8,0},{16,8},{24,16},{32,24},{40,32},{48,40},{56,48},{1,57}... | collective-permute-start | bytes 393224 | tf_op jit(solution)/shard_map/gather/ppermute | solution.py:25
  49.7 1.1 collective-permute-done.10.rest_6_
  52.2 1.3 collective-permute-done.14.rest_12_
  53.5 4.6 %collective-permute-done.13.rest_11_ = bf16[4,128,128]{2,1,0:T(8,128)(2,1)} collective-permute-done((bf16[4,128,128]{2,1,0:T(8,128)(2,1)}, bf16[4,128,128]{2,1,0:T(8,128)(2,1)}, u32[]{:S(2)}, u32[]{:S(2)}) %collective-permute-start.13) | collective-permute-done | bytes 131104 | tf_op jit(solution)/shard_map/gather/ppermute | solution.py:25
  58.1 2.8 %copy-done = bf16[8,1,24,128,128]{4,3,2,1,0:T(8,128)(2,1)S(1)} copy-done((bf16[8,1,24,128,128]{4,3,2,1,0:T(8,128)(2,1)S(1)}, bf16[8,1,24,128,128]{4,3,2,1,0:T(8,128)(2,1)}, u32[]{:S(2)}) %copy-start) | copy-done | bytes 6291480
  60.9 4.8 %forward.1 = (bf16[2,128,128]{2,1,0:T(8,128)(2,1)S(1)}, bf16[2,128,128]{2,1,0:T(8,128)(2,1)S(1)}, bf16[2,128,128]{2,1,0:T(8,128)(2,1)S(1)}, bf16[2,128,128]{2,1,0:T(8,128)(2,1)S(1)}) custom-call(s32[1]{0:T(128)} %bitcast.rep_ref, s32[200]{0:T(256)S(1)} %get-tuple-element.110.meta_ref, bf16[8,1,24,128,128]{4,3,2,1,0:T(8,128)(2,1)S(1)} %copy-done, ...), custom_call_target="tpu_custom_call" | custom-call | flops 805306368 | bytes 11534336 | tf_op jit(solution)/shard_map/forward/pallas_call | solution.py:100
  65.7 7.3 %collective-permute-start.15 = (bf16[2,128,128]{2,1,0:T(8,128)(2,1)S(1)}, bf16[2,128,128]{2,1,0:T(8,128)(2,1)S(1)}, u32[]{:S(2)}, u32[]{:S(2)}) collective-permute-start(bf16[2,128,128]{2,1,0:T(8,128)(2,1)S(1)} %get-tuple-element.51), channel_id=1, source_target_pairs={{0,1},{1,0},{2,3},{3,2},{4,5},{5,4},{6,7},{7,6},{8,9},{9,8},{10,11... | collective-permute-start | bytes 196616 | tf_op jit(solution)/shard_map/sections/ppermute | solution.py:30
  73.0 1.3 collective-permute-start.16
  74.8 1.9 %collective-permute-done.16.p2 = bf16[2,128,128]{2,1,0:T(8,128)(2,1)S(1)} collective-permute-done((bf16[2,128,128]{2,1,0:T(8,128)(2,1)S(1)}, bf16[2,128,128]{2,1,0:T(8,128)(2,1)S(1)}, u32[]{:S(2)}, u32[]{:S(2)}) %collective-permute-start.16) | collective-permute-done | bytes 65568 | tf_op jit(solution)/shard_map/sections/ppermute | solution.py:30
  76.7 1.7 %collective-permute-done.17.p3 = bf16[2,128,128]{2,1,0:T(8,128)(2,1)S(1)} collective-permute-done((bf16[2,128,128]{2,1,0:T(8,128)(2,1)S(1)}, bf16[2,128,128]{2,1,0:T(8,128)(2,1)S(1)}, u32[]{:S(2)}, u32[]{:S(2)}) %collective-permute-start.17) | collective-permute-done | bytes 65568 | tf_op jit(solution)/shard_map/sections/ppermute | solution.py:30
  78.4 1.6 middle.1
  80.4 1.2 collective-permute-start.20
  82.5 1.1 collective-permute-start.22
  83.6 0.9 collective-permute-done.20.s3
  84.5 1.0 collective-permute-done.19.s2
  85.6 5.1 %backward.1 = (bf16[8,128,128]{2,1,0:T(8,128)(2,1)S(1)}, bf16[8,128,128]{2,1,0:T(8,128)(2,1)S(1)}, bf16[8,128,128]{2,1,0:T(8,128)(2,1)S(1)}, bf16[8,128,128]{2,1...) custom-call(s32[1]{0:T(128)} %bitcast.rep_ref, ...), custom_call_target="tpu_custom_call" | custom-call | flops 805306368 | bytes 15728640 | tf_op jit(solution)/shard_map/backward/pallas_call | solution.py:202
  90.8 2.8 %collective-permute-start.23 = (bf16[1184,128]{1,0:T(8,128)(2,1)S(1)}, bf16[1184,128]{1,0:T(8,128)(2,1)S(1)}, u32[]{:S(2)}, u32[]{:S(2)}) collective-permute-start(bf16[1184,128]{1,0:T(8,128)(2,1)S(1)} %pad_maximum_fusion), channel_id=1, source_target_pairs={{0,4},{4,0},{1,5},{5,1},{2,6},{6,2},{3,7},{7,3},{8,12},{12,8},{9,1... | collective-permute-start | bytes 909320 | tf_op jit(solution)/shard_map/scatter/ppermute | solution.py:30
  93.8 6.1 %collective-permute-done.23 = bf16[1184,128]{1,0:T(8,128)(2,1)S(1)} collective-permute-done((bf16[1184,128]{1,0:T(8,128)(2,1)S(1)}, bf16[1184,128]{1,0:T(8,128)(2,1)S(1)}, u32[]{:S(2)}, u32[]{:S(2)}) %collective-permute-start.23) | collective-permute-done | bytes 303136 | tf_op jit(solution)/shard_map/scatter/ppermute | solution.py:30
  100.2 1.5 collective-permute-start.24
  101.7 2.4 %collective-permute-start.29 = (bf16[2048,128]{1,0:T(8,128)(2,1)S(1)}, bf16[2048,128]{1,0:T(8,128)(2,1)S(1)}, u32[]{:S(2)}, u32[]{:S(2)}) collective-permute-start(bf16[2048,128]{1,0:T(8,128)(2,1)S(1)} %bitcast.40), channel_id=1, source_target_pairs={{0,4},{4,0},{1,5},{5,1},{2,6},{6,2},{3,7},{7,3},{8,12},{12,8},{9,1... | collective-permute-start | bytes 1572872 | tf_op jit(solution)/shard_map/scatter/ppermute | solution.py:30
  104.1 7.1 %collective-permute-done.26 = bf16[2048,128]{1,0:T(8,128)(2,1)S(1)} collective-permute-done((bf16[2048,128]{1,0:T(8,128)(2,1)S(1)}, bf16[2048,128]{1,0:T(8,128)(2,1)S(1)}, u32[]{:S(2)}, u32[]{:S(2)}) %collective-permute-start.26) | collective-permute-done | bytes 524320 | tf_op jit(solution)/shard_map/scatter/ppermute | solution.py:30
  111.6 2.7 %collective-permute-start.28 = (bf16[1184,128]{1,0:T(8,128)(2,1)S(1)}, bf16[1184,128]{1,0:T(8,128)(2,1)S(1)}, u32[]{:S(2)}, u32[]{:S(2)}) collective-permute-start(bf16[1184,128]{1,0:T(8,128)(2,1)S(1)} %pad_maximum_fusion.2), channel_id=1, source_target_pairs={{0,56},{8,0},{16,8},{24,16},{32,24},{40,32},{48,40},{56,48},{1,57}... | collective-permute-start | bytes 909320 | tf_op jit(solution)/shard_map/scatter/ppermute | solution.py:25
  114.4 2.4 %collective-permute-start.32 = (bf16[2048,128]{1,0:T(8,128)(2,1)S(1)}, bf16[2048,128]{1,0:T(8,128)(2,1)S(1)}, u32[]{:S(2)}, u32[]{:S(2)}) collective-permute-start(bf16[2048,128]{1,0:T(8,128)(2,1)S(1)} %bitcast.39), channel_id=1, source_target_pairs={{0,4},{4,0},{1,5},{5,1},{2,6},{6,2},{3,7},{7,3},{8,12},{12,8},{9,1... | collective-permute-start | bytes 1572872 | tf_op jit(solution)/shard_map/scatter/ppermute | solution.py:30
  116.8 5.6 %collective-permute-done.29 = bf16[2048,128]{1,0:T(8,128)(2,1)S(1)} collective-permute-done((bf16[2048,128]{1,0:T(8,128)(2,1)S(1)}, bf16[2048,128]{1,0:T(8,128)(2,1)S(1)}, u32[]{:S(2)}, u32[]{:S(2)}) %collective-permute-start.29) | collective-permute-done | bytes 524320 | tf_op jit(solution)/shard_map/scatter/ppermute | solution.py:30
  122.8 1.5 collective-permute-start.30
  124.4 9.3 %collective-permute-done.32 = bf16[2048,128]{1,0:T(8,128)(2,1)S(1)} collective-permute-done((bf16[2048,128]{1,0:T(8,128)(2,1)S(1)}, bf16[2048,128]{1,0:T(8,128)(2,1)S(1)}, u32[]{:S(2)}, u32[]{:S(2)}) %collective-permute-start.32) | collective-permute-done | bytes 524320 | tf_op jit(solution)/shard_map/scatter/ppermute | solution.py:30
  134.0 2.5 %collective-permute-start.35 = (bf16[1024,128]{1,0:T(8,128)(2,1)S(1)}, bf16[1024,128]{1,0:T(8,128)(2,1)S(1)}, u32[]{:S(2)}, u32[]{:S(2)}) collective-permute-start(bf16[1024,128]{1,0:T(8,128)(2,1)S(1)} %bitcast.42), channel_id=1, source_target_pairs={{0,4},{4,0},{1,5},{5,1},{2,6},{6,2},{3,7},{7,3},{8,12},{12,8},{9,1... | collective-permute-start | bytes 786440 | tf_op jit(solution)/shard_map/scatter/ppermute | solution.py:30
  136.6 2.6 %collective-permute-start.34 = (bf16[1024,128]{1,0:T(8,128)(2,1)S(1)}, bf16[1024,128]{1,0:T(8,128)(2,1)S(1)}, u32[]{:S(2)}, u32[]{:S(2)}) collective-permute-start(bf16[1024,128]{1,0:T(8,128)(2,1)S(1)} %get-tuple-element.93), channel_id=1, source_target_pairs={{0,56},{8,0},{16,8},{24,16},{32,24},{40,32},{48,40},{56,48},{1,57}... | collective-permute-start | bytes 786440 | tf_op jit(solution)/shard_map/scatter/ppermute | solution.py:25
  139.1 2.2 %collective-permute-done.35 = bf16[1024,128]{1,0:T(8,128)(2,1)S(1)} collective-permute-done((bf16[1024,128]{1,0:T(8,128)(2,1)S(1)}, bf16[1024,128]{1,0:T(8,128)(2,1)S(1)}, u32[]{:S(2)}, u32[]{:S(2)}) %collective-permute-start.35) | collective-permute-done | bytes 262176 | tf_op jit(solution)/shard_map/scatter/ppermute | solution.py:30
  141.4 1.1 collective-permute-done.34
  143.2 2.3 %collective-permute-start.38 = (bf16[416,128]{1,0:T(8,128)(2,1)S(1)}, bf16[416,128]{1,0:T(8,128)(2,1)S(1)}, u32[]{:S(2)}, u32[]{:S(2)}) collective-permute-start(bf16[416,128]{1,0:T(8,128)(2,1)S(1)} %get-tuple-element.106), channel_id=1, source_target_pairs={{0,192},{64,0},{128,64},{192,128},{1,193},{65,1},{129,65},{193,129... | collective-permute-start | bytes 319496 | tf_op jit(solution)/shard_map/scatter/ppermute | solution.py:21
  145.5 3.2 %collective-permute-done.36 = bf16[416,128]{1,0:T(8,128)(2,1)S(1)} collective-permute-done((bf16[416,128]{1,0:T(8,128)(2,1)S(1)}, bf16[416,128]{1,0:T(8,128)(2,1)S(1)}, u32[]{:S(2)}, u32[]{:S(2)}) %collective-permute-start.36) | collective-permute-done | bytes 106528 | tf_op jit(solution)/shard_map/scatter/ppermute | solution.py:21
  149.4 5.3 %collective-permute-start.39 = (f32[160,128]{1,0:T(8,128)S(1)}, f32[160,128]{1,0:T(8,128)S(1)}, u32[]{:S(2)}, u32[]{:S(2)}) collective-permute-start(f32[160,128]{1,0:T(8,128)S(1)} %convert_add_fusion.8.mine_ref), channel_id=1, source_target_pairs={{0,1},{1,0},{2,3},{3,2},{4,5},{5,4},{6,7},{7,6},{8,9},{9,8},{10,11... | collective-permute-start | bytes 245768 | tf_op jit(solution)/shard_map/scatter/ppermute | solution.py:30
  156.2 1.8 %last.1 = (bf16[1,256,128]{2,1,0:T(8,128)(2,1)}, f32[128,256]{1,0:T(8,128)}, f32[1,256]{1,0:T(1,128)}) custom-call(s32[1]{0:T(128)} %bitcast.rep_ref, f32[2,128,128]{2,1,0:T(8,128)} %bitcast.43, f32[160,128]{1,0:T(8,128)} %copy-done.5, f32[160,128]{1,0:T(8,128)} %copy-done.6), custom_call_target="tpu_custom_call" | custom-call | tf_op jit(solution)/shard_map/last/pallas_call | solution.py:233
  (95 shorter events, 12.2 us)
Async XLA Ops:
  0.6 5.7 %collective-permute-start = (bf16[2,128,128]{2,1,0:T(8,128)(2,1)}, bf16[2,128,128]{2,1,0:T(8,128)(2,1)S(1)}, u32[]{:S(2)}, u32[]{:S(2)}) collective-permute-start(bf16[2,128,128]{2,1,0:T(8,128)(2,1)} %bitcast.44), channel_id=1, source_target_pairs={{0,4},{4,0},{1,5},{5,1},{2,6},{6,2},{3,7},{7,3},{8,12},{12,8},{9,1... | collective-permute-start | bytes 196616 | tf_op jit(solution)/shard_map/gather/ppermute | solution.py:30
  7.2 71.2 %copy-start.4 = (f32[256]{0:T(256)S(1)}, f32[256]{0:T(256)}, u32[]{:S(2)}) copy-start(f32[256]{0:T(256)} %param.9) | copy-start | bytes 3076
  7.2 24.0 %all-to-all-start = ((bf16[16,128,128]{2,1,0:T(8,128)(2,1)}), bf16[16,128,128]{2,1,0:T(8,128)(2,1)S(1)}, u32[]{:S(2)}, u32[]{:S(2)}) async-start(bf16[16,128,128]{2,1,0:T(8,128)(2,1)} %bitcast.3), calls=%async_computation | async-start | bytes 1048576 | tf_op jit(solution)/shard_map/gather/all_to_all | solution.py:250
  15.6 8.1 %collective-permute-start.3 = (bf16[2,128,128]{2,1,0:T(8,128)(2,1)}, bf16[2,128,128]{2,1,0:T(8,128)(2,1)S(1)}, u32[]{:S(2)}, u32[]{:S(2)}) collective-permute-start(bf16[2,128,128]{2,1,0:T(8,128)(2,1)} %bitcast.45), channel_id=1, source_target_pairs={{0,192},{64,0},{128,64},{192,128},{1,193},{65,1},{129,65},{193,129... | collective-permute-start | bytes 196616 | tf_op jit(solution)/shard_map/gather/ppermute | solution.py:21
  18.1 5.5 %collective-permute-start.2 = (bf16[2,128,128]{2,1,0:T(8,128)(2,1)}, bf16[2,128,128]{2,1,0:T(8,128)(2,1)S(1)}, u32[]{:S(2)}, u32[]{:S(2)}) collective-permute-start(bf16[2,128,128]{2,1,0:T(8,128)(2,1)} %bitcast.46), channel_id=1, source_target_pairs={{0,128},{64,192},{128,0},{192,64},{1,129},{65,193},{129,1},{193,65... | collective-permute-start | bytes 196616 | tf_op jit(solution)/shard_map/gather/ppermute | solution.py:21
  18.6 5.0 %collective-permute-start.1 = (bf16[2,128,128]{2,1,0:T(8,128)(2,1)}, bf16[2,128,128]{2,1,0:T(8,128)(2,1)S(1)}, u32[]{:S(2)}, u32[]{:S(2)}) collective-permute-start(bf16[2,128,128]{2,1,0:T(8,128)(2,1)} %bitcast.47), channel_id=1, source_target_pairs={{0,64},{64,128},{128,192},{192,0},{1,65},{65,129},{129,193},{193,1... | collective-permute-start | bytes 196616 | tf_op jit(solution)/shard_map/gather/ppermute | solution.py:21
  23.7 10.4 %collective-permute-start.5 = (bf16[8,128,128]{2,1,0:T(8,128)(2,1)S(1)}, bf16[8,128,128]{2,1,0:T(8,128)(2,1)S(1)}, u32[]{:S(2)}, u32[]{:S(2)}) collective-permute-start(bf16[8,128,128]{2,1,0:T(8,128)(2,1)S(1)} %constant_dynamic-update-slice_fusion.rest_0_), channel_id=1, source_target_pairs={{0,56},{8,0},{16,8},{24,16},{32,24},{40,32},{48,40},{56,48},{1,57}... | collective-permute-start | bytes 786440 | tf_op jit(solution)/shard_map/gather/ppermute | solution.py:25
  26.7 8.9 %collective-permute-start.4 = (bf16[8,128,128]{2,1,0:T(8,128)(2,1)S(1)}, bf16[8,128,128]{2,1,0:T(8,128)(2,1)S(1)}, u32[]{:S(2)}, u32[]{:S(2)}) collective-permute-start(bf16[8,128,128]{2,1,0:T(8,128)(2,1)S(1)} %constant_dynamic-update-slice_fusion.rest_0_), channel_id=1, source_target_pairs={{0,8},{8,16},{16,24},{24,32},{32,40},{40,48},{48,56},{56,0},{1,9},... | collective-permute-start | bytes 786440 | tf_op jit(solution)/shard_map/gather/ppermute | solution.py:25
  31.3 11.1 %collective-permute-start.9 = (bf16[16,128,128]{2,1,0:T(8,128)(2,1)S(1)}, bf16[16,128,128]{2,1,0:T(8,128)(2,1)S(1)}, u32[]{:S(2)}, u32[]{:S(2)}) collective-permute-start(bf16[16,128,128]{2,1,0:T(8,128)(2,1)S(1)} %all-to-all-done.rest_1_), channel_id=1, source_target_pairs={{0,192},{64,0},{128,64},{192,128},{1,193},{65,1},{129,65},{193,129... | collective-permute-start | bytes 1572872 | tf_op jit(solution)/shard_map/gather/ppermute | solution.py:21
  33.8 10.4 %collective-permute-start.8 = (bf16[16,128,128]{2,1,0:T(8,128)(2,1)S(1)}, bf16[16,128,128]{2,1,0:T(8,128)(2,1)S(1)}, u32[]{:S(2)}, u32[]{:S(2)}) collective-permute-start(bf16[16,128,128]{2,1,0:T(8,128)(2,1)S(1)} %all-to-all-done.rest_1_), channel_id=1, source_target_pairs={{0,64},{64,128},{128,192},{192,0},{1,65},{65,129},{129,193},{193,1... | collective-permute-start | bytes 1572872 | tf_op jit(solution)/shard_map/gather/ppermute | solution.py:21
  34.1 5.5 %collective-permute-start.7 = (bf16[8,128,128]{2,1,0:T(8,128)(2,1)S(1)}, bf16[8,128,128]{2,1,0:T(8,128)(2,1)}, u32[]{:S(2)}, u32[]{:S(2)}) collective-permute-start(bf16[8,128,128]{2,1,0:T(8,128)(2,1)S(1)} %collective-permute-done.5.rest_3_), channel_id=1, source_target_pairs={{0,56},{8,0},{16,8},{24,16},{32,24},{40,32},{48,40},{56,48},{1,57}... | collective-permute-start | bytes 786440 | tf_op jit(solution)/shard_map/gather/ppermute | solution.py:25
  35.7 6.7 %collective-permute-start.6 = (bf16[8,128,128]{2,1,0:T(8,128)(2,1)S(1)}, bf16[8,128,128]{2,1,0:T(8,128)(2,1)}, u32[]{:S(2)}, u32[]{:S(2)}) collective-permute-start(bf16[8,128,128]{2,1,0:T(8,128)(2,1)S(1)} %collective-permute-done.4.rest_2_), channel_id=1, source_target_pairs={{0,8},{8,16},{16,24},{24,32},{32,40},{40,48},{48,56},{56,0},{1,9},... | collective-permute-start | bytes 786440 | tf_op jit(solution)/shard_map/gather/ppermute | solution.py:25
  39.6 7.3 %collective-permute-start.11 = (bf16[8,128,128]{2,1,0:T(8,128)(2,1)}, bf16[8,128,128]{2,1,0:T(8,128)(2,1)S(1)}, u32[]{:S(2)}, u32[]{:S(2)}) collective-permute-start(bf16[8,128,128]{2,1,0:T(8,128)(2,1)} %collective-permute-done.7.rest_5_), channel_id=1, source_target_pairs={{0,56},{8,0},{16,8},{24,16},{32,24},{40,32},{48,40},{56,48},{1,57}... | collective-permute-start | bytes 786440 | tf_op jit(solution)/shard_map/gather/ppermute | solution.py:25
  44.1 6.6 %collective-permute-start.10 = (bf16[8,128,128]{2,1,0:T(8,128)(2,1)}, bf16[8,128,128]{2,1,0:T(8,128)(2,1)S(1)}, u32[]{:S(2)}, u32[]{:S(2)}) collective-permute-start(bf16[8,128,128]{2,1,0:T(8,128)(2,1)} %collective-permute-done.6.rest_4_), channel_id=1, source_target_pairs={{0,8},{8,16},{16,24},{24,32},{32,40},{40,48},{48,56},{56,0},{1,9},... | collective-permute-start | bytes 786440 | tf_op jit(solution)/shard_map/gather/ppermute | solution.py:25
  46.1 12.1 %collective-permute-start.12 = (bf16[16,128,128]{2,1,0:T(8,128)(2,1)S(1)}, bf16[16,128,128]{2,1,0:T(8,128)(2,1)S(1)}, u32[]{:S(2)}, u32[]{:S(2)}) collective-permute-start(bf16[16,128,128]{2,1,0:T(8,128)(2,1)S(1)} %collective-permute-done.8.rest_8_), channel_id=1, source_target_pairs={{0,64},{64,128},{128,192},{192,0},{1,65},{65,129},{129,193},{193,1... | collective-permute-start | bytes 1572872 | tf_op jit(solution)/shard_map/gather/ppermute | solution.py:21
  47.6 5.9 %collective-permute-start.14 = (bf16[4,128,128]{2,1,0:T(8,128)(2,1)}, bf16[4,128,128]{2,1,0:T(8,128)(2,1)S(1)}, u32[]{:S(2)}, u32[]{:S(2)}) collective-permute-start(bf16[4,128,128]{2,1,0:T(8,128)(2,1)} %slice.166), channel_id=1, source_target_pairs={{0,56},{8,0},{16,8},{24,16},{32,24},{40,32},{48,40},{56,48},{1,57}... | collective-permute-start | bytes 393224 | tf_op jit(solution)/shard_map/gather/ppermute | solution.py:25
  51.5 6.7 %collective-permute-start.13 = (bf16[4,128,128]{2,1,0:T(8,128)(2,1)}, bf16[4,128,128]{2,1,0:T(8,128)(2,1)}, u32[]{:S(2)}, u32[]{:S(2)}) collective-permute-start(bf16[4,128,128]{2,1,0:T(8,128)(2,1)} %slice.165), channel_id=1, source_target_pairs={{0,8},{8,16},{16,24},{24,32},{32,40},{40,48},{48,56},{56,0},{1,9},... | collective-permute-start | bytes 393224 | tf_op jit(solution)/shard_map/gather/ppermute | solution.py:25
  58.1 2.8 %copy-start = (bf16[8,1,24,128,128]{4,3,2,1,0:T(8,128)(2,1)S(1)}, bf16[8,1,24,128,128]{4,3,2,1,0:T(8,128)(2,1)}, u32[]{:S(2)}) copy-start(bf16[8,1,24,128,128]{4,3,2,1,0:T(8,128)(2,1)} %edges.3) | copy-start | bytes 18874372
  60.9 17.5 %copy-start.2 = (bf16[256,256]{1,0:T(8,128)(2,1)S(1)}, bf16[256,256]{1,0:T(8,128)(2,1)}, u32[]{:S(2)}) copy-start(bf16[256,256]{1,0:T(8,128)(2,1)} %cot_ref.1) | copy-start | bytes 393220
  60.9 17.5 %copy-start.3 = (bf16[128,256]{1,0:T(8,128)(2,1)S(1)}, bf16[128,256]{1,0:T(8,128)(2,1)}, u32[]{:S(2)}) copy-start(bf16[128,256]{1,0:T(8,128)(2,1)} %weight_ref.1) | copy-start | bytes 196612
  60.9 24.6 %copy-start.1 = (bf16[8,1,24,128,128]{4,3,2,1,0:T(8,128)(2,1)S(1)}, bf16[8,1,24,128,128]{4,3,2,1,0:T(8,128)(2,1)}, u32[]{:S(2)}) copy-start(bf16[8,1,24,128,128]{4,3,2,1,0:T(8,128)(2,1)} %edges.3) | copy-start | bytes 18874372
  65.7 9.1 %collective-permute-start.15 = (bf16[2,128,128]{2,1,0:T(8,128)(2,1)S(1)}, bf16[2,128,128]{2,1,0:T(8,128)(2,1)S(1)}, u32[]{:S(2)}, u32[]{:S(2)}) collective-permute-start(bf16[2,128,128]{2,1,0:T(8,128)(2,1)S(1)} %get-tuple-element.51), channel_id=1, source_target_pairs={{0,1},{1,0},{2,3},{3,2},{4,5},{5,4},{6,7},{7,6},{8,9},{9,8},{10,11... | collective-permute-start | bytes 196616 | tf_op jit(solution)/shard_map/sections/ppermute | solution.py:30
  73.0 3.7 %collective-permute-start.16 = (bf16[2,128,128]{2,1,0:T(8,128)(2,1)S(1)}, bf16[2,128,128]{2,1,0:T(8,128)(2,1)S(1)}, u32[]{:S(2)}, u32[]{:S(2)}) collective-permute-start(bf16[2,128,128]{2,1,0:T(8,128)(2,1)S(1)} %get-tuple-element.52), channel_id=1, source_target_pairs={{0,2},{2,0},{1,3},{3,1},{4,6},{6,4},{5,7},{7,5},{8,10},{10,8},{9,1... | collective-permute-start | bytes 196616 | tf_op jit(solution)/shard_map/sections/ppermute | solution.py:30
  74.4 4.1 %collective-permute-start.17 = (bf16[2,128,128]{2,1,0:T(8,128)(2,1)S(1)}, bf16[2,128,128]{2,1,0:T(8,128)(2,1)S(1)}, u32[]{:S(2)}, u32[]{:S(2)}) collective-permute-start(bf16[2,128,128]{2,1,0:T(8,128)(2,1)S(1)} %get-tuple-element.53), channel_id=1, source_target_pairs={{0,3},{1,2},{2,1},{3,0},{4,7},{5,6},{6,5},{7,4},{8,11},{9,10},{10,... | collective-permute-start | bytes 196616 | tf_op jit(solution)/shard_map/sections/ppermute | solution.py:30
  80.0 2.5 %collective-permute-start.21 = (f32[160,128]{1,0:T(8,128)S(1)}, f32[160,128]{1,0:T(8,128)S(1)}, u32[]{:S(2)}, u32[]{:S(2)}) collective-permute-start(f32[160,128]{1,0:T(8,128)S(1)} %get-tuple-element.63), channel_id=1, source_target_pairs={{0,1},{1,0},{2,3},{3,2},{4,5},{5,4},{6,7},{7,6},{8,9},{9,8},{10,11... | collective-permute-start | bytes 245768 | tf_op jit(solution)/shard_map/weights/ppermute | solution.py:30
  80.4 4.2 %collective-permute-start.20 = (bf16[2,128,128]{2,1,0:T(8,128)(2,1)S(1)}, bf16[2,128,128]{2,1,0:T(8,128)(2,1)S(1)}, u32[]{:S(2)}, u32[]{:S(2)}) collective-permute-start(bf16[2,128,128]{2,1,0:T(8,128)(2,1)S(1)} %get-tuple-element.55.s0), channel_id=1, source_target_pairs={{0,3},{1,2},{2,1},{3,0},{4,7},{5,6},{6,5},{7,4},{8,11},{9,10},{10,... | collective-permute-start | bytes 196616 | tf_op jit(solution)/shard_map/slopes/ppermute | solution.py:30
  81.6 4.0 %collective-permute-start.19 = (bf16[2,128,128]{2,1,0:T(8,128)(2,1)S(1)}, bf16[2,128,128]{2,1,0:T(8,128)(2,1)S(1)}, u32[]{:S(2)}, u32[]{:S(2)}) collective-permute-start(bf16[2,128,128]{2,1,0:T(8,128)(2,1)S(1)} %get-tuple-element.55.s0), channel_id=1, source_target_pairs={{0,2},{2,0},{1,3},{3,1},{4,6},{6,4},{5,7},{7,5},{8,10},{10,8},{9,1... | collective-permute-start | bytes 196616 | tf_op jit(solution)/shard_map/slopes/ppermute | solution.py:30
  81.9 3.7 %collective-permute-start.18 = (bf16[2,128,128]{2,1,0:T(8,128)(2,1)S(1)}, bf16[2,128,128]{2,1,0:T(8,128)(2,1)S(1)}, u32[]{:S(2)}, u32[]{:S(2)}) collective-permute-start(bf16[2,128,128]{2,1,0:T(8,128)(2,1)S(1)} %get-tuple-element.55.s0), channel_id=1, source_target_pairs={{0,1},{1,0},{2,3},{3,2},{4,5},{5,4},{6,7},{7,6},{8,9},{9,8},{10,11... | collective-permute-start | bytes 196616 | tf_op jit(solution)/shard_map/slopes/ppermute | solution.py:30
  82.5 8.2 %collective-permute-start.22 = (f32[160,128]{1,0:T(8,128)S(1)}, f32[160,128]{1,0:T(8,128)S(1)}, u32[]{:S(2)}, u32[]{:S(2)}) collective-permute-start(f32[160,128]{1,0:T(8,128)S(1)} %add.175), channel_id=1, source_target_pairs={{0,2},{2,0},{1,3},{3,1},{4,6},{6,4},{5,7},{7,5},{8,10},{10,8},{9,1... | collective-permute-start | bytes 245768 | tf_op jit(solution)/shard_map/weights/ppermute | solution.py:30
  90.8 9.1 %collective-permute-start.23 = (bf16[1184,128]{1,0:T(8,128)(2,1)S(1)}, bf16[1184,128]{1,0:T(8,128)(2,1)S(1)}, u32[]{:S(2)}, u32[]{:S(2)}) collective-permute-start(bf16[1184,128]{1,0:T(8,128)(2,1)S(1)} %pad_maximum_fusion), channel_id=1, source_target_pairs={{0,4},{4,0},{1,5},{5,1},{2,6},{6,2},{3,7},{7,3},{8,12},{12,8},{9,1... | collective-permute-start | bytes 909320 | tf_op jit(solution)/shard_map/scatter/ppermute | solution.py:30
  93.6 17.6 %collective-permute-start.26 = (bf16[2048,128]{1,0:T(8,128)(2,1)S(1)}, bf16[2048,128]{1,0:T(8,128)(2,1)S(1)}, u32[]{:S(2)}, u32[]{:S(2)}) collective-permute-start(bf16[2048,128]{1,0:T(8,128)(2,1)S(1)} %bitcast.41), channel_id=1, source_target_pairs={{0,4},{4,0},{1,5},{5,1},{2,6},{6,2},{3,7},{7,3},{8,12},{12,8},{9,1... | collective-permute-start | bytes 1572872 | tf_op jit(solution)/shard_map/scatter/ppermute | solution.py:30
  100.1 11.1 %collective-permute-start.25 = (bf16[672,128]{1,0:T(8,128)(2,1)S(1)}, bf16[672,128]{1,0:T(8,128)(2,1)S(1)}, u32[]{:S(2)}, u32[]{:S(2)}) collective-permute-start(bf16[672,128]{1,0:T(8,128)(2,1)S(1)} %get-tuple-element.107), channel_id=1, source_target_pairs={{0,56},{8,0},{16,8},{24,16},{32,24},{40,32},{48,40},{56,48},{1,57}... | collective-permute-start | bytes 516104 | tf_op jit(solution)/shard_map/scatter/ppermute | solution.py:25
  100.2 11.0 %collective-permute-start.24 = (bf16[672,128]{1,0:T(8,128)(2,1)S(1)}, bf16[672,128]{1,0:T(8,128)(2,1)S(1)}, u32[]{:S(2)}, u32[]{:S(2)}) collective-permute-start(bf16[672,128]{1,0:T(8,128)(2,1)S(1)} %get-tuple-element.108), channel_id=1, source_target_pairs={{0,8},{8,16},{16,24},{24,32},{32,40},{40,48},{48,56},{56,0},{1,9},... | collective-permute-start | bytes 516104 | tf_op jit(solution)/shard_map/scatter/ppermute | solution.py:25
  101.7 20.8 %collective-permute-start.29 = (bf16[2048,128]{1,0:T(8,128)(2,1)S(1)}, bf16[2048,128]{1,0:T(8,128)(2,1)S(1)}, u32[]{:S(2)}, u32[]{:S(2)}) collective-permute-start(bf16[2048,128]{1,0:T(8,128)(2,1)S(1)} %bitcast.40), channel_id=1, source_target_pairs={{0,4},{4,0},{1,5},{5,1},{2,6},{6,2},{3,7},{7,3},{8,12},{12,8},{9,1... | collective-permute-start | bytes 1572872 | tf_op jit(solution)/shard_map/scatter/ppermute | solution.py:30
  111.5 10.9 %collective-permute-start.27 = (bf16[1184,128]{1,0:T(8,128)(2,1)S(1)}, bf16[1184,128]{1,0:T(8,128)(2,1)S(1)}, u32[]{:S(2)}, u32[]{:S(2)}) collective-permute-start(bf16[1184,128]{1,0:T(8,128)(2,1)S(1)} %pad_maximum_fusion.1), channel_id=1, source_target_pairs={{0,8},{8,16},{16,24},{24,32},{32,40},{40,48},{48,56},{56,0},{1,9},... | collective-permute-start | bytes 909320 | tf_op jit(solution)/shard_map/scatter/ppermute | solution.py:25
  111.6 10.8 %collective-permute-start.28 = (bf16[1184,128]{1,0:T(8,128)(2,1)S(1)}, bf16[1184,128]{1,0:T(8,128)(2,1)S(1)}, u32[]{:S(2)}, u32[]{:S(2)}) collective-permute-start(bf16[1184,128]{1,0:T(8,128)(2,1)S(1)} %pad_maximum_fusion.2), channel_id=1, source_target_pairs={{0,56},{8,0},{16,8},{24,16},{32,24},{40,32},{48,40},{56,48},{1,57}... | collective-permute-start | bytes 909320 | tf_op jit(solution)/shard_map/scatter/ppermute | solution.py:25
  114.4 19.3 %collective-permute-start.32 = (bf16[2048,128]{1,0:T(8,128)(2,1)S(1)}, bf16[2048,128]{1,0:T(8,128)(2,1)S(1)}, u32[]{:S(2)}, u32[]{:S(2)}) collective-permute-start(bf16[2048,128]{1,0:T(8,128)(2,1)S(1)} %bitcast.39), channel_id=1, source_target_pairs={{0,4},{4,0},{1,5},{5,1},{2,6},{6,2},{3,7},{7,3},{8,12},{12,8},{9,1... | collective-permute-start | bytes 1572872 | tf_op jit(solution)/shard_map/scatter/ppermute | solution.py:30
  122.7 10.9 %collective-permute-start.31 = (bf16[1184,128]{1,0:T(8,128)(2,1)S(1)}, bf16[1184,128]{1,0:T(8,128)(2,1)S(1)}, u32[]{:S(2)}, u32[]{:S(2)}) collective-permute-start(bf16[1184,128]{1,0:T(8,128)(2,1)S(1)} %pad_maximum_fusion.4), channel_id=1, source_target_pairs={{0,56},{8,0},{16,8},{24,16},{32,24},{40,32},{48,40},{56,48},{1,57}... | collective-permute-start | bytes 909320 | tf_op jit(solution)/shard_map/scatter/ppermute | solution.py:25
  122.8 10.8 %collective-permute-start.30 = (bf16[1184,128]{1,0:T(8,128)(2,1)S(1)}, bf16[1184,128]{1,0:T(8,128)(2,1)S(1)}, u32[]{:S(2)}, u32[]{:S(2)}) collective-permute-start(bf16[1184,128]{1,0:T(8,128)(2,1)S(1)} %pad_maximum_fusion.3), channel_id=1, source_target_pairs={{0,8},{8,16},{16,24},{24,32},{32,40},{40,48},{48,56},{56,0},{1,9},... | collective-permute-start | bytes 909320 | tf_op jit(solution)/shard_map/scatter/ppermute | solution.py:25
  133.9 8.5 %collective-permute-start.33 = (bf16[1184,128]{1,0:T(8,128)(2,1)S(1)}, bf16[1184,128]{1,0:T(8,128)(2,1)S(1)}, u32[]{:S(2)}, u32[]{:S(2)}) collective-permute-start(bf16[1184,128]{1,0:T(8,128)(2,1)S(1)} %pad_maximum_fusion.5), channel_id=1, source_target_pairs={{0,8},{8,16},{16,24},{24,32},{32,40},{40,48},{48,56},{56,0},{1,9},... | collective-permute-start | bytes 909320 | tf_op jit(solution)/shard_map/scatter/ppermute | solution.py:25
  134.0 7.3 %collective-permute-start.35 = (bf16[1024,128]{1,0:T(8,128)(2,1)S(1)}, bf16[1024,128]{1,0:T(8,128)(2,1)S(1)}, u32[]{:S(2)}, u32[]{:S(2)}) collective-permute-start(bf16[1024,128]{1,0:T(8,128)(2,1)S(1)} %bitcast.42), channel_id=1, source_target_pairs={{0,4},{4,0},{1,5},{5,1},{2,6},{6,2},{3,7},{7,3},{8,12},{12,8},{9,1... | collective-permute-start | bytes 786440 | tf_op jit(solution)/shard_map/scatter/ppermute | solution.py:30
  136.6 5.9 %collective-permute-start.34 = (bf16[1024,128]{1,0:T(8,128)(2,1)S(1)}, bf16[1024,128]{1,0:T(8,128)(2,1)S(1)}, u32[]{:S(2)}, u32[]{:S(2)}) collective-permute-start(bf16[1024,128]{1,0:T(8,128)(2,1)S(1)} %get-tuple-element.93), channel_id=1, source_target_pairs={{0,56},{8,0},{16,8},{24,16},{32,24},{40,32},{48,40},{56,48},{1,57}... | collective-permute-start | bytes 786440 | tf_op jit(solution)/shard_map/scatter/ppermute | solution.py:25
  142.7 6.0 %collective-permute-start.36 = (bf16[416,128]{1,0:T(8,128)(2,1)S(1)}, bf16[416,128]{1,0:T(8,128)(2,1)S(1)}, u32[]{:S(2)}, u32[]{:S(2)}) collective-permute-start(bf16[416,128]{1,0:T(8,128)(2,1)S(1)} %get-tuple-element.104), channel_id=1, source_target_pairs={{0,64},{64,128},{128,192},{192,0},{1,65},{65,129},{129,193},{193,1... | collective-permute-start | bytes 319496 | tf_op jit(solution)/shard_map/scatter/ppermute | solution.py:21
  142.8 5.9 %collective-permute-start.37 = (bf16[416,128]{1,0:T(8,128)(2,1)S(1)}, bf16[416,128]{1,0:T(8,128)(2,1)S(1)}, u32[]{:S(2)}, u32[]{:S(2)}) collective-permute-start(bf16[416,128]{1,0:T(8,128)(2,1)S(1)} %get-tuple-element.105), channel_id=1, source_target_pairs={{0,128},{64,192},{128,0},{192,64},{1,129},{65,193},{129,1},{193,65... | collective-permute-start | bytes 319496 | tf_op jit(solution)/shard_map/scatter/ppermute | solution.py:21
  143.2 6.2 %collective-permute-start.38 = (bf16[416,128]{1,0:T(8,128)(2,1)S(1)}, bf16[416,128]{1,0:T(8,128)(2,1)S(1)}, u32[]{:S(2)}, u32[]{:S(2)}) collective-permute-start(bf16[416,128]{1,0:T(8,128)(2,1)S(1)} %get-tuple-element.106), channel_id=1, source_target_pairs={{0,192},{64,0},{128,64},{192,128},{1,193},{65,1},{129,65},{193,129... | collective-permute-start | bytes 319496 | tf_op jit(solution)/shard_map/scatter/ppermute | solution.py:21
  149.4 6.2 %copy-start.5 = (f32[160,128]{1,0:T(8,128)}, f32[160,128]{1,0:T(8,128)S(1)}, u32[]{:S(2)}) copy-start(f32[160,128]{1,0:T(8,128)S(1)} %convert_add_fusion.8.mine_ref) | copy-start | bytes 245764
  149.4 6.2 %collective-permute-start.39 = (f32[160,128]{1,0:T(8,128)S(1)}, f32[160,128]{1,0:T(8,128)S(1)}, u32[]{:S(2)}, u32[]{:S(2)}) collective-permute-start(f32[160,128]{1,0:T(8,128)S(1)} %convert_add_fusion.8.mine_ref), channel_id=1, source_target_pairs={{0,1},{1,0},{2,3},{3,2},{4,5},{5,4},{6,7},{7,6},{8,9},{9,8},{10,11... | collective-permute-start | bytes 245768 | tf_op jit(solution)/shard_map/scatter/ppermute | solution.py:30
  155.5 0.6 copy-start.6

commit v4 on v3

--- a/solution.py
+++ b/solution.py
@@ -153,7 +153,7 @@
         ),
         in_specs=[pl.BlockSpec(memory_space=SMEM)] + [vmem] * 7,
         out_specs=(vmem,) * 4,
-        compiler_params=pltpu.CompilerParams(vmem_limit_bytes=32 * 2**20),
+        compiler_params=pltpu.CompilerParams(vmem_limit_bytes=16 * 2**20),
         name="middle",
     )(rep, *parts, weight, bias.reshape(1, -1), cotangent)
 
@@ -239,6 +239,7 @@
         ),
         in_specs=[pl.BlockSpec(memory_space=SMEM)] + [vmem] * 3,
         out_specs=(vmem, vmem, vmem),
+        compiler_params=pltpu.CompilerParams(vmem_limit_bytes=8 * 2**20),
         name="last",
     )(rep, total, mine, theirs)
 

time: 158 us -> 156 us (0.987)
    unnamed x18 -> x14, local copies, waits for them, and re-layouts: 4.85 us -> 4.22 us
where the time goes in v4:
time: 156 us
  starting transfers between devices  67.6 us (43%)
  waiting for transfers between devices  65.4 us (42%)
  Pallas kernels  12.3 us (8%)
  local copies, waits for them, and re-layouts  6.64 us (4%)
  other arithmetic  3.42 us (2%)
    ppermute x15, waiting for transfers between devices, swap(): return lax.ppermute(value, axes, pairs)  38.5 us
    ppermute x15, starting transfers between devices, swap(): return lax.ppermute(value, axes, pairs)  32.3 us
    ppermute x16, starting transfers between devices, shift_z(): return lax.ppermute(value, 'z', [(i, (i + k) % NZ) for i in range(NZ)])  18.1 us
    ppermute x16, waiting for transfers between devices, shift_z(): return lax.ppermute(value, 'z', [(i, (i + k) % NZ) for i in range(NZ)])  13.2 us
    ppermute x9, waiting for transfers between devices, shift_x(): return lax.ppermute(value, 'x', [(i, (i + k) % NX) for i in range(NX)])  9.13 us
    ppermute x9, starting transfers between devices, shift_x(): return lax.ppermute(value, 'x', [(i, (i + k) % NX) for i in range(NX)])  8.88 us
    all_to_all x1, starting transfers between devices, gather_features(): line = lax.all_to_all(spread, 'z', 0, 0, tiled=True)  8.37 us
    pallas_call x1, Pallas kernels, backward(): pl.pallas_call(functools.partial(backward_kernel, places), out_shape=tupl...  5.14 us
  transfers between devices with their start and end apart: 41, of which 23 were waited for; matrix products, arithmetic and copies ran while one was open for 4% of the time, Pallas kernels for 3%

profile of v4, /device:TPU:1, one launch (start us, length us, event | category | flops | bytes accessed | tf_op | source)
XLA Modules:
  0.0 156.3 jit_solution(2183300869110858011)
XLA Ops:
  0.6 3.8 %collective-permute-start = (bf16[2,128,128]{2,1,0:T(8,128)(2,1)}, bf16[2,128,128]{2,1,0:T(8,128)(2,1)S(1)}, u32[]{:S(2)}, u32[]{:S(2)}) collective-permute-start(bf16[2,128,128]{2,1,0:T(8,128)(2,1)} %bitcast.44), channel_id=1, source_target_pairs={{0,4},{4,0},{1,5},{5,1},{2,6},{6,2},{3,7},{7,3},{8,12},{12,8},{9,1... | collective-permute-start | bytes 196616 | tf_op jit(solution)/shard_map/gather/ppermute | solution.py:30
  4.5 1.9 %collective-permute-done = bf16[2,128,128]{2,1,0:T(8,128)(2,1)S(1)} collective-permute-done((bf16[2,128,128]{2,1,0:T(8,128)(2,1)}, bf16[2,128,128]{2,1,0:T(8,128)(2,1)S(1)}, u32[]{:S(2)}, u32[]{:S(2)}) %collective-permute-start) | collective-permute-done | bytes 65568 | tf_op jit(solution)/shard_map/gather/ppermute | solution.py:30
  6.3 0.9 broadcast_in_dim.2
  7.2 8.4 %all-to-all-start = ((bf16[16,128,128]{2,1,0:T(8,128)(2,1)}), bf16[16,128,128]{2,1,0:T(8,128)(2,1)S(1)}, u32[]{:S(2)}, u32[]{:S(2)}) async-start(bf16[16,128,128]{2,1,0:T(8,128)(2,1)} %bitcast.3), calls=%async_computation | async-start | bytes 1048576 | tf_op jit(solution)/shard_map/gather/all_to_all | solution.py:251
  15.6 2.5 %collective-permute-start.3 = (bf16[2,128,128]{2,1,0:T(8,128)(2,1)}, bf16[2,128,128]{2,1,0:T(8,128)(2,1)S(1)}, u32[]{:S(2)}, u32[]{:S(2)}) collective-permute-start(bf16[2,128,128]{2,1,0:T(8,128)(2,1)} %bitcast.45), channel_id=1, source_target_pairs={{0,192},{64,0},{128,64},{192,128},{1,193},{65,1},{129,65},{193,129... | collective-permute-start | bytes 196616 | tf_op jit(solution)/shard_map/gather/ppermute | solution.py:21
  20.1 3.5 %collective-permute-done.1 = bf16[2,128,128]{2,1,0:T(8,128)(2,1)S(1)} collective-permute-done((bf16[2,128,128]{2,1,0:T(8,128)(2,1)}, bf16[2,128,128]{2,1,0:T(8,128)(2,1)S(1)}, u32[]{:S(2)}, u32[]{:S(2)}) %collective-permute-start.1) | collective-permute-done | bytes 65568 | tf_op jit(solution)/shard_map/gather/ppermute | solution.py:21
  23.7 3.0 %collective-permute-start.5 = (bf16[8,128,128]{2,1,0:T(8,128)(2,1)S(1)}, bf16[8,128,128]{2,1,0:T(8,128)(2,1)S(1)}, u32[]{:S(2)}, u32[]{:S(2)}) collective-permute-start(bf16[8,128,128]{2,1,0:T(8,128)(2,1)S(1)} %constant_dynamic-update-slice_fusion.rest_0_), channel_id=1, source_target_pairs={{0,56},{8,0},{16,8},{24,16},{32,24},{40,32},{48,40},{56,48},{1,57}... | collective-permute-start | bytes 786440 | tf_op jit(solution)/shard_map/gather/ppermute | solution.py:25
  26.7 4.5 %all-to-all-done.rest_1_ = bf16[16,128,128]{2,1,0:T(8,128)(2,1)S(1)} async-done(((bf16[16,128,128]{2,1,0:T(8,128)(2,1)}), bf16[16,128,128]{2,1,0:T(8,128)(2,1)S(1)}, u32[]{:S(2)}, u32[]{:S(2)}) %all-to-all-start) | async-done | bytes 524320 | tf_op jit(solution)/shard_map/gather/all_to_all | solution.py:251
  31.3 2.5 %collective-permute-start.9 = (bf16[16,128,128]{2,1,0:T(8,128)(2,1)S(1)}, bf16[16,128,128]{2,1,0:T(8,128)(2,1)S(1)}, u32[]{:S(2)}, u32[]{:S(2)}) collective-permute-start(bf16[16,128,128]{2,1,0:T(8,128)(2,1)S(1)} %all-to-all-done.rest_1_), channel_id=1, source_target_pairs={{0,192},{64,0},{128,64},{192,128},{1,193},{65,1},{129,65},{193,129... | collective-permute-start | bytes 1572872 | tf_op jit(solution)/shard_map/gather/ppermute | solution.py:21
  34.1 1.6 collective-permute-start.7
  35.7 4.0 %collective-permute-done.7.rest_5_ = bf16[8,128,128]{2,1,0:T(8,128)(2,1)} collective-permute-done((bf16[8,128,128]{2,1,0:T(8,128)(2,1)S(1)}, bf16[8,128,128]{2,1,0:T(8,128)(2,1)}, u32[]{:S(2)}, u32[]{:S(2)}) %collective-permute-start.7) | collective-permute-done | bytes 262176 | tf_op jit(solution)/shard_map/gather/ppermute | solution.py:25
  39.6 2.8 %collective-permute-start.11 = (bf16[8,128,128]{2,1,0:T(8,128)(2,1)}, bf16[8,128,128]{2,1,0:T(8,128)(2,1)S(1)}, u32[]{:S(2)}, u32[]{:S(2)}) collective-permute-start(bf16[8,128,128]{2,1,0:T(8,128)(2,1)} %collective-permute-done.7.rest_5_), channel_id=1, source_target_pairs={{0,56},{8,0},{16,8},{24,16},{32,24},{40,32},{48,40},{56,48},{1,57}... | collective-permute-start | bytes 786440 | tf_op jit(solution)/shard_map/gather/ppermute | solution.py:25
  42.4 1.7 %collective-permute-done.8.rest_8_ = bf16[16,128,128]{2,1,0:T(8,128)(2,1)S(1)} collective-permute-done((bf16[16,128,128]{2,1,0:T(8,128)(2,1)S(1)}, bf16[16,128,128]{2,1,0:T(8,128)(2,1)S(1)}, u32[]{:S(2)}, u32[]{:S(2)}) %collective-permute-start.8) | collective-permute-done | bytes 524320 | tf_op jit(solution)/shard_map/gather/ppermute | solution.py:21
  44.7 1.3 reduce.3
  47.6 2.1 %collective-permute-start.14 = (bf16[4,128,128]{2,1,0:T(8,128)(2,1)}, bf16[4,128,128]{2,1,0:T(8,128)(2,1)S(1)}, u32[]{:S(2)}, u32[]{:S(2)}) collective-permute-start(bf16[4,128,128]{2,1,0:T(8,128)(2,1)} %slice.166), channel_id=1, source_target_pairs={{0,56},{8,0},{16,8},{24,16},{32,24},{40,32},{48,40},{56,48},{1,57}... | collective-permute-start | bytes 393224 | tf_op jit(solution)/shard_map/gather/ppermute | solution.py:25
  49.7 1.1 collective-permute-done.10.rest_6_
  52.2 1.3 collective-permute-done.14.rest_12_
  53.5 4.6 %collective-permute-done.13.rest_11_ = bf16[4,128,128]{2,1,0:T(8,128)(2,1)} collective-permute-done((bf16[4,128,128]{2,1,0:T(8,128)(2,1)}, bf16[4,128,128]{2,1,0:T(8,128)(2,1)}, u32[]{:S(2)}, u32[]{:S(2)}) %collective-permute-start.13) | collective-permute-done | bytes 131104 | tf_op jit(solution)/shard_map/gather/ppermute | solution.py:25
  58.1 2.8 %copy-done = bf16[8,1,24,128,128]{4,3,2,1,0:T(8,128)(2,1)S(1)} copy-done((bf16[8,1,24,128,128]{4,3,2,1,0:T(8,128)(2,1)S(1)}, bf16[8,1,24,128,128]{4,3,2,1,0:T(8,128)(2,1)}, u32[]{:S(2)}) %copy-start) | copy-done | bytes 6291480
  60.9 4.8 %forward.1 = (bf16[2,128,128]{2,1,0:T(8,128)(2,1)S(1)}, bf16[2,128,128]{2,1,0:T(8,128)(2,1)S(1)}, bf16[2,128,128]{2,1,0:T(8,128)(2,1)S(1)}, bf16[2,128,128]{2,1,0:T(8,128)(2,1)S(1)}) custom-call(s32[1]{0:T(128)} %bitcast.rep_ref, s32[200]{0:T(256)S(1)} %get-tuple-element.110.meta_ref, bf16[8,1,24,128,128]{4,3,2,1,0:T(8,128)(2,1)S(1)} %copy-done, ...), custom_call_target="tpu_custom_call" | custom-call | flops 805306368 | bytes 11534336 | tf_op jit(solution)/shard_map/forward/pallas_call | solution.py:100
  65.7 7.3 %collective-permute-start.15 = (bf16[2,128,128]{2,1,0:T(8,128)(2,1)S(1)}, bf16[2,128,128]{2,1,0:T(8,128)(2,1)S(1)}, u32[]{:S(2)}, u32[]{:S(2)}) collective-permute-start(bf16[2,128,128]{2,1,0:T(8,128)(2,1)S(1)} %get-tuple-element.51), channel_id=1, source_target_pairs={{0,1},{1,0},{2,3},{3,2},{4,5},{5,4},{6,7},{7,6},{8,9},{9,8},{10,11... | collective-permute-start | bytes 196616 | tf_op jit(solution)/shard_map/sections/ppermute | solution.py:30
  73.0 1.3 collective-permute-start.16
  74.8 1.9 %collective-permute-done.16.p2 = bf16[2,128,128]{2,1,0:T(8,128)(2,1)S(1)} collective-permute-done((bf16[2,128,128]{2,1,0:T(8,128)(2,1)S(1)}, bf16[2,128,128]{2,1,0:T(8,128)(2,1)S(1)}, u32[]{:S(2)}, u32[]{:S(2)}) %collective-permute-start.16) | collective-permute-done | bytes 65568 | tf_op jit(solution)/shard_map/sections/ppermute | solution.py:30
  76.7 1.7 %collective-permute-done.17.p3 = bf16[2,128,128]{2,1,0:T(8,128)(2,1)S(1)} collective-permute-done((bf16[2,128,128]{2,1,0:T(8,128)(2,1)S(1)}, bf16[2,128,128]{2,1,0:T(8,128)(2,1)S(1)}, u32[]{:S(2)}, u32[]{:S(2)}) %collective-permute-start.17) | collective-permute-done | bytes 65568 | tf_op jit(solution)/shard_map/sections/ppermute | solution.py:30
  78.4 1.6 %middle.1 = (bf16[256,256]{1,0:T(8,128)(2,1)}, bf16[2,128,128]{2,1,0:T(8,128)(2,1)S(1)}, f32[160,128]{1,0:T(8,128)S(1)}, f32[160,128]{1,0:T(8,128)S(1)}) custom-call(s32[1]{0:T(128)} %bitcast.rep_ref, bf16[2,128,128]{2,1,0:T(8,128)(2,1)S(1)} %get-tuple-element.50.p0, bf16[2,128,128]{2,1,0:T(8,128)(2,1)S(1)} %collective-permute-done.15.p1, ...), custom_call_target="tpu_custom_call" | custom-call | tf_op jit(solution)/shard_map/middle/pallas_call | solution.py:146
  80.4 1.2 collective-permute-start.20
  82.5 1.1 collective-permute-start.22
  83.6 0.9 collective-permute-done.20.s3
  84.5 1.0 collective-permute-done.19.s2
  85.6 5.1 %backward.1 = (bf16[8,128,128]{2,1,0:T(8,128)(2,1)S(1)}, bf16[8,128,128]{2,1,0:T(8,128)(2,1)S(1)}, bf16[8,128,128]{2,1,0:T(8,128)(2,1)S(1)}, bf16[8,128,128]{2,1...) custom-call(s32[1]{0:T(128)} %bitcast.rep_ref, ...), custom_call_target="tpu_custom_call" | custom-call | flops 805306368 | bytes 15728640 | tf_op jit(solution)/shard_map/backward/pallas_call | solution.py:202
  90.8 2.8 %collective-permute-start.23 = (bf16[1184,128]{1,0:T(8,128)(2,1)S(1)}, bf16[1184,128]{1,0:T(8,128)(2,1)S(1)}, u32[]{:S(2)}, u32[]{:S(2)}) collective-permute-start(bf16[1184,128]{1,0:T(8,128)(2,1)S(1)} %pad_maximum_fusion), channel_id=1, source_target_pairs={{0,4},{4,0},{1,5},{5,1},{2,6},{6,2},{3,7},{7,3},{8,12},{12,8},{9,1... | collective-permute-start | bytes 909320 | tf_op jit(solution)/shard_map/scatter/ppermute | solution.py:30
  93.8 6.1 %collective-permute-done.23 = bf16[1184,128]{1,0:T(8,128)(2,1)S(1)} collective-permute-done((bf16[1184,128]{1,0:T(8,128)(2,1)S(1)}, bf16[1184,128]{1,0:T(8,128)(2,1)S(1)}, u32[]{:S(2)}, u32[]{:S(2)}) %collective-permute-start.23) | collective-permute-done | bytes 303136 | tf_op jit(solution)/shard_map/scatter/ppermute | solution.py:30
  100.2 1.5 collective-permute-start.24
  101.6 2.5 %collective-permute-start.29 = (bf16[2048,128]{1,0:T(8,128)(2,1)S(1)}, bf16[2048,128]{1,0:T(8,128)(2,1)S(1)}, u32[]{:S(2)}, u32[]{:S(2)}) collective-permute-start(bf16[2048,128]{1,0:T(8,128)(2,1)S(1)} %bitcast.41), channel_id=1, source_target_pairs={{0,4},{4,0},{1,5},{5,1},{2,6},{6,2},{3,7},{7,3},{8,12},{12,8},{9,1... | collective-permute-start | bytes 1572872 | tf_op jit(solution)/shard_map/scatter/ppermute | solution.py:30
  104.1 7.0 %collective-permute-done.26 = bf16[2048,128]{1,0:T(8,128)(2,1)S(1)} collective-permute-done((bf16[2048,128]{1,0:T(8,128)(2,1)S(1)}, bf16[2048,128]{1,0:T(8,128)(2,1)S(1)}, u32[]{:S(2)}, u32[]{:S(2)}) %collective-permute-start.26) | collective-permute-done | bytes 524320 | tf_op jit(solution)/shard_map/scatter/ppermute | solution.py:30
  111.6 2.7 %collective-permute-start.28 = (bf16[1184,128]{1,0:T(8,128)(2,1)S(1)}, bf16[1184,128]{1,0:T(8,128)(2,1)S(1)}, u32[]{:S(2)}, u32[]{:S(2)}) collective-permute-start(bf16[1184,128]{1,0:T(8,128)(2,1)S(1)} %pad_maximum_fusion.2), channel_id=1, source_target_pairs={{0,56},{8,0},{16,8},{24,16},{32,24},{40,32},{48,40},{56,48},{1,57}... | collective-permute-start | bytes 909320 | tf_op jit(solution)/shard_map/scatter/ppermute | solution.py:25
  114.3 2.5 %collective-permute-start.32 = (bf16[2048,128]{1,0:T(8,128)(2,1)S(1)}, bf16[2048,128]{1,0:T(8,128)(2,1)S(1)}, u32[]{:S(2)}, u32[]{:S(2)}) collective-permute-start(bf16[2048,128]{1,0:T(8,128)(2,1)S(1)} %bitcast.40), channel_id=1, source_target_pairs={{0,4},{4,0},{1,5},{5,1},{2,6},{6,2},{3,7},{7,3},{8,12},{12,8},{9,1... | collective-permute-start | bytes 1572872 | tf_op jit(solution)/shard_map/scatter/ppermute | solution.py:30
  116.8 5.6 %collective-permute-done.29 = bf16[2048,128]{1,0:T(8,128)(2,1)S(1)} collective-permute-done((bf16[2048,128]{1,0:T(8,128)(2,1)S(1)}, bf16[2048,128]{1,0:T(8,128)(2,1)S(1)}, u32[]{:S(2)}, u32[]{:S(2)}) %collective-permute-start.29) | collective-permute-done | bytes 524320 | tf_op jit(solution)/shard_map/scatter/ppermute | solution.py:30
  122.8 1.5 collective-permute-start.30
  124.3 9.3 %collective-permute-done.32 = bf16[2048,128]{1,0:T(8,128)(2,1)S(1)} collective-permute-done((bf16[2048,128]{1,0:T(8,128)(2,1)S(1)}, bf16[2048,128]{1,0:T(8,128)(2,1)S(1)}, u32[]{:S(2)}, u32[]{:S(2)}) %collective-permute-start.32) | collective-permute-done | bytes 524320 | tf_op jit(solution)/shard_map/scatter/ppermute | solution.py:30
  134.0 2.6 %collective-permute-start.35 = (bf16[1024,128]{1,0:T(8,128)(2,1)S(1)}, bf16[1024,128]{1,0:T(8,128)(2,1)S(1)}, u32[]{:S(2)}, u32[]{:S(2)}) collective-permute-start(bf16[1024,128]{1,0:T(8,128)(2,1)S(1)} %bitcast.43), channel_id=1, source_target_pairs={{0,4},{4,0},{1,5},{5,1},{2,6},{6,2},{3,7},{7,3},{8,12},{12,8},{9,1... | collective-permute-start | bytes 786440 | tf_op jit(solution)/shard_map/scatter/ppermute | solution.py:30
  136.6 2.6 %collective-permute-start.34 = (bf16[1024,128]{1,0:T(8,128)(2,1)S(1)}, bf16[1024,128]{1,0:T(8,128)(2,1)S(1)}, u32[]{:S(2)}, u32[]{:S(2)}) collective-permute-start(bf16[1024,128]{1,0:T(8,128)(2,1)S(1)} %get-tuple-element.93), channel_id=1, source_target_pairs={{0,56},{8,0},{16,8},{24,16},{32,24},{40,32},{48,40},{56,48},{1,57}... | collective-permute-start | bytes 786440 | tf_op jit(solution)/shard_map/scatter/ppermute | solution.py:25
  139.2 2.2 %collective-permute-done.35 = bf16[1024,128]{1,0:T(8,128)(2,1)S(1)} collective-permute-done((bf16[1024,128]{1,0:T(8,128)(2,1)S(1)}, bf16[1024,128]{1,0:T(8,128)(2,1)S(1)}, u32[]{:S(2)}, u32[]{:S(2)}) %collective-permute-start.35) | collective-permute-done | bytes 262176 | tf_op jit(solution)/shard_map/scatter/ppermute | solution.py:30
  141.4 1.1 collective-permute-done.34
  143.1 2.4 %collective-permute-start.38 = (bf16[416,128]{1,0:T(8,128)(2,1)S(1)}, bf16[416,128]{1,0:T(8,128)(2,1)S(1)}, u32[]{:S(2)}, u32[]{:S(2)}) collective-permute-start(bf16[416,128]{1,0:T(8,128)(2,1)S(1)} %get-tuple-element.106), channel_id=1, source_target_pairs={{0,192},{64,0},{128,64},{192,128},{1,193},{65,1},{129,65},{193,129... | collective-permute-start | bytes 319496 | tf_op jit(solution)/shard_map/scatter/ppermute | solution.py:21
  145.5 3.2 %collective-permute-done.36 = bf16[416,128]{1,0:T(8,128)(2,1)S(1)} collective-permute-done((bf16[416,128]{1,0:T(8,128)(2,1)S(1)}, bf16[416,128]{1,0:T(8,128)(2,1)S(1)}, u32[]{:S(2)}, u32[]{:S(2)}) %collective-permute-start.36) | collective-permute-done | bytes 106528 | tf_op jit(solution)/shard_map/scatter/ppermute | solution.py:21
  149.4 5.2 %collective-permute-start.39 = (f32[160,128]{1,0:T(8,128)S(1)}, f32[160,128]{1,0:T(8,128)S(1)}, u32[]{:S(2)}, u32[]{:S(2)}) collective-permute-start(f32[160,128]{1,0:T(8,128)S(1)} %convert_add_fusion.8.mine_ref), channel_id=1, source_target_pairs={{0,1},{1,0},{2,3},{3,2},{4,5},{5,4},{6,7},{7,6},{8,9},{9,8},{10,11... | collective-permute-start | bytes 245768 | tf_op jit(solution)/shard_map/scatter/ppermute | solution.py:30
  154.6 0.9 collective-permute-done.39.theirs_ref
  (91 shorter events, 11.4 us)
Async XLA Ops:
  0.6 5.7 %collective-permute-start = (bf16[2,128,128]{2,1,0:T(8,128)(2,1)}, bf16[2,128,128]{2,1,0:T(8,128)(2,1)S(1)}, u32[]{:S(2)}, u32[]{:S(2)}) collective-permute-start(bf16[2,128,128]{2,1,0:T(8,128)(2,1)} %bitcast.44), channel_id=1, source_target_pairs={{0,4},{4,0},{1,5},{5,1},{2,6},{6,2},{3,7},{7,3},{8,12},{12,8},{9,1... | collective-permute-start | bytes 196616 | tf_op jit(solution)/shard_map/gather/ppermute | solution.py:30
  7.2 71.2 %copy-start.4 = (f32[256]{0:T(256)S(1)}, f32[256]{0:T(256)}, u32[]{:S(2)}) copy-start(f32[256]{0:T(256)} %param.9) | copy-start | bytes 3076
  7.2 24.0 %all-to-all-start = ((bf16[16,128,128]{2,1,0:T(8,128)(2,1)}), bf16[16,128,128]{2,1,0:T(8,128)(2,1)S(1)}, u32[]{:S(2)}, u32[]{:S(2)}) async-start(bf16[16,128,128]{2,1,0:T(8,128)(2,1)} %bitcast.3), calls=%async_computation | async-start | bytes 1048576 | tf_op jit(solution)/shard_map/gather/all_to_all | solution.py:251
  15.6 8.1 %collective-permute-start.3 = (bf16[2,128,128]{2,1,0:T(8,128)(2,1)}, bf16[2,128,128]{2,1,0:T(8,128)(2,1)S(1)}, u32[]{:S(2)}, u32[]{:S(2)}) collective-permute-start(bf16[2,128,128]{2,1,0:T(8,128)(2,1)} %bitcast.45), channel_id=1, source_target_pairs={{0,192},{64,0},{128,64},{192,128},{1,193},{65,1},{129,65},{193,129... | collective-permute-start | bytes 196616 | tf_op jit(solution)/shard_map/gather/ppermute | solution.py:21
  18.1 5.5 %collective-permute-start.2 = (bf16[2,128,128]{2,1,0:T(8,128)(2,1)}, bf16[2,128,128]{2,1,0:T(8,128)(2,1)S(1)}, u32[]{:S(2)}, u32[]{:S(2)}) collective-permute-start(bf16[2,128,128]{2,1,0:T(8,128)(2,1)} %bitcast.46), channel_id=1, source_target_pairs={{0,128},{64,192},{128,0},{192,64},{1,129},{65,193},{129,1},{193,65... | collective-permute-start | bytes 196616 | tf_op jit(solution)/shard_map/gather/ppermute | solution.py:21
  18.6 5.0 %collective-permute-start.1 = (bf16[2,128,128]{2,1,0:T(8,128)(2,1)}, bf16[2,128,128]{2,1,0:T(8,128)(2,1)S(1)}, u32[]{:S(2)}, u32[]{:S(2)}) collective-permute-start(bf16[2,128,128]{2,1,0:T(8,128)(2,1)} %bitcast.47), channel_id=1, source_target_pairs={{0,64},{64,128},{128,192},{192,0},{1,65},{65,129},{129,193},{193,1... | collective-permute-start | bytes 196616 | tf_op jit(solution)/shard_map/gather/ppermute | solution.py:21
  23.7 10.4 %collective-permute-start.5 = (bf16[8,128,128]{2,1,0:T(8,128)(2,1)S(1)}, bf16[8,128,128]{2,1,0:T(8,128)(2,1)S(1)}, u32[]{:S(2)}, u32[]{:S(2)}) collective-permute-start(bf16[8,128,128]{2,1,0:T(8,128)(2,1)S(1)} %constant_dynamic-update-slice_fusion.rest_0_), channel_id=1, source_target_pairs={{0,56},{8,0},{16,8},{24,16},{32,24},{40,32},{48,40},{56,48},{1,57}... | collective-permute-start | bytes 786440 | tf_op jit(solution)/shard_map/gather/ppermute | solution.py:25
  26.7 8.9 %collective-permute-start.4 = (bf16[8,128,128]{2,1,0:T(8,128)(2,1)S(1)}, bf16[8,128,128]{2,1,0:T(8,128)(2,1)S(1)}, u32[]{:S(2)}, u32[]{:S(2)}) collective-permute-start(bf16[8,128,128]{2,1,0:T(8,128)(2,1)S(1)} %constant_dynamic-update-slice_fusion.rest_0_), channel_id=1, source_target_pairs={{0,8},{8,16},{16,24},{24,32},{32,40},{40,48},{48,56},{56,0},{1,9},... | collective-permute-start | bytes 786440 | tf_op jit(solution)/shard_map/gather/ppermute | solution.py:25
  31.3 11.1 %collective-permute-start.9 = (bf16[16,128,128]{2,1,0:T(8,128)(2,1)S(1)}, bf16[16,128,128]{2,1,0:T(8,128)(2,1)S(1)}, u32[]{:S(2)}, u32[]{:S(2)}) collective-permute-start(bf16[16,128,128]{2,1,0:T(8,128)(2,1)S(1)} %all-to-all-done.rest_1_), channel_id=1, source_target_pairs={{0,192},{64,0},{128,64},{192,128},{1,193},{65,1},{129,65},{193,129... | collective-permute-start | bytes 1572872 | tf_op jit(solution)/shard_map/gather/ppermute | solution.py:21
  33.8 10.4 %collective-permute-start.8 = (bf16[16,128,128]{2,1,0:T(8,128)(2,1)S(1)}, bf16[16,128,128]{2,1,0:T(8,128)(2,1)S(1)}, u32[]{:S(2)}, u32[]{:S(2)}) collective-permute-start(bf16[16,128,128]{2,1,0:T(8,128)(2,1)S(1)} %all-to-all-done.rest_1_), channel_id=1, source_target_pairs={{0,64},{64,128},{128,192},{192,0},{1,65},{65,129},{129,193},{193,1... | collective-permute-start | bytes 1572872 | tf_op jit(solution)/shard_map/gather/ppermute | solution.py:21
  34.1 5.5 %collective-permute-start.7 = (bf16[8,128,128]{2,1,0:T(8,128)(2,1)S(1)}, bf16[8,128,128]{2,1,0:T(8,128)(2,1)}, u32[]{:S(2)}, u32[]{:S(2)}) collective-permute-start(bf16[8,128,128]{2,1,0:T(8,128)(2,1)S(1)} %collective-permute-done.5.rest_3_), channel_id=1, source_target_pairs={{0,56},{8,0},{16,8},{24,16},{32,24},{40,32},{48,40},{56,48},{1,57}... | collective-permute-start | bytes 786440 | tf_op jit(solution)/shard_map/gather/ppermute | solution.py:25
  35.7 6.7 %collective-permute-start.6 = (bf16[8,128,128]{2,1,0:T(8,128)(2,1)S(1)}, bf16[8,128,128]{2,1,0:T(8,128)(2,1)}, u32[]{:S(2)}, u32[]{:S(2)}) collective-permute-start(bf16[8,128,128]{2,1,0:T(8,128)(2,1)S(1)} %collective-permute-done.4.rest_2_), channel_id=1, source_target_pairs={{0,8},{8,16},{16,24},{24,32},{32,40},{40,48},{48,56},{56,0},{1,9},... | collective-permute-start | bytes 786440 | tf_op jit(solution)/shard_map/gather/ppermute | solution.py:25
  39.6 7.3 %collective-permute-start.11 = (bf16[8,128,128]{2,1,0:T(8,128)(2,1)}, bf16[8,128,128]{2,1,0:T(8,128)(2,1)S(1)}, u32[]{:S(2)}, u32[]{:S(2)}) collective-permute-start(bf16[8,128,128]{2,1,0:T(8,128)(2,1)} %collective-permute-done.7.rest_5_), channel_id=1, source_target_pairs={{0,56},{8,0},{16,8},{24,16},{32,24},{40,32},{48,40},{56,48},{1,57}... | collective-permute-start | bytes 786440 | tf_op jit(solution)/shard_map/gather/ppermute | solution.py:25
  44.1 6.6 %collective-permute-start.10 = (bf16[8,128,128]{2,1,0:T(8,128)(2,1)}, bf16[8,128,128]{2,1,0:T(8,128)(2,1)S(1)}, u32[]{:S(2)}, u32[]{:S(2)}) collective-permute-start(bf16[8,128,128]{2,1,0:T(8,128)(2,1)} %collective-permute-done.6.rest_4_), channel_id=1, source_target_pairs={{0,8},{8,16},{16,24},{24,32},{32,40},{40,48},{48,56},{56,0},{1,9},... | collective-permute-start | bytes 786440 | tf_op jit(solution)/shard_map/gather/ppermute | solution.py:25
  46.1 12.1 %collective-permute-start.12 = (bf16[16,128,128]{2,1,0:T(8,128)(2,1)S(1)}, bf16[16,128,128]{2,1,0:T(8,128)(2,1)S(1)}, u32[]{:S(2)}, u32[]{:S(2)}) collective-permute-start(bf16[16,128,128]{2,1,0:T(8,128)(2,1)S(1)} %collective-permute-done.8.rest_8_), channel_id=1, source_target_pairs={{0,64},{64,128},{128,192},{192,0},{1,65},{65,129},{129,193},{193,1... | collective-permute-start | bytes 1572872 | tf_op jit(solution)/shard_map/gather/ppermute | solution.py:21
  47.6 5.9 %collective-permute-start.14 = (bf16[4,128,128]{2,1,0:T(8,128)(2,1)}, bf16[4,128,128]{2,1,0:T(8,128)(2,1)S(1)}, u32[]{:S(2)}, u32[]{:S(2)}) collective-permute-start(bf16[4,128,128]{2,1,0:T(8,128)(2,1)} %slice.166), channel_id=1, source_target_pairs={{0,56},{8,0},{16,8},{24,16},{32,24},{40,32},{48,40},{56,48},{1,57}... | collective-permute-start | bytes 393224 | tf_op jit(solution)/shard_map/gather/ppermute | solution.py:25
  51.4 6.7 %collective-permute-start.13 = (bf16[4,128,128]{2,1,0:T(8,128)(2,1)}, bf16[4,128,128]{2,1,0:T(8,128)(2,1)}, u32[]{:S(2)}, u32[]{:S(2)}) collective-permute-start(bf16[4,128,128]{2,1,0:T(8,128)(2,1)} %slice.165), channel_id=1, source_target_pairs={{0,8},{8,16},{16,24},{24,32},{32,40},{40,48},{48,56},{56,0},{1,9},... | collective-permute-start | bytes 393224 | tf_op jit(solution)/shard_map/gather/ppermute | solution.py:25
  58.1 2.8 %copy-start = (bf16[8,1,24,128,128]{4,3,2,1,0:T(8,128)(2,1)S(1)}, bf16[8,1,24,128,128]{4,3,2,1,0:T(8,128)(2,1)}, u32[]{:S(2)}) copy-start(bf16[8,1,24,128,128]{4,3,2,1,0:T(8,128)(2,1)} %edges.3) | copy-start | bytes 18874372
  60.9 17.5 %copy-start.2 = (bf16[256,256]{1,0:T(8,128)(2,1)S(1)}, bf16[256,256]{1,0:T(8,128)(2,1)}, u32[]{:S(2)}) copy-start(bf16[256,256]{1,0:T(8,128)(2,1)} %cot_ref.1) | copy-start | bytes 393220
  60.9 17.5 %copy-start.3 = (bf16[128,256]{1,0:T(8,128)(2,1)S(1)}, bf16[128,256]{1,0:T(8,128)(2,1)}, u32[]{:S(2)}) copy-start(bf16[128,256]{1,0:T(8,128)(2,1)} %weight_ref.1) | copy-start | bytes 196612
  60.9 24.6 %copy-start.1 = (bf16[8,1,24,128,128]{4,3,2,1,0:T(8,128)(2,1)S(1)}, bf16[8,1,24,128,128]{4,3,2,1,0:T(8,128)(2,1)}, u32[]{:S(2)}) copy-start(bf16[8,1,24,128,128]{4,3,2,1,0:T(8,128)(2,1)} %edges.3) | copy-start | bytes 18874372
  65.7 9.0 %collective-permute-start.15 = (bf16[2,128,128]{2,1,0:T(8,128)(2,1)S(1)}, bf16[2,128,128]{2,1,0:T(8,128)(2,1)S(1)}, u32[]{:S(2)}, u32[]{:S(2)}) collective-permute-start(bf16[2,128,128]{2,1,0:T(8,128)(2,1)S(1)} %get-tuple-element.51), channel_id=1, source_target_pairs={{0,1},{1,0},{2,3},{3,2},{4,5},{5,4},{6,7},{7,6},{8,9},{9,8},{10,11... | collective-permute-start | bytes 196616 | tf_op jit(solution)/shard_map/sections/ppermute | solution.py:30
  73.0 3.7 %collective-permute-start.16 = (bf16[2,128,128]{2,1,0:T(8,128)(2,1)S(1)}, bf16[2,128,128]{2,1,0:T(8,128)(2,1)S(1)}, u32[]{:S(2)}, u32[]{:S(2)}) collective-permute-start(bf16[2,128,128]{2,1,0:T(8,128)(2,1)S(1)} %get-tuple-element.52), channel_id=1, source_target_pairs={{0,2},{2,0},{1,3},{3,1},{4,6},{6,4},{5,7},{7,5},{8,10},{10,8},{9,1... | collective-permute-start | bytes 196616 | tf_op jit(solution)/shard_map/sections/ppermute | solution.py:30
  74.4 4.1 %collective-permute-start.17 = (bf16[2,128,128]{2,1,0:T(8,128)(2,1)S(1)}, bf16[2,128,128]{2,1,0:T(8,128)(2,1)S(1)}, u32[]{:S(2)}, u32[]{:S(2)}) collective-permute-start(bf16[2,128,128]{2,1,0:T(8,128)(2,1)S(1)} %get-tuple-element.53), channel_id=1, source_target_pairs={{0,3},{1,2},{2,1},{3,0},{4,7},{5,6},{6,5},{7,4},{8,11},{9,10},{10,... | collective-permute-start | bytes 196616 | tf_op jit(solution)/shard_map/sections/ppermute | solution.py:30
  80.0 2.5 %collective-permute-start.21 = (f32[160,128]{1,0:T(8,128)S(1)}, f32[160,128]{1,0:T(8,128)S(1)}, u32[]{:S(2)}, u32[]{:S(2)}) collective-permute-start(f32[160,128]{1,0:T(8,128)S(1)} %get-tuple-element.63), channel_id=1, source_target_pairs={{0,1},{1,0},{2,3},{3,2},{4,5},{5,4},{6,7},{7,6},{8,9},{9,8},{10,11... | collective-permute-start | bytes 245768 | tf_op jit(solution)/shard_map/weights/ppermute | solution.py:30
  80.4 4.2 %collective-permute-start.20 = (bf16[2,128,128]{2,1,0:T(8,128)(2,1)S(1)}, bf16[2,128,128]{2,1,0:T(8,128)(2,1)S(1)}, u32[]{:S(2)}, u32[]{:S(2)}) collective-permute-start(bf16[2,128,128]{2,1,0:T(8,128)(2,1)S(1)} %get-tuple-element.55.s0), channel_id=1, source_target_pairs={{0,3},{1,2},{2,1},{3,0},{4,7},{5,6},{6,5},{7,4},{8,11},{9,10},{10,... | collective-permute-start | bytes 196616 | tf_op jit(solution)/shard_map/slopes/ppermute | solution.py:30
  81.6 4.0 %collective-permute-start.19 = (bf16[2,128,128]{2,1,0:T(8,128)(2,1)S(1)}, bf16[2,128,128]{2,1,0:T(8,128)(2,1)S(1)}, u32[]{:S(2)}, u32[]{:S(2)}) collective-permute-start(bf16[2,128,128]{2,1,0:T(8,128)(2,1)S(1)} %get-tuple-element.55.s0), channel_id=1, source_target_pairs={{0,2},{2,0},{1,3},{3,1},{4,6},{6,4},{5,7},{7,5},{8,10},{10,8},{9,1... | collective-permute-start | bytes 196616 | tf_op jit(solution)/shard_map/slopes/ppermute | solution.py:30
  81.9 3.7 %collective-permute-start.18 = (bf16[2,128,128]{2,1,0:T(8,128)(2,1)S(1)}, bf16[2,128,128]{2,1,0:T(8,128)(2,1)S(1)}, u32[]{:S(2)}, u32[]{:S(2)}) collective-permute-start(bf16[2,128,128]{2,1,0:T(8,128)(2,1)S(1)} %get-tuple-element.55.s0), channel_id=1, source_target_pairs={{0,1},{1,0},{2,3},{3,2},{4,5},{5,4},{6,7},{7,6},{8,9},{9,8},{10,11... | collective-permute-start | bytes 196616 | tf_op jit(solution)/shard_map/slopes/ppermute | solution.py:30
  82.5 8.2 %collective-permute-start.22 = (f32[160,128]{1,0:T(8,128)S(1)}, f32[160,128]{1,0:T(8,128)S(1)}, u32[]{:S(2)}, u32[]{:S(2)}) collective-permute-start(f32[160,128]{1,0:T(8,128)S(1)} %add.175), channel_id=1, source_target_pairs={{0,2},{2,0},{1,3},{3,1},{4,6},{6,4},{5,7},{7,5},{8,10},{10,8},{9,1... | collective-permute-start | bytes 245768 | tf_op jit(solution)/shard_map/weights/ppermute | solution.py:30
  90.8 9.1 %collective-permute-start.23 = (bf16[1184,128]{1,0:T(8,128)(2,1)S(1)}, bf16[1184,128]{1,0:T(8,128)(2,1)S(1)}, u32[]{:S(2)}, u32[]{:S(2)}) collective-permute-start(bf16[1184,128]{1,0:T(8,128)(2,1)S(1)} %pad_maximum_fusion), channel_id=1, source_target_pairs={{0,4},{4,0},{1,5},{5,1},{2,6},{6,2},{3,7},{7,3},{8,12},{12,8},{9,1... | collective-permute-start | bytes 909320 | tf_op jit(solution)/shard_map/scatter/ppermute | solution.py:30
  93.6 17.6 %collective-permute-start.26 = (bf16[2048,128]{1,0:T(8,128)(2,1)S(1)}, bf16[2048,128]{1,0:T(8,128)(2,1)S(1)}, u32[]{:S(2)}, u32[]{:S(2)}) collective-permute-start(bf16[2048,128]{1,0:T(8,128)(2,1)S(1)} %bitcast.42), channel_id=1, source_target_pairs={{0,4},{4,0},{1,5},{5,1},{2,6},{6,2},{3,7},{7,3},{8,12},{12,8},{9,1... | collective-permute-start | bytes 1572872 | tf_op jit(solution)/shard_map/scatter/ppermute | solution.py:30
  100.1 11.1 %collective-permute-start.25 = (bf16[672,128]{1,0:T(8,128)(2,1)S(1)}, bf16[672,128]{1,0:T(8,128)(2,1)S(1)}, u32[]{:S(2)}, u32[]{:S(2)}) collective-permute-start(bf16[672,128]{1,0:T(8,128)(2,1)S(1)} %get-tuple-element.107), channel_id=1, source_target_pairs={{0,56},{8,0},{16,8},{24,16},{32,24},{40,32},{48,40},{56,48},{1,57}... | collective-permute-start | bytes 516104 | tf_op jit(solution)/shard_map/scatter/ppermute | solution.py:25
  100.2 11.0 %collective-permute-start.24 = (bf16[672,128]{1,0:T(8,128)(2,1)S(1)}, bf16[672,128]{1,0:T(8,128)(2,1)S(1)}, u32[]{:S(2)}, u32[]{:S(2)}) collective-permute-start(bf16[672,128]{1,0:T(8,128)(2,1)S(1)} %get-tuple-element.108), channel_id=1, source_target_pairs={{0,8},{8,16},{16,24},{24,32},{32,40},{40,48},{48,56},{56,0},{1,9},... | collective-permute-start | bytes 516104 | tf_op jit(solution)/shard_map/scatter/ppermute | solution.py:25
  101.6 20.8 %collective-permute-start.29 = (bf16[2048,128]{1,0:T(8,128)(2,1)S(1)}, bf16[2048,128]{1,0:T(8,128)(2,1)S(1)}, u32[]{:S(2)}, u32[]{:S(2)}) collective-permute-start(bf16[2048,128]{1,0:T(8,128)(2,1)S(1)} %bitcast.41), channel_id=1, source_target_pairs={{0,4},{4,0},{1,5},{5,1},{2,6},{6,2},{3,7},{7,3},{8,12},{12,8},{9,1... | collective-permute-start | bytes 1572872 | tf_op jit(solution)/shard_map/scatter/ppermute | solution.py:30
  111.5 10.9 %collective-permute-start.27 = (bf16[1184,128]{1,0:T(8,128)(2,1)S(1)}, bf16[1184,128]{1,0:T(8,128)(2,1)S(1)}, u32[]{:S(2)}, u32[]{:S(2)}) collective-permute-start(bf16[1184,128]{1,0:T(8,128)(2,1)S(1)} %pad_maximum_fusion.1), channel_id=1, source_target_pairs={{0,8},{8,16},{16,24},{24,32},{32,40},{40,48},{48,56},{56,0},{1,9},... | collective-permute-start | bytes 909320 | tf_op jit(solution)/shard_map/scatter/ppermute | solution.py:25
  111.6 10.8 %collective-permute-start.28 = (bf16[1184,128]{1,0:T(8,128)(2,1)S(1)}, bf16[1184,128]{1,0:T(8,128)(2,1)S(1)}, u32[]{:S(2)}, u32[]{:S(2)}) collective-permute-start(bf16[1184,128]{1,0:T(8,128)(2,1)S(1)} %pad_maximum_fusion.2), channel_id=1, source_target_pairs={{0,56},{8,0},{16,8},{24,16},{32,24},{40,32},{48,40},{56,48},{1,57}... | collective-permute-start | bytes 909320 | tf_op jit(solution)/shard_map/scatter/ppermute | solution.py:25
  114.3 19.3 %collective-permute-start.32 = (bf16[2048,128]{1,0:T(8,128)(2,1)S(1)}, bf16[2048,128]{1,0:T(8,128)(2,1)S(1)}, u32[]{:S(2)}, u32[]{:S(2)}) collective-permute-start(bf16[2048,128]{1,0:T(8,128)(2,1)S(1)} %bitcast.40), channel_id=1, source_target_pairs={{0,4},{4,0},{1,5},{5,1},{2,6},{6,2},{3,7},{7,3},{8,12},{12,8},{9,1... | collective-permute-start | bytes 1572872 | tf_op jit(solution)/shard_map/scatter/ppermute | solution.py:30
  122.7 10.9 %collective-permute-start.31 = (bf16[1184,128]{1,0:T(8,128)(2,1)S(1)}, bf16[1184,128]{1,0:T(8,128)(2,1)S(1)}, u32[]{:S(2)}, u32[]{:S(2)}) collective-permute-start(bf16[1184,128]{1,0:T(8,128)(2,1)S(1)} %pad_maximum_fusion.4), channel_id=1, source_target_pairs={{0,56},{8,0},{16,8},{24,16},{32,24},{40,32},{48,40},{56,48},{1,57}... | collective-permute-start | bytes 909320 | tf_op jit(solution)/shard_map/scatter/ppermute | solution.py:25
  122.8 10.8 %collective-permute-start.30 = (bf16[1184,128]{1,0:T(8,128)(2,1)S(1)}, bf16[1184,128]{1,0:T(8,128)(2,1)S(1)}, u32[]{:S(2)}, u32[]{:S(2)}) collective-permute-start(bf16[1184,128]{1,0:T(8,128)(2,1)S(1)} %pad_maximum_fusion.3), channel_id=1, source_target_pairs={{0,8},{8,16},{16,24},{24,32},{32,40},{40,48},{48,56},{56,0},{1,9},... | collective-permute-start | bytes 909320 | tf_op jit(solution)/shard_map/scatter/ppermute | solution.py:25
  133.9 8.6 %collective-permute-start.33 = (bf16[1184,128]{1,0:T(8,128)(2,1)S(1)}, bf16[1184,128]{1,0:T(8,128)(2,1)S(1)}, u32[]{:S(2)}, u32[]{:S(2)}) collective-permute-start(bf16[1184,128]{1,0:T(8,128)(2,1)S(1)} %pad_maximum_fusion.5), channel_id=1, source_target_pairs={{0,8},{8,16},{16,24},{24,32},{32,40},{40,48},{48,56},{56,0},{1,9},... | collective-permute-start | bytes 909320 | tf_op jit(solution)/shard_map/scatter/ppermute | solution.py:25
  134.0 7.3 %collective-permute-start.35 = (bf16[1024,128]{1,0:T(8,128)(2,1)S(1)}, bf16[1024,128]{1,0:T(8,128)(2,1)S(1)}, u32[]{:S(2)}, u32[]{:S(2)}) collective-permute-start(bf16[1024,128]{1,0:T(8,128)(2,1)S(1)} %bitcast.43), channel_id=1, source_target_pairs={{0,4},{4,0},{1,5},{5,1},{2,6},{6,2},{3,7},{7,3},{8,12},{12,8},{9,1... | collective-permute-start | bytes 786440 | tf_op jit(solution)/shard_map/scatter/ppermute | solution.py:30
  136.6 5.9 %collective-permute-start.34 = (bf16[1024,128]{1,0:T(8,128)(2,1)S(1)}, bf16[1024,128]{1,0:T(8,128)(2,1)S(1)}, u32[]{:S(2)}, u32[]{:S(2)}) collective-permute-start(bf16[1024,128]{1,0:T(8,128)(2,1)S(1)} %get-tuple-element.93), channel_id=1, source_target_pairs={{0,56},{8,0},{16,8},{24,16},{32,24},{40,32},{48,40},{56,48},{1,57}... | collective-permute-start | bytes 786440 | tf_op jit(solution)/shard_map/scatter/ppermute | solution.py:25
  142.7 6.0 %collective-permute-start.36 = (bf16[416,128]{1,0:T(8,128)(2,1)S(1)}, bf16[416,128]{1,0:T(8,128)(2,1)S(1)}, u32[]{:S(2)}, u32[]{:S(2)}) collective-permute-start(bf16[416,128]{1,0:T(8,128)(2,1)S(1)} %get-tuple-element.104), channel_id=1, source_target_pairs={{0,64},{64,128},{128,192},{192,0},{1,65},{65,129},{129,193},{193,1... | collective-permute-start | bytes 319496 | tf_op jit(solution)/shard_map/scatter/ppermute | solution.py:21
  142.8 5.9 %collective-permute-start.37 = (bf16[416,128]{1,0:T(8,128)(2,1)S(1)}, bf16[416,128]{1,0:T(8,128)(2,1)S(1)}, u32[]{:S(2)}, u32[]{:S(2)}) collective-permute-start(bf16[416,128]{1,0:T(8,128)(2,1)S(1)} %get-tuple-element.105), channel_id=1, source_target_pairs={{0,128},{64,192},{128,0},{192,64},{1,129},{65,193},{129,1},{193,65... | collective-permute-start | bytes 319496 | tf_op jit(solution)/shard_map/scatter/ppermute | solution.py:21
  143.1 6.2 %collective-permute-start.38 = (bf16[416,128]{1,0:T(8,128)(2,1)S(1)}, bf16[416,128]{1,0:T(8,128)(2,1)S(1)}, u32[]{:S(2)}, u32[]{:S(2)}) collective-permute-start(bf16[416,128]{1,0:T(8,128)(2,1)S(1)} %get-tuple-element.106), channel_id=1, source_target_pairs={{0,192},{64,0},{128,64},{192,128},{1,193},{65,1},{129,65},{193,129... | collective-permute-start | bytes 319496 | tf_op jit(solution)/shard_map/scatter/ppermute | solution.py:21
  149.4 6.2 %collective-permute-start.39 = (f32[160,128]{1,0:T(8,128)S(1)}, f32[160,128]{1,0:T(8,128)S(1)}, u32[]{:S(2)}, u32[]{:S(2)}) collective-permute-start(f32[160,128]{1,0:T(8,128)S(1)} %convert_add_fusion.8.mine_ref), channel_id=1, source_target_pairs={{0,1},{1,0},{2,3},{3,2},{4,5},{5,4},{6,7},{7,6},{8,9},{9,8},{10,11... | collective-permute-start | bytes 245768 | tf_op jit(solution)/shard_map/scatter/ppermute | solution.py:30

commit v5 on v4

--- a/solution.py
+++ b/solution.py
@@ -71,11 +71,13 @@
     rows, _, slots = edges.shape[:3]
     for piece, (place, size) in zip(pieces, places):
 
-        def copy(i, carry, piece=piece, place=place):
-            table[pl.ds(place + i * 4, 4)] = piece[pl.ds(i * 4, 4)]
+        unit = min(size, 8)
+
+        def copy(i, carry, piece=piece, place=place, unit=unit):
+            table[pl.ds(place + i * unit, unit)] = piece[pl.ds(i * unit, unit)]
             return carry
 
-        lax.fori_loop(0, size // 4, copy, 0)
+        lax.fori_loop(0, size // unit, copy, 0)
 
     def body(t, count, size):
         left = [live_tile(edges, t, s, count) for s in range(size)]
@@ -189,10 +191,10 @@
         for place, size in segments:
 
             def store(i, carry, out=out, place=place, offset=offset):
-                out[pl.ds(offset + i * 4, 4)] = totals[pl.ds(place + i * 4, 4)].astype(out.dtype)
+                out[pl.ds(offset + i * 8, 8)] = totals[pl.ds(place + i * 8, 8)].astype(out.dtype)
                 return carry
 
-            lax.fori_loop(0, size // 4, store, 0)
+            lax.fori_loop(0, size // 8, store, 0)
             offset += size
 
 

time: 156 us -> 156 us (level)
  starting transfers between devices: 67.6 us -> 59.5 us
  waiting for transfers between devices: 65.4 us -> 72.1 us
    ppermute x15, starting transfers between devices: 32.3 us -> 24.2 us  [swap(): return lax.ppermute(value, axes, pairs)]
    ppermute x15, waiting for transfers between devices: 38.5 us -> 45.9 us  [swap(): return lax.ppermute(value, axes, pairs)]
where the time goes in v5:
time: 156 us; the launch traced here: 155 us
  waiting for transfers between devices  72.1 us (46%)
  starting transfers between devices  59.5 us (38%)
  Pallas kernels  12.2 us (8%)
  local copies, waits for them, and re-layouts  6.64 us (4%)
  other arithmetic  3.42 us (2%)
    ppermute x15, waiting for transfers between devices, swap(): return lax.ppermute(value, axes, pairs)  45.9 us
    ppermute x15, starting transfers between devices, swap(): return lax.ppermute(value, axes, pairs)  24.2 us
    ppermute x16, starting transfers between devices, shift_z(): return lax.ppermute(value, 'z', [(i, (i + k) % NZ) for i in range(NZ)])  18.1 us
    ppermute x16, waiting for transfers between devices, shift_z(): return lax.ppermute(value, 'z', [(i, (i + k) % NZ) for i in range(NZ)])  12.6 us
    ppermute x9, waiting for transfers between devices, shift_x(): return lax.ppermute(value, 'x', [(i, (i + k) % NX) for i in range(NX)])  9.13 us
    ppermute x9, starting transfers between devices, shift_x(): return lax.ppermute(value, 'x', [(i, (i + k) % NX) for i in range(NX)])  8.88 us
    all_to_all x1, starting transfers between devices, gather_features(): line = lax.all_to_all(spread, 'z', 0, 0, tiled=True)  8.37 us
    pallas_call x1, Pallas kernels, backward(): pl.pallas_call(functools.partial(backward_kernel, places), out_shape=tupl...  5.04 us
  transfers between devices with their start and end apart: 41, of which 23 were waited for; matrix products, arithmetic and copies ran while one was open for 4% of the time, Pallas kernels for 3%

profile of v5, /device:TPU:1, one launch (start us, length us, event | category | flops | bytes accessed | tf_op | source)
XLA Modules:
  0.0 154.8 jit_solution(12385182381559352559)
XLA Ops:
  0.6 3.8 %collective-permute-start = (bf16[2,128,128]{2,1,0:T(8,128)(2,1)}, bf16[2,128,128]{2,1,0:T(8,128)(2,1)S(1)}, u32[]{:S(2)}, u32[]{:S(2)}) collective-permute-start(bf16[2,128,128]{2,1,0:T(8,128)(2,1)} %bitcast.44), channel_id=1, source_target_pairs={{0,4},{4,0},{1,5},{5,1},{2,6},{6,2},{3,7},{7,3},{8,12},{12,8},{9,1... | collective-permute-start | bytes 196616 | tf_op jit(solution)/shard_map/gather/ppermute | solution.py:30
  4.5 1.9 %collective-permute-done = bf16[2,128,128]{2,1,0:T(8,128)(2,1)S(1)} collective-permute-done((bf16[2,128,128]{2,1,0:T(8,128)(2,1)}, bf16[2,128,128]{2,1,0:T(8,128)(2,1)S(1)}, u32[]{:S(2)}, u32[]{:S(2)}) %collective-permute-start) | collective-permute-done | bytes 65568 | tf_op jit(solution)/shard_map/gather/ppermute | solution.py:30
  6.3 0.9 broadcast_in_dim.2
  7.2 8.4 %all-to-all-start = ((bf16[16,128,128]{2,1,0:T(8,128)(2,1)}), bf16[16,128,128]{2,1,0:T(8,128)(2,1)S(1)}, u32[]{:S(2)}, u32[]{:S(2)}) async-start(bf16[16,128,128]{2,1,0:T(8,128)(2,1)} %bitcast.3), calls=%async_computation | async-start | bytes 1048576 | tf_op jit(solution)/shard_map/gather/all_to_all | solution.py:253
  15.6 2.5 %collective-permute-start.3 = (bf16[2,128,128]{2,1,0:T(8,128)(2,1)}, bf16[2,128,128]{2,1,0:T(8,128)(2,1)S(1)}, u32[]{:S(2)}, u32[]{:S(2)}) collective-permute-start(bf16[2,128,128]{2,1,0:T(8,128)(2,1)} %bitcast.45), channel_id=1, source_target_pairs={{0,192},{64,0},{128,64},{192,128},{1,193},{65,1},{129,65},{193,129... | collective-permute-start | bytes 196616 | tf_op jit(solution)/shard_map/gather/ppermute | solution.py:21
  19.2 0.9 constant_dynamic-update-slice_fusion.3
  20.1 3.5 %collective-permute-done.1 = bf16[2,128,128]{2,1,0:T(8,128)(2,1)S(1)} collective-permute-done((bf16[2,128,128]{2,1,0:T(8,128)(2,1)}, bf16[2,128,128]{2,1,0:T(8,128)(2,1)S(1)}, u32[]{:S(2)}, u32[]{:S(2)}) %collective-permute-start.1) | collective-permute-done | bytes 65568 | tf_op jit(solution)/shard_map/gather/ppermute | solution.py:21
  23.7 3.0 %collective-permute-start.5 = (bf16[8,128,128]{2,1,0:T(8,128)(2,1)S(1)}, bf16[8,128,128]{2,1,0:T(8,128)(2,1)S(1)}, u32[]{:S(2)}, u32[]{:S(2)}) collective-permute-start(bf16[8,128,128]{2,1,0:T(8,128)(2,1)S(1)} %constant_dynamic-update-slice_fusion.rest_0_), channel_id=1, source_target_pairs={{0,56},{8,0},{16,8},{24,16},{32,24},{40,32},{48,40},{56,48},{1,57}... | collective-permute-start | bytes 786440 | tf_op jit(solution)/shard_map/gather/ppermute | solution.py:25
  26.7 4.5 %all-to-all-done.rest_1_ = bf16[16,128,128]{2,1,0:T(8,128)(2,1)S(1)} async-done(((bf16[16,128,128]{2,1,0:T(8,128)(2,1)}), bf16[16,128,128]{2,1,0:T(8,128)(2,1)S(1)}, u32[]{:S(2)}, u32[]{:S(2)}) %all-to-all-start) | async-done | bytes 524320 | tf_op jit(solution)/shard_map/gather/all_to_all | solution.py:253
  31.3 2.5 %collective-permute-start.9 = (bf16[16,128,128]{2,1,0:T(8,128)(2,1)S(1)}, bf16[16,128,128]{2,1,0:T(8,128)(2,1)S(1)}, u32[]{:S(2)}, u32[]{:S(2)}) collective-permute-start(bf16[16,128,128]{2,1,0:T(8,128)(2,1)S(1)} %all-to-all-done.rest_1_), channel_id=1, source_target_pairs={{0,192},{64,0},{128,64},{192,128},{1,193},{65,1},{129,65},{193,129... | collective-permute-start | bytes 1572872 | tf_op jit(solution)/shard_map/gather/ppermute | solution.py:21
  34.1 1.6 %collective-permute-start.7 = (bf16[8,128,128]{2,1,0:T(8,128)(2,1)S(1)}, bf16[8,128,128]{2,1,0:T(8,128)(2,1)}, u32[]{:S(2)}, u32[]{:S(2)}) collective-permute-start(bf16[8,128,128]{2,1,0:T(8,128)(2,1)S(1)} %collective-permute-done.5.rest_3_), channel_id=1, source_target_pairs={{0,56},{8,0},{16,8},{24,16},{32,24},{40,32},{48,40},{56,48},{1,57}... | collective-permute-start | bytes 786440 | tf_op jit(solution)/shard_map/gather/ppermute | solution.py:25
  35.7 4.0 %collective-permute-done.7.rest_5_ = bf16[8,128,128]{2,1,0:T(8,128)(2,1)} collective-permute-done((bf16[8,128,128]{2,1,0:T(8,128)(2,1)S(1)}, bf16[8,128,128]{2,1,0:T(8,128)(2,1)}, u32[]{:S(2)}, u32[]{:S(2)}) %collective-permute-start.7) | collective-permute-done | bytes 262176 | tf_op jit(solution)/shard_map/gather/ppermute | solution.py:25
  39.6 2.8 %collective-permute-start.11 = (bf16[8,128,128]{2,1,0:T(8,128)(2,1)}, bf16[8,128,128]{2,1,0:T(8,128)(2,1)S(1)}, u32[]{:S(2)}, u32[]{:S(2)}) collective-permute-start(bf16[8,128,128]{2,1,0:T(8,128)(2,1)} %collective-permute-done.7.rest_5_), channel_id=1, source_target_pairs={{0,56},{8,0},{16,8},{24,16},{32,24},{40,32},{48,40},{56,48},{1,57}... | collective-permute-start | bytes 786440 | tf_op jit(solution)/shard_map/gather/ppermute | solution.py:25
  42.4 1.7 %collective-permute-done.8.rest_8_ = bf16[16,128,128]{2,1,0:T(8,128)(2,1)S(1)} collective-permute-done((bf16[16,128,128]{2,1,0:T(8,128)(2,1)S(1)}, bf16[16,128,128]{2,1,0:T(8,128)(2,1)S(1)}, u32[]{:S(2)}, u32[]{:S(2)}) %collective-permute-start.8) | collective-permute-done | bytes 524320 | tf_op jit(solution)/shard_map/gather/ppermute | solution.py:21
  44.7 1.3 reduce.3
  46.2 0.8 collective-permute-done.11.rest_7_
  47.6 2.1 %collective-permute-start.14 = (bf16[4,128,128]{2,1,0:T(8,128)(2,1)}, bf16[4,128,128]{2,1,0:T(8,128)(2,1)S(1)}, u32[]{:S(2)}, u32[]{:S(2)}) collective-permute-start(bf16[4,128,128]{2,1,0:T(8,128)(2,1)} %slice.166), channel_id=1, source_target_pairs={{0,56},{8,0},{16,8},{24,16},{32,24},{40,32},{48,40},{56,48},{1,57}... | collective-permute-start | bytes 393224 | tf_op jit(solution)/shard_map/gather/ppermute | solution.py:25
  49.7 1.1 collective-permute-done.10.rest_6_
  51.5 0.7 pad_add_fusion
  52.2 1.3 collective-permute-done.14.rest_12_
  53.5 4.6 %collective-permute-done.13.rest_11_ = bf16[4,128,128]{2,1,0:T(8,128)(2,1)} collective-permute-done((bf16[4,128,128]{2,1,0:T(8,128)(2,1)}, bf16[4,128,128]{2,1,0:T(8,128)(2,1)}, u32[]{:S(2)}, u32[]{:S(2)}) %collective-permute-start.13) | collective-permute-done | bytes 131104 | tf_op jit(solution)/shard_map/gather/ppermute | solution.py:25
  58.1 2.8 %copy-done = bf16[8,1,24,128,128]{4,3,2,1,0:T(8,128)(2,1)S(1)} copy-done((bf16[8,1,24,128,128]{4,3,2,1,0:T(8,128)(2,1)S(1)}, bf16[8,1,24,128,128]{4,3,2,1,0:T(8,128)(2,1)}, u32[]{:S(2)}) %copy-start) | copy-done | bytes 6291480
  60.9 4.7 %forward.1 = (bf16[2,128,128]{2,1,0:T(8,128)(2,1)S(1)}, bf16[2,128,128]{2,1,0:T(8,128)(2,1)S(1)}, bf16[2,128,128]{2,1,0:T(8,128)(2,1)S(1)}, bf16[2,128,128]{2,1,0:T(8,128)(2,1)S(1)}) custom-call(s32[1]{0:T(128)} %bitcast.rep_ref, s32[200]{0:T(256)S(1)} %get-tuple-element.110.meta_ref, bf16[8,1,24,128,128]{4,3,2,1,0:T(8,128)(2,1)S(1)} %copy-done, ...), custom_call_target="tpu_custom_call" | custom-call | flops 805306368 | bytes 11534336 | tf_op jit(solution)/shard_map/forward/pallas_call | solution.py:102
  65.7 7.3 %collective-permute-start.15 = (bf16[2,128,128]{2,1,0:T(8,128)(2,1)S(1)}, bf16[2,128,128]{2,1,0:T(8,128)(2,1)S(1)}, u32[]{:S(2)}, u32[]{:S(2)}) collective-permute-start(bf16[2,128,128]{2,1,0:T(8,128)(2,1)S(1)} %get-tuple-element.51), channel_id=1, source_target_pairs={{0,1},{1,0},{2,3},{3,2},{4,5},{5,4},{6,7},{7,6},{8,9},{9,8},{10,11... | collective-permute-start | bytes 196616 | tf_op jit(solution)/shard_map/sections/ppermute | solution.py:30
  73.0 1.3 collective-permute-start.16
  74.7 1.9 %collective-permute-done.16.p2 = bf16[2,128,128]{2,1,0:T(8,128)(2,1)S(1)} collective-permute-done((bf16[2,128,128]{2,1,0:T(8,128)(2,1)S(1)}, bf16[2,128,128]{2,1,0:T(8,128)(2,1)S(1)}, u32[]{:S(2)}, u32[]{:S(2)}) %collective-permute-start.16) | collective-permute-done | bytes 65568 | tf_op jit(solution)/shard_map/sections/ppermute | solution.py:30
  76.6 1.7 %collective-permute-done.17.p3 = bf16[2,128,128]{2,1,0:T(8,128)(2,1)S(1)} collective-permute-done((bf16[2,128,128]{2,1,0:T(8,128)(2,1)S(1)}, bf16[2,128,128]{2,1,0:T(8,128)(2,1)S(1)}, u32[]{:S(2)}, u32[]{:S(2)}) %collective-permute-start.17) | collective-permute-done | bytes 65568 | tf_op jit(solution)/shard_map/sections/ppermute | solution.py:30
  78.4 1.6 %middle.1 = (bf16[256,256]{1,0:T(8,128)(2,1)}, bf16[2,128,128]{2,1,0:T(8,128)(2,1)S(1)}, f32[160,128]{1,0:T(8,128)S(1)}, f32[160,128]{1,0:T(8,128)S(1)}) custom-call(s32[1]{0:T(128)} %bitcast.rep_ref, bf16[2,128,128]{2,1,0:T(8,128)(2,1)S(1)} %get-tuple-element.50.p0, bf16[2,128,128]{2,1,0:T(8,128)(2,1)S(1)} %collective-permute-done.15.p1, ...), custom_call_target="tpu_custom_call" | custom-call | tf_op jit(solution)/shard_map/middle/pallas_call | solution.py:148
  80.3 1.2 collective-permute-start.20
  82.5 1.1 collective-permute-start.22
  83.6 0.9 collective-permute-done.20.s3
  84.5 1.0 collective-permute-done.19.s2
  85.5 5.0 %backward.1 = (bf16[8,128,128]{2,1,0:T(8,128)(2,1)S(1)}, bf16[8,128,128]{2,1,0:T(8,128)(2,1)S(1)}, bf16[8,128,128]{2,1,0:T(8,128)(2,1)S(1)}, bf16[8,128,128]{2,1...) custom-call(s32[1]{0:T(128)} %bitcast.rep_ref, ...), custom_call_target="tpu_custom_call" | custom-call | flops 805306368 | bytes 15728640 | tf_op jit(solution)/shard_map/backward/pallas_call | solution.py:204
  90.7 3.0 %collective-permute-start.26 = (bf16[2048,128]{1,0:T(8,128)(2,1)S(1)}, bf16[2048,128]{1,0:T(8,128)(2,1)S(1)}, u32[]{:S(2)}, u32[]{:S(2)}) collective-permute-start(bf16[2048,128]{1,0:T(8,128)(2,1)S(1)} %bitcast.42), channel_id=1, source_target_pairs={{0,4},{4,0},{1,5},{5,1},{2,6},{6,2},{3,7},{7,3},{8,12},{12,8},{9,1... | collective-permute-start | bytes 1572872 | tf_op jit(solution)/shard_map/scatter/ppermute | solution.py:30
  93.7 6.1 %collective-permute-done.23 = bf16[1184,128]{1,0:T(8,128)(2,1)S(1)} collective-permute-done((bf16[1184,128]{1,0:T(8,128)(2,1)S(1)}, bf16[1184,128]{1,0:T(8,128)(2,1)S(1)}, u32[]{:S(2)}, u32[]{:S(2)}) %collective-permute-start.23) | collective-permute-done | bytes 303136 | tf_op jit(solution)/shard_map/scatter/ppermute | solution.py:30
  100.0 1.5 collective-permute-start.24
  101.5 9.5 %collective-permute-done.26 = bf16[2048,128]{1,0:T(8,128)(2,1)S(1)} collective-permute-done((bf16[2048,128]{1,0:T(8,128)(2,1)S(1)}, bf16[2048,128]{1,0:T(8,128)(2,1)S(1)}, u32[]{:S(2)}, u32[]{:S(2)}) %collective-permute-start.26) | collective-permute-done | bytes 524320 | tf_op jit(solution)/shard_map/scatter/ppermute | solution.py:30
  111.5 2.7 %collective-permute-start.28 = (bf16[1184,128]{1,0:T(8,128)(2,1)S(1)}, bf16[1184,128]{1,0:T(8,128)(2,1)S(1)}, u32[]{:S(2)}, u32[]{:S(2)}) collective-permute-start(bf16[1184,128]{1,0:T(8,128)(2,1)S(1)} %pad_maximum_fusion.2), channel_id=1, source_target_pairs={{0,56},{8,0},{16,8},{24,16},{32,24},{40,32},{48,40},{56,48},{1,57}... | collective-permute-start | bytes 909320 | tf_op jit(solution)/shard_map/scatter/ppermute | solution.py:25
  114.2 8.0 %collective-permute-done.29 = bf16[2048,128]{1,0:T(8,128)(2,1)S(1)} collective-permute-done((bf16[2048,128]{1,0:T(8,128)(2,1)S(1)}, bf16[2048,128]{1,0:T(8,128)(2,1)S(1)}, u32[]{:S(2)}, u32[]{:S(2)}) %collective-permute-start.29) | collective-permute-done | bytes 524320 | tf_op jit(solution)/shard_map/scatter/ppermute | solution.py:30
  122.7 1.5 collective-permute-start.30
  124.2 9.3 %collective-permute-done.32 = bf16[2048,128]{1,0:T(8,128)(2,1)S(1)} collective-permute-done((bf16[2048,128]{1,0:T(8,128)(2,1)S(1)}, bf16[2048,128]{1,0:T(8,128)(2,1)S(1)}, u32[]{:S(2)}, u32[]{:S(2)}) %collective-permute-start.32) | collective-permute-done | bytes 524320 | tf_op jit(solution)/shard_map/scatter/ppermute | solution.py:30
  134.0 2.6 %collective-permute-start.34 = (bf16[1024,128]{1,0:T(8,128)(2,1)S(1)}, bf16[1024,128]{1,0:T(8,128)(2,1)S(1)}, u32[]{:S(2)}, u32[]{:S(2)}) collective-permute-start(bf16[1024,128]{1,0:T(8,128)(2,1)S(1)} %get-tuple-element.93), channel_id=1, source_target_pairs={{0,56},{8,0},{16,8},{24,16},{32,24},{40,32},{48,40},{56,48},{1,57}... | collective-permute-start | bytes 786440 | tf_op jit(solution)/shard_map/scatter/ppermute | solution.py:25
  136.6 4.6 %collective-permute-done.35 = bf16[1024,128]{1,0:T(8,128)(2,1)S(1)} collective-permute-done((bf16[1024,128]{1,0:T(8,128)(2,1)S(1)}, bf16[1024,128]{1,0:T(8,128)(2,1)S(1)}, u32[]{:S(2)}, u32[]{:S(2)}) %collective-permute-start.35) | collective-permute-done | bytes 262176 | tf_op jit(solution)/shard_map/scatter/ppermute | solution.py:30
  142.7 2.0 %collective-permute-start.38 = (bf16[416,128]{1,0:T(8,128)(2,1)S(1)}, bf16[416,128]{1,0:T(8,128)(2,1)S(1)}, u32[]{:S(2)}, u32[]{:S(2)}) collective-permute-start(bf16[416,128]{1,0:T(8,128)(2,1)S(1)} %get-tuple-element.106), channel_id=1, source_target_pairs={{0,192},{64,0},{128,64},{192,128},{1,193},{65,1},{129,65},{193,129... | collective-permute-start | bytes 319496 | tf_op jit(solution)/shard_map/scatter/ppermute | solution.py:21
  144.7 3.2 %collective-permute-done.36 = bf16[416,128]{1,0:T(8,128)(2,1)S(1)} collective-permute-done((bf16[416,128]{1,0:T(8,128)(2,1)S(1)}, bf16[416,128]{1,0:T(8,128)(2,1)S(1)}, u32[]{:S(2)}, u32[]{:S(2)}) %collective-permute-start.36) | collective-permute-done | bytes 106528 | tf_op jit(solution)/shard_map/scatter/ppermute | solution.py:21
  148.6 4.5 %collective-permute-start.39 = (f32[160,128]{1,0:T(8,128)S(1)}, f32[160,128]{1,0:T(8,128)S(1)}, u32[]{:S(2)}, u32[]{:S(2)}) collective-permute-start(f32[160,128]{1,0:T(8,128)S(1)} %convert_add_fusion.8.mine_ref), channel_id=1, source_target_pairs={{0,1},{1,0},{2,3},{3,2},{4,5},{5,4},{6,7},{7,6},{8,9},{9,8},{10,11... | collective-permute-start | bytes 245768 | tf_op jit(solution)/shard_map/scatter/ppermute | solution.py:30
  153.1 0.9 collective-permute-done.39.theirs_ref
  154.0 0.8 last.1
  (91 shorter events, 9.1 us)
Async XLA Ops:
  0.6 5.7 %collective-permute-start = (bf16[2,128,128]{2,1,0:T(8,128)(2,1)}, bf16[2,128,128]{2,1,0:T(8,128)(2,1)S(1)}, u32[]{:S(2)}, u32[]{:S(2)}) collective-permute-start(bf16[2,128,128]{2,1,0:T(8,128)(2,1)} %bitcast.44), channel_id=1, source_target_pairs={{0,4},{4,0},{1,5},{5,1},{2,6},{6,2},{3,7},{7,3},{8,12},{12,8},{9,1... | collective-permute-start | bytes 196616 | tf_op jit(solution)/shard_map/gather/ppermute | solution.py:30
  7.2 71.1 %copy-start.4 = (f32[256]{0:T(256)S(1)}, f32[256]{0:T(256)}, u32[]{:S(2)}) copy-start(f32[256]{0:T(256)} %param.9) | copy-start | bytes 3076
  7.2 24.0 %all-to-all-start = ((bf16[16,128,128]{2,1,0:T(8,128)(2,1)}), bf16[16,128,128]{2,1,0:T(8,128)(2,1)S(1)}, u32[]{:S(2)}, u32[]{:S(2)}) async-start(bf16[16,128,128]{2,1,0:T(8,128)(2,1)} %bitcast.3), calls=%async_computation | async-start | bytes 1048576 | tf_op jit(solution)/shard_map/gather/all_to_all | solution.py:253
  15.6 8.1 %collective-permute-start.3 = (bf16[2,128,128]{2,1,0:T(8,128)(2,1)}, bf16[2,128,128]{2,1,0:T(8,128)(2,1)S(1)}, u32[]{:S(2)}, u32[]{:S(2)}) collective-permute-start(bf16[2,128,128]{2,1,0:T(8,128)(2,1)} %bitcast.45), channel_id=1, source_target_pairs={{0,192},{64,0},{128,64},{192,128},{1,193},{65,1},{129,65},{193,129... | collective-permute-start | bytes 196616 | tf_op jit(solution)/shard_map/gather/ppermute | solution.py:21
  18.1 5.5 %collective-permute-start.2 = (bf16[2,128,128]{2,1,0:T(8,128)(2,1)}, bf16[2,128,128]{2,1,0:T(8,128)(2,1)S(1)}, u32[]{:S(2)}, u32[]{:S(2)}) collective-permute-start(bf16[2,128,128]{2,1,0:T(8,128)(2,1)} %bitcast.46), channel_id=1, source_target_pairs={{0,128},{64,192},{128,0},{192,64},{1,129},{65,193},{129,1},{193,65... | collective-permute-start | bytes 196616 | tf_op jit(solution)/shard_map/gather/ppermute | solution.py:21
  18.6 5.0 %collective-permute-start.1 = (bf16[2,128,128]{2,1,0:T(8,128)(2,1)}, bf16[2,128,128]{2,1,0:T(8,128)(2,1)S(1)}, u32[]{:S(2)}, u32[]{:S(2)}) collective-permute-start(bf16[2,128,128]{2,1,0:T(8,128)(2,1)} %bitcast.47), channel_id=1, source_target_pairs={{0,64},{64,128},{128,192},{192,0},{1,65},{65,129},{129,193},{193,1... | collective-permute-start | bytes 196616 | tf_op jit(solution)/shard_map/gather/ppermute | solution.py:21
  23.7 10.4 %collective-permute-start.5 = (bf16[8,128,128]{2,1,0:T(8,128)(2,1)S(1)}, bf16[8,128,128]{2,1,0:T(8,128)(2,1)S(1)}, u32[]{:S(2)}, u32[]{:S(2)}) collective-permute-start(bf16[8,128,128]{2,1,0:T(8,128)(2,1)S(1)} %constant_dynamic-update-slice_fusion.rest_0_), channel_id=1, source_target_pairs={{0,56},{8,0},{16,8},{24,16},{32,24},{40,32},{48,40},{56,48},{1,57}... | collective-permute-start | bytes 786440 | tf_op jit(solution)/shard_map/gather/ppermute | solution.py:25
  26.7 8.9 %collective-permute-start.4 = (bf16[8,128,128]{2,1,0:T(8,128)(2,1)S(1)}, bf16[8,128,128]{2,1,0:T(8,128)(2,1)S(1)}, u32[]{:S(2)}, u32[]{:S(2)}) collective-permute-start(bf16[8,128,128]{2,1,0:T(8,128)(2,1)S(1)} %constant_dynamic-update-slice_fusion.rest_0_), channel_id=1, source_target_pairs={{0,8},{8,16},{16,24},{24,32},{32,40},{40,48},{48,56},{56,0},{1,9},... | collective-permute-start | bytes 786440 | tf_op jit(solution)/shard_map/gather/ppermute | solution.py:25
  31.3 11.1 %collective-permute-start.9 = (bf16[16,128,128]{2,1,0:T(8,128)(2,1)S(1)}, bf16[16,128,128]{2,1,0:T(8,128)(2,1)S(1)}, u32[]{:S(2)}, u32[]{:S(2)}) collective-permute-start(bf16[16,128,128]{2,1,0:T(8,128)(2,1)S(1)} %all-to-all-done.rest_1_), channel_id=1, source_target_pairs={{0,192},{64,0},{128,64},{192,128},{1,193},{65,1},{129,65},{193,129... | collective-permute-start | bytes 1572872 | tf_op jit(solution)/shard_map/gather/ppermute | solution.py:21
  33.8 10.4 %collective-permute-start.8 = (bf16[16,128,128]{2,1,0:T(8,128)(2,1)S(1)}, bf16[16,128,128]{2,1,0:T(8,128)(2,1)S(1)}, u32[]{:S(2)}, u32[]{:S(2)}) collective-permute-start(bf16[16,128,128]{2,1,0:T(8,128)(2,1)S(1)} %all-to-all-done.rest_1_), channel_id=1, source_target_pairs={{0,64},{64,128},{128,192},{192,0},{1,65},{65,129},{129,193},{193,1... | collective-permute-start | bytes 1572872 | tf_op jit(solution)/shard_map/gather/ppermute | solution.py:21
  34.1 5.5 %collective-permute-start.7 = (bf16[8,128,128]{2,1,0:T(8,128)(2,1)S(1)}, bf16[8,128,128]{2,1,0:T(8,128)(2,1)}, u32[]{:S(2)}, u32[]{:S(2)}) collective-permute-start(bf16[8,128,128]{2,1,0:T(8,128)(2,1)S(1)} %collective-permute-done.5.rest_3_), channel_id=1, source_target_pairs={{0,56},{8,0},{16,8},{24,16},{32,24},{40,32},{48,40},{56,48},{1,57}... | collective-permute-start | bytes 786440 | tf_op jit(solution)/shard_map/gather/ppermute | solution.py:25
  35.7 6.7 %collective-permute-start.6 = (bf16[8,128,128]{2,1,0:T(8,128)(2,1)S(1)}, bf16[8,128,128]{2,1,0:T(8,128)(2,1)}, u32[]{:S(2)}, u32[]{:S(2)}) collective-permute-start(bf16[8,128,128]{2,1,0:T(8,128)(2,1)S(1)} %collective-permute-done.4.rest_2_), channel_id=1, source_target_pairs={{0,8},{8,16},{16,24},{24,32},{32,40},{40,48},{48,56},{56,0},{1,9},... | collective-permute-start | bytes 786440 | tf_op jit(solution)/shard_map/gather/ppermute | solution.py:25
  39.6 7.3 %collective-permute-start.11 = (bf16[8,128,128]{2,1,0:T(8,128)(2,1)}, bf16[8,128,128]{2,1,0:T(8,128)(2,1)S(1)}, u32[]{:S(2)}, u32[]{:S(2)}) collective-permute-start(bf16[8,128,128]{2,1,0:T(8,128)(2,1)} %collective-permute-done.7.rest_5_), channel_id=1, source_target_pairs={{0,56},{8,0},{16,8},{24,16},{32,24},{40,32},{48,40},{56,48},{1,57}... | collective-permute-start | bytes 786440 | tf_op jit(solution)/shard_map/gather/ppermute | solution.py:25
  44.1 6.6 %collective-permute-start.10 = (bf16[8,128,128]{2,1,0:T(8,128)(2,1)}, bf16[8,128,128]{2,1,0:T(8,128)(2,1)S(1)}, u32[]{:S(2)}, u32[]{:S(2)}) collective-permute-start(bf16[8,128,128]{2,1,0:T(8,128)(2,1)} %collective-permute-done.6.rest_4_), channel_id=1, source_target_pairs={{0,8},{8,16},{16,24},{24,32},{32,40},{40,48},{48,56},{56,0},{1,9},... | collective-permute-start | bytes 786440 | tf_op jit(solution)/shard_map/gather/ppermute | solution.py:25
  46.1 12.1 %collective-permute-start.12 = (bf16[16,128,128]{2,1,0:T(8,128)(2,1)S(1)}, bf16[16,128,128]{2,1,0:T(8,128)(2,1)S(1)}, u32[]{:S(2)}, u32[]{:S(2)}) collective-permute-start(bf16[16,128,128]{2,1,0:T(8,128)(2,1)S(1)} %collective-permute-done.8.rest_8_), channel_id=1, source_target_pairs={{0,64},{64,128},{128,192},{192,0},{1,65},{65,129},{129,193},{193,1... | collective-permute-start | bytes 1572872 | tf_op jit(solution)/shard_map/gather/ppermute | solution.py:21
  47.6 5.9 %collective-permute-start.14 = (bf16[4,128,128]{2,1,0:T(8,128)(2,1)}, bf16[4,128,128]{2,1,0:T(8,128)(2,1)S(1)}, u32[]{:S(2)}, u32[]{:S(2)}) collective-permute-start(bf16[4,128,128]{2,1,0:T(8,128)(2,1)} %slice.166), channel_id=1, source_target_pairs={{0,56},{8,0},{16,8},{24,16},{32,24},{40,32},{48,40},{56,48},{1,57}... | collective-permute-start | bytes 393224 | tf_op jit(solution)/shard_map/gather/ppermute | solution.py:25
  51.4 6.7 %collective-permute-start.13 = (bf16[4,128,128]{2,1,0:T(8,128)(2,1)}, bf16[4,128,128]{2,1,0:T(8,128)(2,1)}, u32[]{:S(2)}, u32[]{:S(2)}) collective-permute-start(bf16[4,128,128]{2,1,0:T(8,128)(2,1)} %slice.165), channel_id=1, source_target_pairs={{0,8},{8,16},{16,24},{24,32},{32,40},{40,48},{48,56},{56,0},{1,9},... | collective-permute-start | bytes 393224 | tf_op jit(solution)/shard_map/gather/ppermute | solution.py:25
  58.1 2.8 %copy-start = (bf16[8,1,24,128,128]{4,3,2,1,0:T(8,128)(2,1)S(1)}, bf16[8,1,24,128,128]{4,3,2,1,0:T(8,128)(2,1)}, u32[]{:S(2)}) copy-start(bf16[8,1,24,128,128]{4,3,2,1,0:T(8,128)(2,1)} %edges.3) | copy-start | bytes 18874372
  60.9 17.5 %copy-start.2 = (bf16[256,256]{1,0:T(8,128)(2,1)S(1)}, bf16[256,256]{1,0:T(8,128)(2,1)}, u32[]{:S(2)}) copy-start(bf16[256,256]{1,0:T(8,128)(2,1)} %cot_ref.1) | copy-start | bytes 393220
  60.9 17.5 %copy-start.3 = (bf16[128,256]{1,0:T(8,128)(2,1)S(1)}, bf16[128,256]{1,0:T(8,128)(2,1)}, u32[]{:S(2)}) copy-start(bf16[128,256]{1,0:T(8,128)(2,1)} %weight_ref.1) | copy-start | bytes 196612
  60.9 24.6 %copy-start.1 = (bf16[8,1,24,128,128]{4,3,2,1,0:T(8,128)(2,1)S(1)}, bf16[8,1,24,128,128]{4,3,2,1,0:T(8,128)(2,1)}, u32[]{:S(2)}) copy-start(bf16[8,1,24,128,128]{4,3,2,1,0:T(8,128)(2,1)} %edges.3) | copy-start | bytes 18874372
  65.7 9.0 %collective-permute-start.15 = (bf16[2,128,128]{2,1,0:T(8,128)(2,1)S(1)}, bf16[2,128,128]{2,1,0:T(8,128)(2,1)S(1)}, u32[]{:S(2)}, u32[]{:S(2)}) collective-permute-start(bf16[2,128,128]{2,1,0:T(8,128)(2,1)S(1)} %get-tuple-element.51), channel_id=1, source_target_pairs={{0,1},{1,0},{2,3},{3,2},{4,5},{5,4},{6,7},{7,6},{8,9},{9,8},{10,11... | collective-permute-start | bytes 196616 | tf_op jit(solution)/shard_map/sections/ppermute | solution.py:30
  73.0 3.7 %collective-permute-start.16 = (bf16[2,128,128]{2,1,0:T(8,128)(2,1)S(1)}, bf16[2,128,128]{2,1,0:T(8,128)(2,1)S(1)}, u32[]{:S(2)}, u32[]{:S(2)}) collective-permute-start(bf16[2,128,128]{2,1,0:T(8,128)(2,1)S(1)} %get-tuple-element.52), channel_id=1, source_target_pairs={{0,2},{2,0},{1,3},{3,1},{4,6},{6,4},{5,7},{7,5},{8,10},{10,8},{9,1... | collective-permute-start | bytes 196616 | tf_op jit(solution)/shard_map/sections/ppermute | solution.py:30
  74.3 4.1 %collective-permute-start.17 = (bf16[2,128,128]{2,1,0:T(8,128)(2,1)S(1)}, bf16[2,128,128]{2,1,0:T(8,128)(2,1)S(1)}, u32[]{:S(2)}, u32[]{:S(2)}) collective-permute-start(bf16[2,128,128]{2,1,0:T(8,128)(2,1)S(1)} %get-tuple-element.53), channel_id=1, source_target_pairs={{0,3},{1,2},{2,1},{3,0},{4,7},{5,6},{6,5},{7,4},{8,11},{9,10},{10,... | collective-permute-start | bytes 196616 | tf_op jit(solution)/shard_map/sections/ppermute | solution.py:30
  79.9 2.5 %collective-permute-start.21 = (f32[160,128]{1,0:T(8,128)S(1)}, f32[160,128]{1,0:T(8,128)S(1)}, u32[]{:S(2)}, u32[]{:S(2)}) collective-permute-start(f32[160,128]{1,0:T(8,128)S(1)} %get-tuple-element.63), channel_id=1, source_target_pairs={{0,1},{1,0},{2,3},{3,2},{4,5},{5,4},{6,7},{7,6},{8,9},{9,8},{10,11... | collective-permute-start | bytes 245768 | tf_op jit(solution)/shard_map/weights/ppermute | solution.py:30
  80.3 4.2 %collective-permute-start.20 = (bf16[2,128,128]{2,1,0:T(8,128)(2,1)S(1)}, bf16[2,128,128]{2,1,0:T(8,128)(2,1)S(1)}, u32[]{:S(2)}, u32[]{:S(2)}) collective-permute-start(bf16[2,128,128]{2,1,0:T(8,128)(2,1)S(1)} %get-tuple-element.55.s0), channel_id=1, source_target_pairs={{0,3},{1,2},{2,1},{3,0},{4,7},{5,6},{6,5},{7,4},{8,11},{9,10},{10,... | collective-permute-start | bytes 196616 | tf_op jit(solution)/shard_map/slopes/ppermute | solution.py:30
  81.5 4.0 %collective-permute-start.19 = (bf16[2,128,128]{2,1,0:T(8,128)(2,1)S(1)}, bf16[2,128,128]{2,1,0:T(8,128)(2,1)S(1)}, u32[]{:S(2)}, u32[]{:S(2)}) collective-permute-start(bf16[2,128,128]{2,1,0:T(8,128)(2,1)S(1)} %get-tuple-element.55.s0), channel_id=1, source_target_pairs={{0,2},{2,0},{1,3},{3,1},{4,6},{6,4},{5,7},{7,5},{8,10},{10,8},{9,1... | collective-permute-start | bytes 196616 | tf_op jit(solution)/shard_map/slopes/ppermute | solution.py:30
  81.8 3.7 %collective-permute-start.18 = (bf16[2,128,128]{2,1,0:T(8,128)(2,1)S(1)}, bf16[2,128,128]{2,1,0:T(8,128)(2,1)S(1)}, u32[]{:S(2)}, u32[]{:S(2)}) collective-permute-start(bf16[2,128,128]{2,1,0:T(8,128)(2,1)S(1)} %get-tuple-element.55.s0), channel_id=1, source_target_pairs={{0,1},{1,0},{2,3},{3,2},{4,5},{5,4},{6,7},{7,6},{8,9},{9,8},{10,11... | collective-permute-start | bytes 196616 | tf_op jit(solution)/shard_map/slopes/ppermute | solution.py:30
  82.5 8.1 %collective-permute-start.22 = (f32[160,128]{1,0:T(8,128)S(1)}, f32[160,128]{1,0:T(8,128)S(1)}, u32[]{:S(2)}, u32[]{:S(2)}) collective-permute-start(f32[160,128]{1,0:T(8,128)S(1)} %add.175), channel_id=1, source_target_pairs={{0,2},{2,0},{1,3},{3,1},{4,6},{6,4},{5,7},{7,5},{8,10},{10,8},{9,1... | collective-permute-start | bytes 245768 | tf_op jit(solution)/shard_map/weights/ppermute | solution.py:30
  90.6 9.1 %collective-permute-start.23 = (bf16[1184,128]{1,0:T(8,128)(2,1)S(1)}, bf16[1184,128]{1,0:T(8,128)(2,1)S(1)}, u32[]{:S(2)}, u32[]{:S(2)}) collective-permute-start(bf16[1184,128]{1,0:T(8,128)(2,1)S(1)} %pad_maximum_fusion), channel_id=1, source_target_pairs={{0,4},{4,0},{1,5},{5,1},{2,6},{6,2},{3,7},{7,3},{8,12},{12,8},{9,1... | collective-permute-start | bytes 909320 | tf_op jit(solution)/shard_map/scatter/ppermute | solution.py:30
  90.7 20.3 %collective-permute-start.26 = (bf16[2048,128]{1,0:T(8,128)(2,1)S(1)}, bf16[2048,128]{1,0:T(8,128)(2,1)S(1)}, u32[]{:S(2)}, u32[]{:S(2)}) collective-permute-start(bf16[2048,128]{1,0:T(8,128)(2,1)S(1)} %bitcast.42), channel_id=1, source_target_pairs={{0,4},{4,0},{1,5},{5,1},{2,6},{6,2},{3,7},{7,3},{8,12},{12,8},{9,1... | collective-permute-start | bytes 1572872 | tf_op jit(solution)/shard_map/scatter/ppermute | solution.py:30
  99.9 11.1 %collective-permute-start.25 = (bf16[672,128]{1,0:T(8,128)(2,1)S(1)}, bf16[672,128]{1,0:T(8,128)(2,1)S(1)}, u32[]{:S(2)}, u32[]{:S(2)}) collective-permute-start(bf16[672,128]{1,0:T(8,128)(2,1)S(1)} %get-tuple-element.107), channel_id=1, source_target_pairs={{0,56},{8,0},{16,8},{24,16},{32,24},{40,32},{48,40},{56,48},{1,57}... | collective-permute-start | bytes 516104 | tf_op jit(solution)/shard_map/scatter/ppermute | solution.py:25
  100.0 11.0 %collective-permute-start.24 = (bf16[672,128]{1,0:T(8,128)(2,1)S(1)}, bf16[672,128]{1,0:T(8,128)(2,1)S(1)}, u32[]{:S(2)}, u32[]{:S(2)}) collective-permute-start(bf16[672,128]{1,0:T(8,128)(2,1)S(1)} %get-tuple-element.108), channel_id=1, source_target_pairs={{0,8},{8,16},{16,24},{24,32},{32,40},{40,48},{48,56},{56,0},{1,9},... | collective-permute-start | bytes 516104 | tf_op jit(solution)/shard_map/scatter/ppermute | solution.py:25
  101.5 20.8 %collective-permute-start.29 = (bf16[2048,128]{1,0:T(8,128)(2,1)S(1)}, bf16[2048,128]{1,0:T(8,128)(2,1)S(1)}, u32[]{:S(2)}, u32[]{:S(2)}) collective-permute-start(bf16[2048,128]{1,0:T(8,128)(2,1)S(1)} %bitcast.41), channel_id=1, source_target_pairs={{0,4},{4,0},{1,5},{5,1},{2,6},{6,2},{3,7},{7,3},{8,12},{12,8},{9,1... | collective-permute-start | bytes 1572872 | tf_op jit(solution)/shard_map/scatter/ppermute | solution.py:30
  111.3 10.9 %collective-permute-start.27 = (bf16[1184,128]{1,0:T(8,128)(2,1)S(1)}, bf16[1184,128]{1,0:T(8,128)(2,1)S(1)}, u32[]{:S(2)}, u32[]{:S(2)}) collective-permute-start(bf16[1184,128]{1,0:T(8,128)(2,1)S(1)} %pad_maximum_fusion.1), channel_id=1, source_target_pairs={{0,8},{8,16},{16,24},{24,32},{32,40},{40,48},{48,56},{56,0},{1,9},... | collective-permute-start | bytes 909320 | tf_op jit(solution)/shard_map/scatter/ppermute | solution.py:25
  111.5 10.8 %collective-permute-start.28 = (bf16[1184,128]{1,0:T(8,128)(2,1)S(1)}, bf16[1184,128]{1,0:T(8,128)(2,1)S(1)}, u32[]{:S(2)}, u32[]{:S(2)}) collective-permute-start(bf16[1184,128]{1,0:T(8,128)(2,1)S(1)} %pad_maximum_fusion.2), channel_id=1, source_target_pairs={{0,56},{8,0},{16,8},{24,16},{32,24},{40,32},{48,40},{56,48},{1,57}... | collective-permute-start | bytes 909320 | tf_op jit(solution)/shard_map/scatter/ppermute | solution.py:25
  114.2 19.3 %collective-permute-start.32 = (bf16[2048,128]{1,0:T(8,128)(2,1)S(1)}, bf16[2048,128]{1,0:T(8,128)(2,1)S(1)}, u32[]{:S(2)}, u32[]{:S(2)}) collective-permute-start(bf16[2048,128]{1,0:T(8,128)(2,1)S(1)} %bitcast.40), channel_id=1, source_target_pairs={{0,4},{4,0},{1,5},{5,1},{2,6},{6,2},{3,7},{7,3},{8,12},{12,8},{9,1... | collective-permute-start | bytes 1572872 | tf_op jit(solution)/shard_map/scatter/ppermute | solution.py:30
  122.6 10.9 %collective-permute-start.31 = (bf16[1184,128]{1,0:T(8,128)(2,1)S(1)}, bf16[1184,128]{1,0:T(8,128)(2,1)S(1)}, u32[]{:S(2)}, u32[]{:S(2)}) collective-permute-start(bf16[1184,128]{1,0:T(8,128)(2,1)S(1)} %pad_maximum_fusion.4), channel_id=1, source_target_pairs={{0,56},{8,0},{16,8},{24,16},{32,24},{40,32},{48,40},{56,48},{1,57}... | collective-permute-start | bytes 909320 | tf_op jit(solution)/shard_map/scatter/ppermute | solution.py:25
  122.7 10.8 %collective-permute-start.30 = (bf16[1184,128]{1,0:T(8,128)(2,1)S(1)}, bf16[1184,128]{1,0:T(8,128)(2,1)S(1)}, u32[]{:S(2)}, u32[]{:S(2)}) collective-permute-start(bf16[1184,128]{1,0:T(8,128)(2,1)S(1)} %pad_maximum_fusion.3), channel_id=1, source_target_pairs={{0,8},{8,16},{16,24},{24,32},{32,40},{40,48},{48,56},{56,0},{1,9},... | collective-permute-start | bytes 909320 | tf_op jit(solution)/shard_map/scatter/ppermute | solution.py:25
  133.8 7.9 %collective-permute-start.33 = (bf16[1184,128]{1,0:T(8,128)(2,1)S(1)}, bf16[1184,128]{1,0:T(8,128)(2,1)S(1)}, u32[]{:S(2)}, u32[]{:S(2)}) collective-permute-start(bf16[1184,128]{1,0:T(8,128)(2,1)S(1)} %pad_maximum_fusion.5), channel_id=1, source_target_pairs={{0,8},{8,16},{16,24},{24,32},{32,40},{40,48},{48,56},{56,0},{1,9},... | collective-permute-start | bytes 909320 | tf_op jit(solution)/shard_map/scatter/ppermute | solution.py:25
  133.9 7.3 %collective-permute-start.35 = (bf16[1024,128]{1,0:T(8,128)(2,1)S(1)}, bf16[1024,128]{1,0:T(8,128)(2,1)S(1)}, u32[]{:S(2)}, u32[]{:S(2)}) collective-permute-start(bf16[1024,128]{1,0:T(8,128)(2,1)S(1)} %bitcast.43), channel_id=1, source_target_pairs={{0,4},{4,0},{1,5},{5,1},{2,6},{6,2},{3,7},{7,3},{8,12},{12,8},{9,1... | collective-permute-start | bytes 786440 | tf_op jit(solution)/shard_map/scatter/ppermute | solution.py:30
  134.0 7.2 %collective-permute-start.34 = (bf16[1024,128]{1,0:T(8,128)(2,1)S(1)}, bf16[1024,128]{1,0:T(8,128)(2,1)S(1)}, u32[]{:S(2)}, u32[]{:S(2)}) collective-permute-start(bf16[1024,128]{1,0:T(8,128)(2,1)S(1)} %get-tuple-element.93), channel_id=1, source_target_pairs={{0,56},{8,0},{16,8},{24,16},{32,24},{40,32},{48,40},{56,48},{1,57}... | collective-permute-start | bytes 786440 | tf_op jit(solution)/shard_map/scatter/ppermute | solution.py:25
  142.0 6.0 %collective-permute-start.36 = (bf16[416,128]{1,0:T(8,128)(2,1)S(1)}, bf16[416,128]{1,0:T(8,128)(2,1)S(1)}, u32[]{:S(2)}, u32[]{:S(2)}) collective-permute-start(bf16[416,128]{1,0:T(8,128)(2,1)S(1)} %get-tuple-element.104), channel_id=1, source_target_pairs={{0,64},{64,128},{128,192},{192,0},{1,65},{65,129},{129,193},{193,1... | collective-permute-start | bytes 319496 | tf_op jit(solution)/shard_map/scatter/ppermute | solution.py:21
  142.1 5.9 %collective-permute-start.37 = (bf16[416,128]{1,0:T(8,128)(2,1)S(1)}, bf16[416,128]{1,0:T(8,128)(2,1)S(1)}, u32[]{:S(2)}, u32[]{:S(2)}) collective-permute-start(bf16[416,128]{1,0:T(8,128)(2,1)S(1)} %get-tuple-element.105), channel_id=1, source_target_pairs={{0,128},{64,192},{128,0},{192,64},{1,129},{65,193},{129,1},{193,65... | collective-permute-start | bytes 319496 | tf_op jit(solution)/shard_map/scatter/ppermute | solution.py:21
  142.7 5.8 %collective-permute-start.38 = (bf16[416,128]{1,0:T(8,128)(2,1)S(1)}, bf16[416,128]{1,0:T(8,128)(2,1)S(1)}, u32[]{:S(2)}, u32[]{:S(2)}) collective-permute-start(bf16[416,128]{1,0:T(8,128)(2,1)S(1)} %get-tuple-element.106), channel_id=1, source_target_pairs={{0,192},{64,0},{128,64},{192,128},{1,193},{65,1},{129,65},{193,129... | collective-permute-start | bytes 319496 | tf_op jit(solution)/shard_map/scatter/ppermute | solution.py:21
  148.6 5.4 %collective-permute-start.39 = (f32[160,128]{1,0:T(8,128)S(1)}, f32[160,128]{1,0:T(8,128)S(1)}, u32[]{:S(2)}, u32[]{:S(2)}) collective-permute-start(f32[160,128]{1,0:T(8,128)S(1)} %convert_add_fusion.8.mine_ref), channel_id=1, source_target_pairs={{0,1},{1,0},{2,3},{3,2},{4,5},{5,4},{6,7},{7,6},{8,9},{9,8},{10,11... | collective-permute-start | bytes 245768 | tf_op jit(solution)/shard_map/scatter/ppermute | solution.py:30
